TPU v7x, 32 devices: a whole 2x2x4 slice. The times are simulated.
32 devices in a mesh: pipe: 2 (over x), dp: 4 (over z), expert: 4 (over y, core).
Axes of the slice: x: 2, y: 2, z: 4, core: 2. Of those that a mesh axis runs over, the one named last changes fastest.
Arguments:
- out_grad: bfloat16 [2, 2, 512, 3072], P('pipe', None, 'expert', 'dp'), may hold values from -6 to 6
- expert_outputs: bfloat16 [2, 2, 512, 2, 3072], P('pipe', None, 'expert', None, 'dp'), may hold values from -0.1796875 to 0.1796875
- logits: float32 [2, 2, 512, 2], P('pipe', None, 'expert'), may hold values from -9 to 9
- routes: int32 [2, 2, 512, 2], P('pipe', None, 'expert'), may hold values from 0 to 3, all different within a row; in each aligned block of 128 rows (0 to 127, 128 to 255, ..., all dimensions but the last counted through in order) at most 68 rows name the same one
- down_weights: bfloat16 [4, 16384, 3072], P('expert', 'dp'), may hold values from -0.046875 to 0.046875
Outputs:
- grad_hidden: bfloat16 [2, 2, 4, 4, 68, 16384], P('pipe', None, 'expert', None, None, 'dp')
- grad_logits: bfloat16 [2, 2, 512, 2], P('pipe', None, 'expert')
Inputs may be any that keep to these rules, and one draw needn't show every extreme that they name: `routes`: each token names two different experts. The 128 tokens of one group, section and micro-batch (aligned blocks of 128 tokens) name one expert at most 68 times, and in every draw some block names some expert exactly 68 times.
All inputs are finite; a program needn't handle non-finite values.
Results may differ from a plain program's by a relative error of at most 0.0049.
Values may be sent and summed in bfloat16 or wider, within the bound.
No kernel may reach another device: no remote copies, remote signals or barrier semaphores. Data moves between devices by JAX's collectives and lax.ppermute only.
A program may use at most 64 MiB of HBM per device.

v0:
```python
import jax
import jax.numpy as jnp
from jax import lax
from jax.sharding import PartitionSpec as P


def shifted(x, axis, by):
    count = lax.axis_size(axis)
    pairs = [(i, i + by) for i in range(count) if 0 <= i + by < count]
    return lax.ppermute(x, axis, pairs)


def per_device(out_grad, expert_outputs, logits, routes, down_weights):
    micro_count = out_grad.shape[1]
    token_count = out_grad.shape[2]
    expert_count = lax.axis_size("expert")
    capacity = min(token_count, 2 * token_count // expert_count + token_count // 32)
    partial_sums = jnp.einsum(
        "smtkd,smtd->smtk", expert_outputs, out_grad, preferred_element_type=jnp.float32
    )
    scores = lax.psum(partial_sums, "dp")
    weight_first = jax.nn.sigmoid(logits[..., 0] - logits[..., 1])
    weight_second = jax.nn.sigmoid(logits[..., 1] - logits[..., 0])
    difference = weight_first * weight_second * (scores[..., 0] - scores[..., 1])
    logit_grad = jnp.stack([difference, -difference], -1).astype(jnp.bfloat16)
    pair_weights = jnp.stack([weight_first, weight_second], -1).reshape(
        1, micro_count, 2 * token_count
    )
    doubled = jnp.repeat(out_grad, 2, axis=2)
    weighted_all = (pair_weights[..., None] * doubled).astype(jnp.bfloat16)
    pair_routes = routes.reshape(micro_count, 2 * token_count)
    onehot = (pair_routes[..., None] == jnp.arange(expert_count, dtype=jnp.int32)).astype(jnp.int32)
    earlier = jnp.cumsum(onehot, axis=1) - onehot
    slot_index = jnp.sum(earlier * onehot, -1)
    target_slot = pair_routes * capacity + slot_index
    slot_numbers = jnp.arange(expert_count * capacity, dtype=jnp.int32)
    weights = down_weights[0]
    outputs = []
    for micro_index in range(micro_count):
        placement = (slot_numbers[:, None] == target_slot[micro_index][None, :]).astype(
            jnp.bfloat16
        )
        weighted_rows = weighted_all[0, micro_index]
        dispatched = jnp.dot(placement, weighted_rows, preferred_element_type=jnp.float32).astype(
            jnp.bfloat16
        )
        dispatched = dispatched.reshape(expert_count, capacity, weighted_rows.shape[1])
        result = jnp.einsum(
            "gnd,fd->gnf",
            lax.all_gather(
                lax.all_to_all(dispatched, "expert", split_axis=0, concat_axis=0, tiled=True),
                "dp",
                axis=2,
                tiled=True,
            ),
            weights,
            preferred_element_type=jnp.float32,
        ).astype(jnp.bfloat16)
        outputs.append(result)
    hidden = jnp.stack(outputs)[None, :, None]
    moved_hidden, moved_logits = shifted((hidden, logit_grad), "pipe", -1)
    return (moved_hidden, moved_logits)


def solution(mesh):
    in_specs = (
        P("pipe", None, "expert", "dp"),
        P("pipe", None, "expert", None, "dp"),
        P("pipe", None, "expert", None),
        P("pipe", None, "expert", None),
        P("expert", "dp", None),
    )
    out_specs = (P("pipe", None, "expert", None, None, "dp"), P("pipe", None, "expert", None))
    return jax.shard_map(
        per_device, mesh=mesh, in_specs=in_specs, out_specs=out_specs, check_vma=False
    )
```

profile of v0, /device:TPU:9, one launch (start us, length us, event | category | flops | bytes accessed | tf_op | source)
XLA Modules:
  0.0 247.8 jit_solution(5722249744619905798)
XLA Ops:
  7.2 0.9 copy.16
  8.1 0.1 reshape.123
  8.3 0.1 eq.57
  8.4 2.4 reduce-window.6
  10.9 0.1 copy.18
  11.1 0.1 copy.19
  11.3 1.1 bitcast_convert_fusion
  12.4 2.6 %fusion.16 = f32[2,128,1,2]{3,2,1,0:T(1,128)S(1)} fusion(bf16[1,2,128,2,768]{4,3,2,1,0:T(2,128)(2,1)S(1)} %copy-done, bf16[2,128,768,1]{2,1,0,3:T(8,128)(2,1)} %bitcast.51), kind=kOutput, calls=%fused_computation.12 | convolution fusion | flops 786432 | bytes 1181696 | tf_op jit(solution)/shard_map/smtkd,smtd->smtk/dot_general | solution.py:18
  15.0 0.1 copy.23
  15.1 7.2 %psum.7 = f32[1,2,128,2]{2,3,1,0:T(2,128)S(1)} all-reduce(f32[1,2,128,2]{2,3,1,0:T(2,128)S(1)} %bitcast.52), channel_id=1, replica_groups=mesh['pipe'=2,'dp'=4,'expert'=4] {'dp'}, use_global_device_ids=true, to_apply=%region_3.4 | all-reduce | flops 512 | bytes 4096 | tf_op jit(solution)/shard_map/psum | solution.py:21
  22.4 0.1 copy.20
  22.5 0.1 mul.46
  22.7 0.5 broadcast_in_dim.4
  23.2 2.2 convert_element_type.59
  25.4 1.6 multiply_convert_fusion
  27.0 0.3 convolution_convert_fusion
  27.3 0.1 reshape.126
  27.4 12.8 %all_to_all.10 = bf16[4,68,768]{2,1,0:T(8,128)(2,1)} all-to-all(bf16[4,68,768]{2,1,0:T(8,128)(2,1)S(1)} %reshape.126), channel_id=1, replica_groups=mesh['pipe'=2,'dp'=4,'expert'=4] {'expert'}, dimensions={0} | all-to-all | bytes 835584 | tf_op jit(solution)/shard_map/all_to_all | solution.py:51
  40.2 0.3 convolution_convert_fusion.1
  40.5 0.1 reshape.125
  40.6 11.2 %all_to_all.11 = bf16[4,68,768]{2,1,0:T(8,128)(2,1)} all-to-all(bf16[4,68,768]{2,1,0:T(8,128)(2,1)S(1)} %reshape.125), channel_id=1, replica_groups=mesh['pipe'=2,'dp'=4,'expert'=4] {'expert'}, dimensions={0} | all-to-all | bytes 835584 | tf_op jit(solution)/shard_map/all_to_all | solution.py:51
  51.8 27.6 %all-gather.5.cloned.1.call-done = bf16[4,68,3072]{2,1,0:T(8,128)(2,1)} async-done(((bf16[4,68,768]{2,1,0:T(8,128)(2,1)}), bf16[4,68,3072]{2,1,0:T(8,128)(2,1)}) %all-gather.5.cloned.1.call-update) | async-done | bytes 1671184 | tf_op jit(solution)/shard_map/all_gather | solution.py:50
  79.5 12.8 %fusion.10 = bf16[1,4,68,4096]{3,2,1,0:T(8,128)(2,1)S(1)} fusion(bf16[4,68,3072]{2,1,0:T(8,128)(2,1)} %all-gather.5.cloned.1.call-done, bf16[1,4096,3072]{2,1,0:T(8,128)(2,1)} %param.9), kind=kOutput, calls=%fused_computation.6 | convolution fusion | flops 6846218240 | bytes 29065216 | tf_op jit(solution)/shard_map/gnd,fd->gnf/dot_general | solution.py:48
  92.3 28.0 %all-gather.3.cloned.1.call-done = bf16[4,68,3072]{2,1,0:T(8,128)(2,1)} async-done(((bf16[4,68,768]{2,1,0:T(8,128)(2,1)}), bf16[4,68,3072]{2,1,0:T(8,128)(2,1)}) %all-gather.3.cloned.1.call-update) | async-done | bytes 1671184 | tf_op jit(solution)/shard_map/all_gather | solution.py:50
  120.3 13.8 %fusion.13 = bf16[1,4,68,4096]{3,2,1,0:T(8,128)(2,1)} fusion(bf16[4,68,3072]{2,1,0:T(8,128)(2,1)} %all-gather.3.cloned.1.call-done, bf16[1,4096,3072]{2,1,0:T(8,128)(2,1)} %param.9), kind=kOutput, calls=%fused_computation.7 | convolution fusion | flops 6846218240 | bytes 29065216 | tf_op jit(solution)/shard_map/gnd,fd->gnf/dot_general | solution.py:48
  134.1 2.1 maximum_bitcast_fusion
  136.2 3.4 %copy.21 = bf16[1,2,1,4,68,4096]{5,3,4,2,1,0:T(4,128)(2,1)S(1)} copy(bf16[1,2,1,4,68,4096]{5,4,3,1,2,0:T(8,128)(2,1)S(1)} %maximum_bitcast_fusion) | data formatting | bytes 8912896 | tf_op jit(solution)/shard_map/broadcast_in_dim | solution.py:60
  139.6 1.3 collective-permute-start
  140.9 1.3 collective-permute-start.1
  142.2 96.1 %collective-permute-done.1 = bf16[1,2,128,2]{2,3,1,0:T(2,128)(2,1)S(1)} collective-permute-done((bf16[1,2,128,2]{2,3,1,0:T(2,128)(2,1)S(1)}, bf16[1,2,128,2]{2,3,1,0:T(2,128)(2,1)S(1)}, u32[]{:S(2)}, u32[]{:S(2)}) %collective-permute-start.1) | collective-permute-done | bytes 1056 | tf_op jit(solution)/shard_map/ppermute | solution.py:10
  238.3 2.1 copy.28
  240.4 0.6 copy.29
  (22 shorter events, 0.4 us)
Async XLA Ops:
  7.2 5.2 %copy-start = (bf16[1,2,128,2,768]{4,3,2,1,0:T(2,128)(2,1)S(1)}, bf16[1,2,128,2,768]{4,3,2,1,0:T(2,128)(2,1)}, u32[]{:S(2)}) copy-start(bf16[1,2,128,2,768]{4,3,2,1,0:T(2,128)(2,1)} %param.6) | copy-start | bytes 2359300
  7.2 72.3 %all-gather.5.cloned.1.call-start = ((), (), s32[]{:S(2)}) async-start(), calls=%async_computation.3 | async-start | bytes 2211840 | tf_op jit(solution)/shard_map/all_gather | solution.py:50
  12.4 9.9 %copy-start.1 = (f32[1,2,128,2]{2,3,1,0:T(2,128)S(1)}, f32[1,2,128,2]{2,3,1,0:T(2,128)}, u32[]{:S(2)}) copy-start(f32[1,2,128,2]{2,3,1,0:T(2,128)} %param.7) | copy-start | bytes 6148
  40.2 80.1 %all-gather.3.cloned.1.call-start = ((), (), s32[]{:S(2)}) async-start(), calls=%async_computation.2 | async-start | bytes 2211840 | tf_op jit(solution)/shard_map/all_gather | solution.py:50
  139.6 98.7 %collective-permute-start = (bf16[1,2,1,4,68,4096]{5,3,4,2,1,0:T(4,128)(2,1)S(1)}, bf16[1,2,1,4,68,4096]{5,3,4,2,1,0:T(4,128)(2,1)S(1)}, u32[]{:S(2)}, u32[]{:S(2)}) collective-permute-start(bf16[1,2,1,4,68,4096]{5,3,4,2,1,0:T(4,128)(2,1)S(1)} %copy.21), channel_id=1, source_target_pairs={{16,0},{17,1},{18,2},{19,3},{20,4},{21,5},{22,6},{23,7},{24,8},{25... | collective-permute-start | bytes 13369352 | tf_op jit(solution)/shard_map/ppermute | solution.py:10
  140.9 97.4 %collective-permute-start.1 = (bf16[1,2,128,2]{2,3,1,0:T(2,128)(2,1)S(1)}, bf16[1,2,128,2]{2,3,1,0:T(2,128)(2,1)S(1)}, u32[]{:S(2)}, u32[]{:S(2)}) collective-permute-start(bf16[1,2,128,2]{2,3,1,0:T(2,128)(2,1)S(1)} %pad_maximum_fusion.1), channel_id=1, source_target_pairs={{16,0},{17,1},{18,2},{19,3},{20,4},{21,5},{22,6},{23,7},{24,8},{25... | collective-permute-start | bytes 3080 | tf_op jit(solution)/shard_map/ppermute | solution.py:10
Sparse Core Ops, SparseCore 0:
  40.3 39.1 all-gather.4
  81.0 39.1 all-gather.2
where the time goes:
time: 252 us; the launch traced here: 248 us
  waiting for transfers between devices  152 us (60%)
  blocking collectives  31.2 us (12%)
  matrix products  29.7 us (12%)
  between operations  14.2 us (6%)
  local copies, waits for them, and re-layouts  10.9 us (4%)
  other arithmetic  7.33 us (3%)
  starting transfers between devices  2.66 us (1%)
    ppermute x2, waiting for transfers between devices, shifted(): return lax.ppermute(x, axis, pairs)  96.1 us
    all_gather x2, waiting for transfers between devices, per_device(): lax.all_gather(lax.all_to_all(dispatched, 'expert', split_axis=0, concat_...  55.6 us
    dot_general x2, matrix products, per_device(): jnp.einsum('gnd,fd->gnf', lax.all_gather(lax.all_to_all(dispatched, 'expe...  26.6 us
    all_to_all x2, blocking collectives, per_device(): lax.all_to_all(dispatched, 'expert', split_axis=0, concat_axis=0, tiled=T...  24 us
    psum x1, blocking collectives, per_device(): scores = lax.psum(partial_sums, 'dp')  7.24 us
  transfers between devices with their start and end apart: 4, of which 3 were waited for; matrix products, arithmetic and copies ran while one was open for 5% of the time, Pallas kernels for 0%

commit v1 on v0

v1 whole, which is shorter than its diff:
```python
import functools

import jax
import jax.numpy as jnp
from jax import lax
from jax.experimental import pallas as pl
from jax.experimental.pallas import tpu as pltpu
from jax.sharding import PartitionSpec as P

MEBI = 1024 * 1024
NT = (((1,), (1,)), ((), ()))


def hop(x, pipe_by, dp_xor):
    sections, shares = lax.axis_size("pipe"), lax.axis_size("dp")
    pairs = [
        (s * shares + z, (s - pipe_by) * shares + (z ^ dp_xor))
        for s in range(pipe_by, sections)
        for z in range(shares)
    ]
    return lax.ppermute(x, ("pipe", "dp"), pairs)


def swap(x, bit):
    sections, experts = lax.axis_size("pipe"), lax.axis_size("expert")
    pairs = [
        (s * experts + e, s * experts + (e ^ bit))
        for s in range(sections - 1)
        for e in range(experts)
    ]
    return lax.ppermute(x, ("pipe", "expert"), pairs)


def spread(x):
    bit = lax.axis_size("expert") // 2
    held = {0: x}
    while bit:
        for j in sorted(held):
            held[j ^ bit] = swap(held[j], bit)
        bit //= 2
    return [held[j] for j in sorted(held)]


def fill_rows(place_ref, meta_ref, token_refs, rows_ref, cap, padded):
    expert = place_ref[0].astype(jnp.float32)
    groups = len(token_refs)
    tokens = meta_ref.shape[2]
    micros = meta_ref.shape[1] // 4
    earlier = lax.broadcasted_iota(jnp.int32, (tokens, tokens), 0) < lax.broadcasted_iota(
        jnp.int32, (tokens, tokens), 1
    )
    earlier = earlier.astype(jnp.bfloat16)
    slots = lax.broadcasted_iota(jnp.int32, (padded, tokens), 0).astype(jnp.float32)
    for micro in range(micros):
        blocks = []
        for j in range(groups):
            meta = meta_ref[j]
            first = meta[4 * micro : 4 * micro + 1] == expert
            second = meta[4 * micro + 1 : 4 * micro + 2] == expert
            here = jnp.logical_or(first, second)
            weight = jnp.where(
                first, meta[4 * micro + 2 : 4 * micro + 3], meta[4 * micro + 3 : 4 * micro + 4]
            )
            named = jnp.broadcast_to(here.astype(jnp.float32), (16, tokens)).astype(jnp.bfloat16)
            slot = jnp.dot(named, earlier, preferred_element_type=jnp.float32)[0:1]
            picked = jnp.logical_and(slots == slot, here)
            picked = jnp.logical_and(picked, slots < cap)
            row_weight = jnp.sum(jnp.where(picked, weight, 0.0), axis=1, keepdims=True)
            block = jnp.dot(
                picked.astype(jnp.float32).astype(jnp.bfloat16),
                token_refs[j][micro * tokens : (micro + 1) * tokens, :],
                preferred_element_type=jnp.float32,
            )
            blocks.append(block * row_weight)
        for j in range(0, groups, 2):
            at = (micro * groups + j) * padded
            rows_ref[at : at + 2 * padded, :] = jnp.concatenate(blocks[j : j + 2], 0).astype(
                jnp.bfloat16
            )


def part_kernel(groups, cap, padded, first, last, *refs):
    place_ref, meta_ref = refs[:2]
    token_refs = refs[2 : 2 + groups]
    weight_ref = refs[2 + groups]
    rest = refs[3 + groups :]
    total_ref = None
    if not first:
        total_ref, rest = rest[0], rest[1:]
    out_ref, rows_ref = rest

    @pl.when(pl.program_id(0) == 0)
    def _():
        fill_rows(place_ref, meta_ref, token_refs, rows_ref, cap, padded)

    product = lax.dot_general(
        rows_ref[...], weight_ref[0], NT, preferred_element_type=jnp.float32
    )
    if not first:
        product = product + total_ref[...]
    if not last:
        out_ref[...] = product
    else:
        for micro in range(out_ref.shape[1]):
            for j in range(groups):
                at = (micro * groups + j) * padded
                out_ref[0, micro, 0, place_ref[0] ^ j] = product[at : at + cap].astype(
                    out_ref.dtype
                )


def add_part(place, meta, tokens, weights, total, cap, last):
    groups = len(tokens)
    micros = meta.shape[1] // 4
    padded = -(-cap // 8) * 8
    rows = micros * groups * padded
    depth = tokens[0].shape[1]
    hidden = weights.shape[1]
    block = min(512, hidden)
    whole = lambda *shape: pl.BlockSpec(shape, lambda f, p: (0,) * len(shape))
    in_specs = [whole(*meta.shape)] + [whole(*t.shape) for t in tokens]
    in_specs.append(pl.BlockSpec((1, block, depth), lambda f, p: (0, f, p[1])))
    args = [place, meta, *tokens, weights]
    aliases = {}
    total_spec = pl.BlockSpec((rows, block), lambda f, p: (0, f))
    if total is not None:
        in_specs.append(total_spec)
        args.append(total)
        if not last:
            aliases = {len(args) - 1: 0}
    if last:
        out_shape = jax.ShapeDtypeStruct((1, micros, 1, groups, cap, hidden), jnp.bfloat16)
        out_spec = pl.BlockSpec(
            (1, micros, 1, groups, cap, block), lambda f, p: (0, 0, 0, 0, 0, f)
        )
    else:
        out_shape = jax.ShapeDtypeStruct((rows, hidden), jnp.float32)
        out_spec = total_spec
    return pl.pallas_call(
        functools.partial(part_kernel, groups, cap, padded, total is None, last),
        grid_spec=pltpu.PrefetchScalarGridSpec(
            num_scalar_prefetch=1,
            grid=(hidden // block,),
            in_specs=in_specs,
            out_specs=out_spec,
            scratch_shapes=[pltpu.VMEM((rows, depth), jnp.bfloat16)],
        ),
        out_shape=out_shape,
        input_output_aliases=aliases,
        compiler_params=pltpu.CompilerParams(vmem_limit_bytes=40 * MEBI),
        cost_estimate=pl.CostEstimate(
            flops=2 * rows * depth * hidden,
            bytes_accessed=2 * hidden * depth + 8 * rows * hidden,
            transcendentals=0,
        ),
    )(*args)


def per_device(out_grad, expert_outputs, logits, routes, down_weights):
    micros, token_count, share = out_grad.shape[1:]
    experts, shares = lax.axis_size("expert"), lax.axis_size("dp")
    cap = min(token_count, 2 * token_count // experts + token_count // 32)
    expert, mine = lax.axis_index("expert"), lax.axis_index("dp")

    own = out_grad.reshape(micros * token_count, share)
    together = 1
    while (share * together) % 128:
        together *= 2
    arrived = [hop(own, 1, k) for k in range(shares)]

    grads = out_grad[0].astype(jnp.float32)
    outputs = expert_outputs[0].astype(jnp.float32)
    difference = jnp.sum(grads * (outputs[:, :, 0] - outputs[:, :, 1]), -1)
    weight_first = jax.nn.sigmoid(logits[0, ..., 0] - logits[0, ..., 1])
    weight_second = jax.nn.sigmoid(logits[0, ..., 1] - logits[0, ..., 0])
    named = routes[0].astype(jnp.float32)
    meta = jnp.stack([named[..., 0], named[..., 1], weight_first, weight_second], 1)
    meta = meta.reshape(4 * micros, token_count)
    small = jnp.concatenate([meta, difference], 0)
    smalls = [hop(small, 1, k) for k in range(shares)]
    meta = smalls[0][: 4 * micros]
    score = sum(s[4 * micros :] for s in smalls)
    by_micro = meta.reshape(micros, 4, token_count)
    slope = by_micro[:, 2] * by_micro[:, 3] * score
    moved_logits = jnp.stack([slope, -slope], -1).astype(jnp.bfloat16)[None]

    metas = jnp.stack(spread(meta))
    total = None
    for part in range(0, shares, together):
        pieces = [spread(arrived[part + i]) for i in range(together)]
        low = mine % together
        tokens = []
        for j in range(experts):
            if together == 1:
                tokens.append(pieces[0][j])
            else:
                stacked = jnp.stack([piece[j] for piece in pieces])
                order = jnp.arange(together) ^ low
                tokens.append(
                    jnp.take(stacked, order, axis=0).transpose(1, 0, 2).reshape(
                        micros * token_count, together * share
                    )
                )
        place = jnp.stack([expert, (mine ^ part) // together]).astype(jnp.int32)
        total = add_part(
            place, metas, tokens, down_weights, total, cap, part + together == shares
        )
    return total, moved_logits


def solution(mesh):
    in_specs = (
        P("pipe", None, "expert", "dp"),
        P("pipe", None, "expert", None, "dp"),
        P("pipe", None, "expert", None),
        P("pipe", None, "expert", None),
        P("expert", "dp", None),
    )
    out_specs = (P("pipe", None, "expert", None, None, "dp"), P("pipe", None, "expert", None))
    return jax.shard_map(
        per_device, mesh=mesh, in_specs=in_specs, out_specs=out_specs, check_vma=False
    )
```

time: 252 us -> 136 us (0.54)
  waiting for transfers between devices: 152 us -> 23.9 us
  starting transfers between devices: 2.66 us -> 50.7 us
  Pallas kernels: 0 us -> 43.2 us
  blocking collectives: 31.2 us -> 0 us
  matrix products: 29.7 us -> 0 us
  between operations: 14.2 us -> 1.09 us
  other arithmetic: 7.33 us -> 3.69 us
    ppermute x2 -> x23, waiting for transfers between devices: 96.1 us -> 23.9 us  [the longest x8 23.9 us: hop(): return lax.ppermute(x, ('pipe', 'dp'), pairs)]
    all_gather x2 -> x0, waiting for transfers between devices: 55.6 us -> none  [per_device(): lax.all_gather(lax.all_to_all(dispatched, 'expert', split_axis=0, concat_...]
    ppermute x2 -> x23, starting transfers between devices: 2.58 us -> 50.7 us  [the longest x15 40.2 us: swap(): return lax.ppermute(x, ('pipe', 'expert'), pairs)]
    pallas_call x0 -> x4, Pallas kernels: none -> 43.2 us  [add_part(): pl.pallas_call(functools.partial(part_kernel, groups, cap, padded, total...]
    dot_general x5 -> x0, matrix products: 29.7 us -> none  [the longest x2 26.6 us: per_device(): jnp.einsum('gnd,fd->gnf', lax.all_gather(lax.all_to_all(dispatched, 'expe...]
    all_to_all x2 -> x0, blocking collectives: 24 us -> none  [per_device(): lax.all_to_all(dispatched, 'expert', split_axis=0, concat_axis=0, tiled=T...]
    psum x1 -> x0, blocking collectives: 7.24 us -> none  [per_device(): scores = lax.psum(partial_sums, 'dp')]
    unnamed x7 -> x6, local copies, waits for them, and re-layouts: 3.55 us -> 9.77 us
  transfers between devices with their start and end apart: 4 -> 23, of which waited for: 3 -> 2; matrix products, arithmetic and copies ran while one was open for 5% -> 4% of each run, Pallas kernels for 0% -> 23%
where the time goes in v1:
time: 136 us; the launch traced here: 133 us
  starting transfers between devices  50.7 us (37%)
  Pallas kernels  43.2 us (32%)
  waiting for transfers between devices  23.9 us (18%)
  local copies, waits for them, and re-layouts  10.6 us (8%)
  other arithmetic  3.69 us (3%)
    pallas_call x4, Pallas kernels, add_part(): pl.pallas_call(functools.partial(part_kernel, groups, cap, padded, total...  43.2 us
    ppermute x15, starting transfers between devices, swap(): return lax.ppermute(x, ('pipe', 'expert'), pairs)  40.2 us
    ppermute x8, waiting for transfers between devices, hop(): return lax.ppermute(x, ('pipe', 'dp'), pairs)  23.9 us
    ppermute x8, starting transfers between devices, hop(): return lax.ppermute(x, ('pipe', 'dp'), pairs)  10.4 us
    unnamed x6, local copies, waits for them, and re-layouts  9.77 us
  transfers between devices with their start and end apart: 23, of which 2 were waited for; matrix products, arithmetic and copies ran while one was open for 4% of the time, Pallas kernels for 23%

profile of v1, /device:TPU:9, one launch (start us, length us, event | category | flops | bytes accessed | tf_op | source)
XLA Modules:
  0.0 133.1 jit_solution(5407005347145182987)
XLA Ops:
  0.6 1.4 %collective-permute-start.16 = (bf16[256,768]{1,0:T(8,128)(2,1)}, bf16[256,768]{1,0:T(8,128)(2,1)S(1)}, u32[]{:S(2)}, u32[]{:S(2)}) collective-permute-start(bf16[256,768]{1,0:T(8,128)(2,1)} %bitcast.44), channel_id=1, source_target_pairs={{16,0},{20,4},{24,8},{28,12},{17,1},{21,5},{25,9},{29,13},{18,2},{... | collective-permute-start | bytes 1179656 | tf_op jit(solution)/shard_map/ppermute | solution.py:21
  2.1 1.3 collective-permute-start.12
  4.9 1.7 %bitcast_convert_fusion = f32[2,128,2,768]{3,2,1,0:T(2,128)S(1)} fusion(bf16[1,2,128,2,768]{4,3,2,1,0:T(2,128)(2,1)} %param.6), kind=kLoop, calls=%fused_computation.3 | loop fusion | flops 393216 | bytes 2359296 | tf_op jit(solution)/shard_map/convert_element_type | solution.py:172
  7.5 1.3 collective-permute-start
  8.8 1.3 collective-permute-start.20
  10.1 1.3 collective-permute-start.21
  11.7 10.1 %collective-permute-done = f32[10,128]{1,0:T(8,128)S(1)} collective-permute-done((f32[10,128]{1,0:T(8,128)S(1)}, f32[10,128]{1,0:T(8,128)S(1)}, u32[]{:S(2)}, u32[]{:S(2)}) %collective-permute-start) | collective-permute-done | bytes 5152 | tf_op jit(solution)/shard_map/ppermute | solution.py:21
  21.8 1.3 collective-permute-start.22
  23.1 3.1 %collective-permute-start.2 = (f32[8,128]{1,0:T(8,128)S(1)}, f32[8,128]{1,0:T(8,128)S(1)}, u32[]{:S(2)}, u32[]{:S(2)}) collective-permute-start(f32[8,128]{1,0:T(8,128)S(1)} %get-tuple-element.7), channel_id=1, source_target_pairs={{0,2},{1,3},{2,0},{3,1},{4,6},{5,7},{6,4},{7,5},{8,10},{9,11},{10,... | collective-permute-start | bytes 12296 | tf_op jit(solution)/shard_map/ppermute | solution.py:31
  26.4 1.3 collective-permute-start.8
  27.7 4.1 %collective-permute-start.1 = (f32[8,128]{1,0:T(8,128)S(1)}, f32[8,128]{1,0:T(8,128)S(1)}, u32[]{:S(2)}, u32[]{:S(2)}) collective-permute-start(f32[8,128]{1,0:T(8,128)S(1)} %get-tuple-element.7), channel_id=1, source_target_pairs={{0,1},{1,0},{2,3},{3,2},{4,5},{5,4},{6,7},{7,6},{8,9},{9,8},{10,11... | collective-permute-start | bytes 12296 | tf_op jit(solution)/shard_map/ppermute | solution.py:31
  31.7 1.9 %collective-permute-start.3 = (f32[8,128]{1,0:T(8,128)S(1)}, f32[8,128]{1,0:T(8,128)S(1)}, u32[]{:S(2)}, u32[]{:S(2)}) collective-permute-start(f32[8,128]{1,0:T(8,128)S(1)} %collective-permute-done.2), channel_id=1, source_target_pairs={{0,1},{1,0},{2,3},{3,2},{4,5},{5,4},{6,7},{7,6},{8,9},{9,8},{10,11... | collective-permute-start | bytes 12296 | tf_op jit(solution)/shard_map/ppermute | solution.py:31
  33.7 3.1 %collective-permute-start.18 = (bf16[256,768]{1,0:T(8,128)(2,1)S(1)}, bf16[256,768]{1,0:T(8,128)(2,1)S(1)}, u32[]{:S(2)}, u32[]{:S(2)}) collective-permute-start(bf16[256,768]{1,0:T(8,128)(2,1)S(1)} %collective-permute-done.16.refs_2_), channel_id=1, source_target_pairs={{0,2},{1,3},{2,0},{3,1},{4,6},{5,7},{6,4},{7,5},{8,10},{9,11},{10,... | collective-permute-start | bytes 1179656 | tf_op jit(solution)/shard_map/ppermute | solution.py:31
  36.8 1.3 collective-permute-start.4
  38.1 2.7 %collective-permute-start.17 = (bf16[256,768]{1,0:T(8,128)(2,1)S(1)}, bf16[256,768]{1,0:T(8,128)(2,1)S(1)}, u32[]{:S(2)}, u32[]{:S(2)}) collective-permute-start(bf16[256,768]{1,0:T(8,128)(2,1)S(1)} %collective-permute-done.16.refs_2_), channel_id=1, source_target_pairs={{0,1},{1,0},{2,3},{3,2},{4,5},{5,4},{6,7},{7,6},{8,9},{9,8},{10,11... | collective-permute-start | bytes 1179656 | tf_op jit(solution)/shard_map/ppermute | solution.py:31
  40.8 2.2 %collective-permute-start.14 = (bf16[256,768]{1,0:T(8,128)(2,1)S(1)}, bf16[256,768]{1,0:T(8,128)(2,1)S(1)}, u32[]{:S(2)}, u32[]{:S(2)}) collective-permute-start(bf16[256,768]{1,0:T(8,128)(2,1)S(1)} %collective-permute-done.12.refs_2_), channel_id=1, source_target_pairs={{0,2},{1,3},{2,0},{3,1},{4,6},{5,7},{6,4},{7,5},{8,10},{9,11},{10,... | collective-permute-start | bytes 1179656 | tf_op jit(solution)/shard_map/ppermute | solution.py:31
  43.1 3.1 %collective-permute-start.10 = (bf16[256,768]{1,0:T(8,128)(2,1)S(1)}, bf16[256,768]{1,0:T(8,128)(2,1)S(1)}, u32[]{:S(2)}, u32[]{:S(2)}) collective-permute-start(bf16[256,768]{1,0:T(8,128)(2,1)S(1)} %collective-permute-done.8.refs_2_), channel_id=1, source_target_pairs={{0,2},{1,3},{2,0},{3,1},{4,6},{5,7},{6,4},{7,5},{8,10},{9,11},{10,... | collective-permute-start | bytes 1179656 | tf_op jit(solution)/shard_map/ppermute | solution.py:31
  46.2 3.8 %collective-permute-start.19 = (bf16[256,768]{1,0:T(8,128)(2,1)S(1)}, bf16[256,768]{1,0:T(8,128)(2,1)S(1)}, u32[]{:S(2)}, u32[]{:S(2)}) collective-permute-start(bf16[256,768]{1,0:T(8,128)(2,1)S(1)} %collective-permute-done.18.refs_4_), channel_id=1, source_target_pairs={{0,1},{1,0},{2,3},{3,2},{4,5},{5,4},{6,7},{7,6},{8,9},{9,8},{10,11... | collective-permute-start | bytes 1179656 | tf_op jit(solution)/shard_map/ppermute | solution.py:31
  50.6 13.7 %collective-permute-done.4.refs_2_ = bf16[256,768]{1,0:T(8,128)(2,1)S(1)} collective-permute-done((bf16[256,768]{1,0:T(8,128)(2,1)S(1)}, bf16[256,768]{1,0:T(8,128)(2,1)S(1)}, u32[]{:S(2)}, u32[]{:S(2)}) %collective-permute-start.4) | collective-permute-done | bytes 393248 | tf_op jit(solution)/shard_map/ppermute | solution.py:21
  64.3 3.5 %collective-permute-start.13 = (bf16[256,768]{1,0:T(8,128)(2,1)S(1)}, bf16[256,768]{1,0:T(8,128)(2,1)S(1)}, u32[]{:S(2)}, u32[]{:S(2)}) collective-permute-start(bf16[256,768]{1,0:T(8,128)(2,1)S(1)} %collective-permute-done.12.refs_2_), channel_id=1, source_target_pairs={{0,1},{1,0},{2,3},{3,2},{4,5},{5,4},{6,7},{7,6},{8,9},{9,8},{10,11... | collective-permute-start | bytes 1179656 | tf_op jit(solution)/shard_map/ppermute | solution.py:31
  67.8 1.9 %collective-permute-start.6 = (bf16[256,768]{1,0:T(8,128)(2,1)S(1)}, bf16[256,768]{1,0:T(8,128)(2,1)S(1)}, u32[]{:S(2)}, u32[]{:S(2)}) collective-permute-start(bf16[256,768]{1,0:T(8,128)(2,1)S(1)} %collective-permute-done.4.refs_2_), channel_id=1, source_target_pairs={{0,2},{1,3},{2,0},{3,1},{4,6},{5,7},{6,4},{7,5},{8,10},{9,11},{10,... | collective-permute-start | bytes 1179656 | tf_op jit(solution)/shard_map/ppermute | solution.py:31
  69.7 2.2 %collective-permute-start.15 = (bf16[256,768]{1,0:T(8,128)(2,1)S(1)}, bf16[256,768]{1,0:T(8,128)(2,1)S(1)}, u32[]{:S(2)}, u32[]{:S(2)}) collective-permute-start(bf16[256,768]{1,0:T(8,128)(2,1)S(1)} %collective-permute-done.14.refs_4_), channel_id=1, source_target_pairs={{0,1},{1,0},{2,3},{3,2},{4,5},{5,4},{6,7},{7,6},{8,9},{9,8},{10,11... | collective-permute-start | bytes 1179656 | tf_op jit(solution)/shard_map/ppermute | solution.py:31
  71.9 2.1 %collective-permute-start.9 = (bf16[256,768]{1,0:T(8,128)(2,1)S(1)}, bf16[256,768]{1,0:T(8,128)(2,1)S(1)}, u32[]{:S(2)}, u32[]{:S(2)}) collective-permute-start(bf16[256,768]{1,0:T(8,128)(2,1)S(1)} %collective-permute-done.8.refs_2_), channel_id=1, source_target_pairs={{0,1},{1,0},{2,3},{3,2},{4,5},{5,4},{6,7},{7,6},{8,9},{9,8},{10,11... | collective-permute-start | bytes 1179656 | tf_op jit(solution)/shard_map/ppermute | solution.py:31
  74.1 2.2 %collective-permute-start.11 = (bf16[256,768]{1,0:T(8,128)(2,1)S(1)}, bf16[256,768]{1,0:T(8,128)(2,1)S(1)}, u32[]{:S(2)}, u32[]{:S(2)}) collective-permute-start(bf16[256,768]{1,0:T(8,128)(2,1)S(1)} %collective-permute-done.10.refs_4_), channel_id=1, source_target_pairs={{0,1},{1,0},{2,3},{3,2},{4,5},{5,4},{6,7},{7,6},{8,9},{9,8},{10,11... | collective-permute-start | bytes 1179656 | tf_op jit(solution)/shard_map/ppermute | solution.py:31
  76.3 10.3 %shard_map.68.refs_7_ = f32[576,4096]{1,0:T(8,128)S(1)} custom-call(s32[2]{0:T(128)S(1)} %pad_add_fusion.3.refs_0_, f32[4,8,128]{2,1,0:T(8,128)S(1)} %pad_maximum_fusion.refs_1_, bf16[256,768]{1,0:T(8,128)(2,1)S(1)} %collective-permute-done.16.refs_2_, bf16[256,768]{1,0:T(8,128)(2,1)S(1)} %collective-permute-done.17.refs_3_, ...), custom_call_target="tpu_custom_call" | custom-call | flops 3623878656 | bytes 25165824 | tf_op jit(solution)/shard_map/pallas_call | solution.py:139
  86.6 2.1 %collective-permute-start.5 = (bf16[256,768]{1,0:T(8,128)(2,1)S(1)}, bf16[256,768]{1,0:T(8,128)(2,1)S(1)}, u32[]{:S(2)}, u32[]{:S(2)}) collective-permute-start(bf16[256,768]{1,0:T(8,128)(2,1)S(1)} %collective-permute-done.4.refs_2_), channel_id=1, source_target_pairs={{0,1},{1,0},{2,3},{3,2},{4,5},{5,4},{6,7},{7,6},{8,9},{9,8},{10,11... | collective-permute-start | bytes 1179656 | tf_op jit(solution)/shard_map/ppermute | solution.py:31
  88.7 2.2 %collective-permute-start.7 = (bf16[256,768]{1,0:T(8,128)(2,1)S(1)}, bf16[256,768]{1,0:T(8,128)(2,1)S(1)}, u32[]{:S(2)}, u32[]{:S(2)}) collective-permute-start(bf16[256,768]{1,0:T(8,128)(2,1)S(1)} %collective-permute-done.6.refs_4_), channel_id=1, source_target_pairs={{0,1},{1,0},{2,3},{3,2},{4,5},{5,4},{6,7},{7,6},{8,9},{9,8},{10,11... | collective-permute-start | bytes 1179656 | tf_op jit(solution)/shard_map/ppermute | solution.py:31
  91.0 10.4 %shard_map.69.refs_7_ = f32[576,4096]{1,0:T(8,128)S(1)} custom-call(s32[2]{0:T(128)S(1)} %pad_add_fusion.2.refs_0_, f32[4,8,128]{2,1,0:T(8,128)S(1)} %pad_maximum_fusion.refs_1_, bf16[256,768]{1,0:T(8,128)(2,1)S(1)} %collective-permute-done.12.refs_2_, bf16[256,768]{1,0:T(8,128)(2,1)S(1)} %collective-permute-done.13.refs_3_, ...), custom_call_target="tpu_custom_call", output_to_operand_aliasing={{}: (7, {})} | custom-call | flops 3623878656 | bytes 25165824 | tf_op jit(solution)/shard_map/pallas_call | solution.py:139
  101.4 10.4 %shard_map.70.refs_7_ = f32[576,4096]{1,0:T(8,128)S(1)} custom-call(s32[2]{0:T(128)S(1)} %pad_add_fusion.1.refs_0_, f32[4,8,128]{2,1,0:T(8,128)S(1)} %pad_maximum_fusion.refs_1_, bf16[256,768]{1,0:T(8,128)(2,1)S(1)} %collective-permute-done.8.refs_2_, bf16[256,768]{1,0:T(8,128)(2,1)S(1)} %collective-permute-done.9.refs_3_, ...), custom_call_target="tpu_custom_call", output_to_operand_aliasing={{}: (7, {})} | custom-call | flops 3623878656 | bytes 25165824 | tf_op jit(solution)/shard_map/pallas_call | solution.py:139
  111.9 3.7 %copy-done = f32[576,4096]{1,0:T(8,128)} copy-done((f32[576,4096]{1,0:T(8,128)}, f32[576,4096]{1,0:T(8,128)S(1)}, u32[]{:S(2)}) %copy-start) | copy-done | bytes 9437208
  115.6 12.0 %shard_map.71 = bf16[1,2,1,4,68,4096]{5,4,3,2,1,0:T(8,128)(2,1)S(1)} custom-call(s32[2]{0:T(128)S(1)} %pad_add_fusion.refs_0_, f32[4,8,128]{2,1,0:T(8,128)S(1)} %pad_maximum_fusion.refs_1_, bf16[256,768]{1,0:T(8,128)(2,1)S(1)} %collective-permute-done.4.refs_2_, bf16[256,768]{1,0:T(8,128)(2,1)S(1)} %collective-permute-done.5.refs_3_, ...), custom_call_target="tpu_custom_call" | custom-call | flops 3623878656 | bytes 25165824 | tf_op jit(solution)/shard_map/pallas_call | solution.py:139
  127.6 5.5 %copy.15 = bf16[1,2,1,4,68,4096]{5,3,4,2,1,0:T(4,128)(2,1)} copy(bf16[1,2,1,4,68,4096]{5,4,3,2,1,0:T(8,128)(2,1)S(1)} %shard_map.71) | data formatting | bytes 8912896
  (44 shorter events, 3.4 us)
Async XLA Ops:
  0.6 6.7 %copy-start.1 = (bf16[1,2,128,768]{3,2,1,0:T(8,128)(2,1)S(1)}, bf16[1,2,128,768]{3,2,1,0:T(8,128)(2,1)}, u32[]{:S(2)}) copy-start(bf16[1,2,128,768]{3,2,1,0:T(8,128)(2,1)} %param.5) | copy-start | bytes 1179652
  0.6 33.0 %collective-permute-start.16 = (bf16[256,768]{1,0:T(8,128)(2,1)}, bf16[256,768]{1,0:T(8,128)(2,1)S(1)}, u32[]{:S(2)}, u32[]{:S(2)}) collective-permute-start(bf16[256,768]{1,0:T(8,128)(2,1)} %bitcast.44), channel_id=1, source_target_pairs={{16,0},{20,4},{24,8},{28,12},{17,1},{21,5},{25,9},{29,13},{18,2},{... | collective-permute-start | bytes 1179656 | tf_op jit(solution)/shard_map/ppermute | solution.py:21
  2.1 38.8 %collective-permute-start.12 = (bf16[256,768]{1,0:T(8,128)(2,1)}, bf16[256,768]{1,0:T(8,128)(2,1)S(1)}, u32[]{:S(2)}, u32[]{:S(2)}) collective-permute-start(bf16[256,768]{1,0:T(8,128)(2,1)} %bitcast.45), channel_id=1, source_target_pairs={{16,4},{20,0},{24,12},{28,8},{17,5},{21,1},{25,13},{29,9},{18,6},{... | collective-permute-start | bytes 1179656 | tf_op jit(solution)/shard_map/ppermute | solution.py:21
  7.5 14.3 %collective-permute-start = (f32[10,128]{1,0:T(8,128)S(1)}, f32[10,128]{1,0:T(8,128)S(1)}, u32[]{:S(2)}, u32[]{:S(2)}) collective-permute-start(f32[10,128]{1,0:T(8,128)S(1)} %pad_maximum_fusion.1), channel_id=1, source_target_pairs={{16,0},{20,4},{24,8},{28,12},{17,1},{21,5},{25,9},{29,13},{18,2},{... | collective-permute-start | bytes 15368 | tf_op jit(solution)/shard_map/ppermute | solution.py:21
  8.8 14.3 %collective-permute-start.20 = (f32[10,128]{1,0:T(8,128)S(1)}, f32[10,128]{1,0:T(8,128)S(1)}, u32[]{:S(2)}, u32[]{:S(2)}) collective-permute-start(f32[10,128]{1,0:T(8,128)S(1)} %pad_maximum_fusion.1), channel_id=1, source_target_pairs={{16,4},{20,0},{24,12},{28,8},{17,5},{21,1},{25,13},{29,9},{18,6},{... | collective-permute-start | bytes 15368 | tf_op jit(solution)/shard_map/ppermute | solution.py:21
  10.1 16.2 %collective-permute-start.21 = (f32[10,128]{1,0:T(8,128)S(1)}, f32[10,128]{1,0:T(8,128)S(1)}, u32[]{:S(2)}, u32[]{:S(2)}) collective-permute-start(f32[10,128]{1,0:T(8,128)S(1)} %pad_maximum_fusion.1), channel_id=1, source_target_pairs={{16,8},{20,12},{24,0},{28,4},{17,9},{21,13},{25,1},{29,5},{18,10},... | collective-permute-start | bytes 15368 | tf_op jit(solution)/shard_map/ppermute | solution.py:21
  21.8 5.8 %collective-permute-start.22 = (f32[10,128]{1,0:T(8,128)S(1)}, f32[10,128]{1,0:T(8,128)S(1)}, u32[]{:S(2)}, u32[]{:S(2)}) collective-permute-start(f32[10,128]{1,0:T(8,128)S(1)} %pad_maximum_fusion.1), channel_id=1, source_target_pairs={{16,12},{20,8},{24,4},{28,0},{17,13},{21,9},{25,5},{29,1},{18,14},... | collective-permute-start | bytes 15368 | tf_op jit(solution)/shard_map/ppermute | solution.py:21
  23.1 8.6 %collective-permute-start.2 = (f32[8,128]{1,0:T(8,128)S(1)}, f32[8,128]{1,0:T(8,128)S(1)}, u32[]{:S(2)}, u32[]{:S(2)}) collective-permute-start(f32[8,128]{1,0:T(8,128)S(1)} %get-tuple-element.7), channel_id=1, source_target_pairs={{0,2},{1,3},{2,0},{3,1},{4,6},{5,7},{6,4},{7,5},{8,10},{9,11},{10,... | collective-permute-start | bytes 12296 | tf_op jit(solution)/shard_map/ppermute | solution.py:31
  26.4 16.7 %collective-permute-start.8 = (bf16[256,768]{1,0:T(8,128)(2,1)S(1)}, bf16[256,768]{1,0:T(8,128)(2,1)S(1)}, u32[]{:S(2)}, u32[]{:S(2)}) collective-permute-start(bf16[256,768]{1,0:T(8,128)(2,1)S(1)} %bitcast.46), channel_id=1, source_target_pairs={{16,8},{20,12},{24,0},{28,4},{17,9},{21,13},{25,1},{29,5},{18,10},... | collective-permute-start | bytes 1179656 | tf_op jit(solution)/shard_map/ppermute | solution.py:21
  27.7 9.2 %collective-permute-start.1 = (f32[8,128]{1,0:T(8,128)S(1)}, f32[8,128]{1,0:T(8,128)S(1)}, u32[]{:S(2)}, u32[]{:S(2)}) collective-permute-start(f32[8,128]{1,0:T(8,128)S(1)} %get-tuple-element.7), channel_id=1, source_target_pairs={{0,1},{1,0},{2,3},{3,2},{4,5},{5,4},{6,7},{7,6},{8,9},{9,8},{10,11... | collective-permute-start | bytes 12296 | tf_op jit(solution)/shard_map/ppermute | solution.py:31
  31.7 6.4 %collective-permute-start.3 = (f32[8,128]{1,0:T(8,128)S(1)}, f32[8,128]{1,0:T(8,128)S(1)}, u32[]{:S(2)}, u32[]{:S(2)}) collective-permute-start(f32[8,128]{1,0:T(8,128)S(1)} %collective-permute-done.2), channel_id=1, source_target_pairs={{0,1},{1,0},{2,3},{3,2},{4,5},{5,4},{6,7},{7,6},{8,9},{9,8},{10,11... | collective-permute-start | bytes 12296 | tf_op jit(solution)/shard_map/ppermute | solution.py:31
  33.7 12.5 %collective-permute-start.18 = (bf16[256,768]{1,0:T(8,128)(2,1)S(1)}, bf16[256,768]{1,0:T(8,128)(2,1)S(1)}, u32[]{:S(2)}, u32[]{:S(2)}) collective-permute-start(bf16[256,768]{1,0:T(8,128)(2,1)S(1)} %collective-permute-done.16.refs_2_), channel_id=1, source_target_pairs={{0,2},{1,3},{2,0},{3,1},{4,6},{5,7},{6,4},{7,5},{8,10},{9,11},{10,... | collective-permute-start | bytes 1179656 | tf_op jit(solution)/shard_map/ppermute | solution.py:31
  36.8 27.4 %collective-permute-start.4 = (bf16[256,768]{1,0:T(8,128)(2,1)S(1)}, bf16[256,768]{1,0:T(8,128)(2,1)S(1)}, u32[]{:S(2)}, u32[]{:S(2)}) collective-permute-start(bf16[256,768]{1,0:T(8,128)(2,1)S(1)} %bitcast.47), channel_id=1, source_target_pairs={{16,12},{20,8},{24,4},{28,0},{17,13},{21,9},{25,5},{29,1},{18,14},... | collective-permute-start | bytes 1179656 | tf_op jit(solution)/shard_map/ppermute | solution.py:21
  38.1 29.6 %collective-permute-start.17 = (bf16[256,768]{1,0:T(8,128)(2,1)S(1)}, bf16[256,768]{1,0:T(8,128)(2,1)S(1)}, u32[]{:S(2)}, u32[]{:S(2)}) collective-permute-start(bf16[256,768]{1,0:T(8,128)(2,1)S(1)} %collective-permute-done.16.refs_2_), channel_id=1, source_target_pairs={{0,1},{1,0},{2,3},{3,2},{4,5},{5,4},{6,7},{7,6},{8,9},{9,8},{10,11... | collective-permute-start | bytes 1179656 | tf_op jit(solution)/shard_map/ppermute | solution.py:31
  40.8 28.8 %collective-permute-start.14 = (bf16[256,768]{1,0:T(8,128)(2,1)S(1)}, bf16[256,768]{1,0:T(8,128)(2,1)S(1)}, u32[]{:S(2)}, u32[]{:S(2)}) collective-permute-start(bf16[256,768]{1,0:T(8,128)(2,1)S(1)} %collective-permute-done.12.refs_2_), channel_id=1, source_target_pairs={{0,2},{1,3},{2,0},{3,1},{4,6},{5,7},{6,4},{7,5},{8,10},{9,11},{10,... | collective-permute-start | bytes 1179656 | tf_op jit(solution)/shard_map/ppermute | solution.py:31
  43.1 28.9 %collective-permute-start.10 = (bf16[256,768]{1,0:T(8,128)(2,1)S(1)}, bf16[256,768]{1,0:T(8,128)(2,1)S(1)}, u32[]{:S(2)}, u32[]{:S(2)}) collective-permute-start(bf16[256,768]{1,0:T(8,128)(2,1)S(1)} %collective-permute-done.8.refs_2_), channel_id=1, source_target_pairs={{0,2},{1,3},{2,0},{3,1},{4,6},{5,7},{6,4},{7,5},{8,10},{9,11},{10,... | collective-permute-start | bytes 1179656 | tf_op jit(solution)/shard_map/ppermute | solution.py:31
  46.2 27.9 %collective-permute-start.19 = (bf16[256,768]{1,0:T(8,128)(2,1)S(1)}, bf16[256,768]{1,0:T(8,128)(2,1)S(1)}, u32[]{:S(2)}, u32[]{:S(2)}) collective-permute-start(bf16[256,768]{1,0:T(8,128)(2,1)S(1)} %collective-permute-done.18.refs_4_), channel_id=1, source_target_pairs={{0,1},{1,0},{2,3},{3,2},{4,5},{5,4},{6,7},{7,6},{8,9},{9,8},{10,11... | collective-permute-start | bytes 1179656 | tf_op jit(solution)/shard_map/ppermute | solution.py:31
  64.3 22.3 %collective-permute-start.13 = (bf16[256,768]{1,0:T(8,128)(2,1)S(1)}, bf16[256,768]{1,0:T(8,128)(2,1)S(1)}, u32[]{:S(2)}, u32[]{:S(2)}) collective-permute-start(bf16[256,768]{1,0:T(8,128)(2,1)S(1)} %collective-permute-done.12.refs_2_), channel_id=1, source_target_pairs={{0,1},{1,0},{2,3},{3,2},{4,5},{5,4},{6,7},{7,6},{8,9},{9,8},{10,11... | collective-permute-start | bytes 1179656 | tf_op jit(solution)/shard_map/ppermute | solution.py:31
  67.8 21.0 %collective-permute-start.6 = (bf16[256,768]{1,0:T(8,128)(2,1)S(1)}, bf16[256,768]{1,0:T(8,128)(2,1)S(1)}, u32[]{:S(2)}, u32[]{:S(2)}) collective-permute-start(bf16[256,768]{1,0:T(8,128)(2,1)S(1)} %collective-permute-done.4.refs_2_), channel_id=1, source_target_pairs={{0,2},{1,3},{2,0},{3,1},{4,6},{5,7},{6,4},{7,5},{8,10},{9,11},{10,... | collective-permute-start | bytes 1179656 | tf_op jit(solution)/shard_map/ppermute | solution.py:31
  69.7 21.3 %collective-permute-start.15 = (bf16[256,768]{1,0:T(8,128)(2,1)S(1)}, bf16[256,768]{1,0:T(8,128)(2,1)S(1)}, u32[]{:S(2)}, u32[]{:S(2)}) collective-permute-start(bf16[256,768]{1,0:T(8,128)(2,1)S(1)} %collective-permute-done.14.refs_4_), channel_id=1, source_target_pairs={{0,1},{1,0},{2,3},{3,2},{4,5},{5,4},{6,7},{7,6},{8,9},{9,8},{10,11... | collective-permute-start | bytes 1179656 | tf_op jit(solution)/shard_map/ppermute | solution.py:31
  71.9 29.5 %collective-permute-start.9 = (bf16[256,768]{1,0:T(8,128)(2,1)S(1)}, bf16[256,768]{1,0:T(8,128)(2,1)S(1)}, u32[]{:S(2)}, u32[]{:S(2)}) collective-permute-start(bf16[256,768]{1,0:T(8,128)(2,1)S(1)} %collective-permute-done.8.refs_2_), channel_id=1, source_target_pairs={{0,1},{1,0},{2,3},{3,2},{4,5},{5,4},{6,7},{7,6},{8,9},{9,8},{10,11... | collective-permute-start | bytes 1179656 | tf_op jit(solution)/shard_map/ppermute | solution.py:31
  74.1 27.4 %collective-permute-start.11 = (bf16[256,768]{1,0:T(8,128)(2,1)S(1)}, bf16[256,768]{1,0:T(8,128)(2,1)S(1)}, u32[]{:S(2)}, u32[]{:S(2)}) collective-permute-start(bf16[256,768]{1,0:T(8,128)(2,1)S(1)} %collective-permute-done.10.refs_4_), channel_id=1, source_target_pairs={{0,1},{1,0},{2,3},{3,2},{4,5},{5,4},{6,7},{7,6},{8,9},{9,8},{10,11... | collective-permute-start | bytes 1179656 | tf_op jit(solution)/shard_map/ppermute | solution.py:31
  86.6 28.9 %collective-permute-start.5 = (bf16[256,768]{1,0:T(8,128)(2,1)S(1)}, bf16[256,768]{1,0:T(8,128)(2,1)S(1)}, u32[]{:S(2)}, u32[]{:S(2)}) collective-permute-start(bf16[256,768]{1,0:T(8,128)(2,1)S(1)} %collective-permute-done.4.refs_2_), channel_id=1, source_target_pairs={{0,1},{1,0},{2,3},{3,2},{4,5},{5,4},{6,7},{7,6},{8,9},{9,8},{10,11... | collective-permute-start | bytes 1179656 | tf_op jit(solution)/shard_map/ppermute | solution.py:31
  88.7 26.8 %collective-permute-start.7 = (bf16[256,768]{1,0:T(8,128)(2,1)S(1)}, bf16[256,768]{1,0:T(8,128)(2,1)S(1)}, u32[]{:S(2)}, u32[]{:S(2)}) collective-permute-start(bf16[256,768]{1,0:T(8,128)(2,1)S(1)} %collective-permute-done.6.refs_4_), channel_id=1, source_target_pairs={{0,1},{1,0},{2,3},{3,2},{4,5},{5,4},{6,7},{7,6},{8,9},{9,8},{10,11... | collective-permute-start | bytes 1179656 | tf_op jit(solution)/shard_map/ppermute | solution.py:31
  111.9 3.7 %copy-start = (f32[576,4096]{1,0:T(8,128)}, f32[576,4096]{1,0:T(8,128)S(1)}, u32[]{:S(2)}) copy-start(f32[576,4096]{1,0:T(8,128)S(1)} %shard_map.70.refs_7_) | copy-start | bytes 28311556

commit v2 on v0

v2 whole, which is shorter than its diff:
```python
import functools

import jax
import jax.numpy as jnp
from jax import lax
from jax.experimental import pallas as pl
from jax.experimental.pallas import tpu as pltpu
from jax.sharding import PartitionSpec as P

MEBI = 1024 * 1024
NT = (((1,), (1,)), ((), ()))
EXTRA = 16


def from_next(x):
    sections = lax.axis_size("pipe")
    return lax.ppermute(x, "pipe", [(s, (s - 1) % sections) for s in range(sections)])


def from_next_share(x, dp_xor):
    sections, shares = lax.axis_size("pipe"), lax.axis_size("dp")
    pairs = [
        (s * shares + z, (s - 1) * shares + (z ^ dp_xor))
        for s in range(1, sections)
        for z in range(shares)
    ]
    return lax.ppermute(x, ("pipe", "dp"), pairs)


def from_share(x, dp_xor):
    sections, shares = lax.axis_size("pipe"), lax.axis_size("dp")
    pairs = [
        (s * shares + z, s * shares + (z ^ dp_xor))
        for s in range(sections - 1)
        for z in range(shares)
    ]
    return lax.ppermute(x, ("pipe", "dp"), pairs)


def swap(x, bit):
    experts = lax.axis_size("expert")
    return lax.ppermute(x, "expert", [(e, e ^ bit) for e in range(experts)])


def after(x, *first):
    return lax.optimization_barrier((x, *first))[0]


def thirds(x):
    high = lax.reduce_precision(x, 8, 7)
    middle = lax.reduce_precision(x - high, 8, 7)
    return [high, middle, x - high - middle]


def place_kernel(expert_ref, meta_ref, places_ref, weights_ref):
    expert = expert_ref[0]
    groups, _, tokens = meta_ref.shape
    micros = meta_ref.shape[1] // 4
    rows = places_ref.shape[1]
    earlier = lax.broadcasted_iota(jnp.int32, (tokens, tokens), 0) < lax.broadcasted_iota(
        jnp.int32, (tokens, tokens), 1
    )
    earlier = earlier.astype(jnp.bfloat16)
    row = lax.broadcasted_iota(jnp.int32, (rows, tokens), 0)
    weights = []
    for micro in range(micros):
        for j in range(groups):
            meta = meta_ref[j]
            first = meta[4 * micro : 4 * micro + 1] == expert.astype(jnp.float32)
            second = meta[4 * micro + 1 : 4 * micro + 2] == expert.astype(jnp.float32)
            here = jnp.logical_or(first, second)
            weights.append(
                jnp.where(
                    first, meta[4 * micro + 2 : 4 * micro + 3], meta[4 * micro + 3 : 4 * micro + 4]
                )
            )
            named = jnp.broadcast_to(here.astype(jnp.float32), (16, tokens)).astype(jnp.bfloat16)
            slot = jnp.dot(named, earlier, preferred_element_type=jnp.float32)[0:1]
            target = slot.astype(jnp.int32) * groups + (expert ^ j)
            picked = row == jnp.where(here, target, -1)
            places_ref[micro, :, j * tokens : (j + 1) * tokens] = picked.astype(
                jnp.float32
            ).astype(jnp.bfloat16)
    weights = jnp.concatenate(weights, 0)
    padding = jnp.zeros((tokens - weights.shape[0], tokens), jnp.float32)
    weights_ref[...] = jnp.transpose(jnp.concatenate([weights, padding], 0))


def find_places(expert, meta, cap):
    groups, quads, tokens = meta.shape
    micros = quads // 4
    in_vmem = pl.BlockSpec(memory_space=pltpu.VMEM)
    return pl.pallas_call(
        place_kernel,
        in_specs=[pl.BlockSpec(memory_space=pltpu.SMEM), in_vmem],
        out_specs=[in_vmem, in_vmem],
        out_shape=[
            jax.ShapeDtypeStruct((micros, cap * groups, groups * tokens), jnp.bfloat16),
            jax.ShapeDtypeStruct((tokens, tokens), jnp.float32),
        ],
        compiler_params=pltpu.CompilerParams(vmem_limit_bytes=16 * MEBI),
    )(expert, meta)


def fill_kernel(cut, places_ref, weights_ref, *refs):
    token_refs, rows_ref = refs[:-1], refs[-1]
    micros, rows, _ = places_ref.shape
    tokens = weights_ref.shape[0]
    half = len(token_refs)
    late = micros * tokens - cut
    for micro in range(micros):
        blocks = []
        for j in range(2 * half):
            source, top = token_refs[j % half], j // half
            low, high = micro * tokens, (micro + 1) * tokens
            pieces = []
            if low < cut:
                pieces.append(source[top * cut + low : top * cut + min(high, cut), :])
            if high > cut:
                at = 2 * cut + top * late - cut
                pieces.append(source[at + max(low, cut) : at + high, :])
            held = pieces[0] if len(pieces) == 1 else jnp.concatenate(pieces, 0)
            weight = weights_ref[:, micro * 2 * half + j : micro * 2 * half + j + 1]
            blocks.append((held.astype(jnp.float32) * weight).astype(jnp.bfloat16))
        rows_ref[micro * rows : (micro + 1) * rows, :] = jnp.dot(
            places_ref[micro], jnp.concatenate(blocks, 0), preferred_element_type=jnp.float32
        ).astype(jnp.bfloat16)


def fill_rows(places, weights, tokens, cut):
    micros, rows, _ = places.shape
    depth = tokens[0].shape[1]
    in_vmem = pl.BlockSpec(memory_space=pltpu.VMEM)
    return pl.pallas_call(
        functools.partial(fill_kernel, cut),
        in_specs=[in_vmem] * (2 + len(tokens)),
        out_specs=in_vmem,
        out_shape=jax.ShapeDtypeStruct((micros * rows, depth), jnp.bfloat16),
        compiler_params=pltpu.CompilerParams(vmem_limit_bytes=24 * MEBI),
    )(places, weights, *tokens)


def part_kernel(parts, groups, first, last, *refs):
    place_ref = refs[0]
    row_refs = refs[1 : 1 + parts]
    weight_ref = refs[1 + parts]
    rest = refs[2 + parts :]
    step = pl.program_id(0)
    block, depth = weight_ref.shape[1], row_refs[0].shape[1]
    here = pl.ds(pl.multiple_of(step * block, block), block)
    product = None
    for part in range(parts):
        at = pl.multiple_of((place_ref[1] ^ part) * depth, depth)
        term = lax.dot_general(
            row_refs[part][...],
            weight_ref[0, :, pl.ds(at, depth)],
            NT,
            preferred_element_type=jnp.float32,
        )
        product = term if product is None else product + term
    if not first:
        product = product + rest[0][:, here]
    out_ref = rest[-1]
    if not last:
        out_ref[:, here] = product
    else:
        micros, cap = out_ref.shape[1], out_ref.shape[3]
        rows = cap * groups
        for micro in range(micros):
            out_ref[0, micro, 0] = (
                product[micro * rows : (micro + 1) * rows]
                .reshape(cap, groups, block)
                .astype(out_ref.dtype)
            )


def add_part(place, rows, weights, total, micros, groups, last):
    count, depth = rows[0].shape
    hidden = weights.shape[1]
    block = min(1024, hidden)
    in_vmem = pl.BlockSpec(memory_space=pltpu.VMEM)
    in_specs = [in_vmem] * len(rows)
    in_specs.append(pl.BlockSpec((1, block, depth * len(rows)), lambda f, p: (0, f, p[0])))
    args = [place, *rows, weights]
    if total is not None:
        in_specs.append(in_vmem)
        args.append(total)
    if last:
        cap = count // (micros * groups)
        out_shape = jax.ShapeDtypeStruct((1, micros, 1, cap, groups, hidden), jnp.bfloat16)
        out_spec = pl.BlockSpec(
            (1, micros, 1, cap, groups, block), lambda f, p: (0, 0, 0, 0, 0, f)
        )
    else:
        out_shape = jax.ShapeDtypeStruct((count, hidden), jnp.float32)
        out_spec = in_vmem
    return pl.pallas_call(
        functools.partial(part_kernel, len(rows), groups, total is None, last),
        grid_spec=pltpu.PrefetchScalarGridSpec(
            num_scalar_prefetch=1,
            grid=(hidden // block,),
            in_specs=in_specs,
            out_specs=out_spec,
        ),
        out_shape=out_shape,
        compiler_params=pltpu.CompilerParams(vmem_limit_bytes=36 * MEBI),
        cost_estimate=pl.CostEstimate(
            flops=2 * count * depth * len(rows) * hidden,
            bytes_accessed=2 * hidden * depth * len(rows),
            transcendentals=0,
        ),
    )(*args)


def per_device(out_grad, expert_outputs, logits, routes, down_weights):
    micros, token_count, share = out_grad.shape[1:]
    experts, shares = lax.axis_size("expert"), lax.axis_size("dp")
    cap = min(token_count, 2 * token_count // experts + token_count // 32)
    expert, mine = lax.axis_index("expert"), lax.axis_index("dp")
    received = lax.axis_index("pipe") < lax.axis_size("pipe") - 1
    top = experts // 2

    own = out_grad.reshape(micros * token_count, share)
    cut = micros * token_count * 11 // 16
    early, late = own[:cut], own[cut:]

    grads = out_grad[0].astype(jnp.float32)
    outputs = expert_outputs[0].astype(jnp.float32)
    difference = jnp.sum(grads * (outputs[:, :, 0] - outputs[:, :, 1]), -1)
    named = routes[0].astype(jnp.float32)
    gap = logits[0, ..., 0] - logits[0, ..., 1]
    extra = jnp.stack(
        [named[..., 0], named[..., 1], *thirds(gap), *thirds(difference)], 0
    ).reshape(EXTRA, token_count)
    extra = jnp.pad(extra.astype(jnp.bfloat16), ((0, 0), (0, share - token_count)))

    late = from_next(late)
    direct = {}
    for k in range(2, shares):
        direct[k] = from_next_share(early if k < 3 else after(early, direct[k - 1]), k)
    direct[1] = from_next_share(early, 1)
    zero = from_next(jnp.concatenate([early, extra], 0))
    late_top = swap(late, top)
    direct[0], extra = zero[:cut], zero[cut:]
    zero_top = swap(zero, top)
    direct_top = {0: zero_top[:cut]}
    for k in range(1, shares):
        direct_top[k] = swap(direct[k], top)
    pair = jnp.concatenate([late, late_top, extra], 0)
    pairs = {0: pair}
    for k in range(1, shares):
        pairs[k] = from_share(pair, k)

    def spread(x):
        held, bit = {0: x}, top // 2
        while bit:
            for j in sorted(held):
                held[j ^ bit] = swap(held[j], bit)
            bit //= 2
        return [held[j] for j in sorted(held)]

    extras = spread(jnp.stack([extra[:, :token_count], zero_top[cut:, :token_count]]))
    extras = jnp.concatenate([jnp.stack([e[b] for e in extras]) for b in range(2)], 0)
    extras = extras.astype(jnp.float32).reshape(experts, 8, micros, token_count)
    gap = extras[:, 2] + extras[:, 3] + extras[:, 4]
    weight_first, weight_second = jax.nn.sigmoid(gap), jax.nn.sigmoid(-gap)
    meta = jnp.stack(
        [
            extras[:, 0],
            extras[:, 1],
            jnp.where(received, weight_first, 0.0),
            jnp.where(received, weight_second, 0.0),
        ],
        2,
    ).reshape(experts, 4 * micros, token_count)

    scores = 0.0
    for k in range(shares):
        terms = pairs[k][-EXTRA:, :token_count].astype(jnp.float32)
        terms = terms.reshape(8, micros, token_count)
        scores += terms[5] + terms[6] + terms[7]
    slope = jnp.where(received, weight_first[0] * weight_second[0] * scores, 0.0)
    moved_logits = jnp.stack([slope, -slope], -1).astype(jnp.bfloat16)[None]

    places, weights = find_places(expert.astype(jnp.int32)[None], meta, cap)

    together = 1
    while (share * together) % 128:
        together *= 2
    rows = []
    for part in range(0, shares, together):
        pieces = []
        for k in range(part, part + together):
            block = jnp.concatenate([direct[k], direct_top[k], pairs[k][:-EXTRA]], 0)
            pieces.append(spread(block))
        tokens = pieces[0]
        if together > 1:
            order = jnp.arange(together) ^ (mine % together)
            tokens = []
            for j in range(top):
                stacked = jnp.take(jnp.stack([piece[j] for piece in pieces]), order, axis=0)
                tokens.append(stacked.transpose(1, 0, 2).reshape(-1, together * share))
        rows.append(fill_rows(places, weights, tokens, cut))
    half = len(rows) // 2
    which = mine // together
    total = None
    for side in range(2):
        place = jnp.stack([(which // half) ^ side, which % half]).astype(jnp.int32)
        total = add_part(
            place,
            rows[side * half : (side + 1) * half],
            down_weights,
            total,
            micros,
            experts,
            side == 1,
        )
    return total.transpose(0, 1, 2, 4, 3, 5), moved_logits


def solution(mesh):
    in_specs = (
        P("pipe", None, "expert", "dp"),
        P("pipe", None, "expert", None, "dp"),
        P("pipe", None, "expert", None),
        P("pipe", None, "expert", None),
        P("expert", "dp", None),
    )
    out_specs = (P("pipe", None, "expert", None, None, "dp"), P("pipe", None, "expert", None))
    return jax.shard_map(
        per_device, mesh=mesh, in_specs=in_specs, out_specs=out_specs, check_vma=False
    )
```

time: 252 us -> 91.6 us (0.36)
  the two profiles are of different devices: /device:TPU:9 before, /device:TPU:1 now
where the time goes in v2:
time: 91.6 us; the launch traced here: 91.1 us
  starting transfers between devices  38.5 us (42%)
  Pallas kernels  25.4 us (28%)
  waiting for transfers between devices  19.7 us (22%)
  other arithmetic  3.92 us (4%)
  local copies, waits for them, and re-layouts  2.59 us (3%)
  between operations  0.98 us (1%)
    pallas_call x2, Pallas kernels, add_part(): pl.pallas_call(functools.partial(part_kernel, len(rows), groups, total is...  22.1 us
    ppermute x3, starting transfers between devices, from_share(): return lax.ppermute(x, ('pipe', 'dp'), pairs)  16.6 us
    ppermute x10, starting transfers between devices, swap(): return lax.ppermute(x, 'expert', [(e, e ^ bit) for e in range(experts)])  11.8 us
    ppermute x3, waiting for transfers between devices, from_share(): return lax.ppermute(x, ('pipe', 'dp'), pairs)  6.95 us
    ppermute x2, starting transfers between devices, from_next(): lax.ppermute(x, 'pipe', [(s, (s - 1) % sections) for s in range(sections)])  6.29 us
    ppermute x2, waiting for transfers between devices, from_next(): lax.ppermute(x, 'pipe', [(s, (s - 1) % sections) for s in range(sections)])  4.99 us
    ppermute x10, waiting for transfers between devices, swap(): return lax.ppermute(x, 'expert', [(e, e ^ bit) for e in range(experts)])  4.01 us
    ppermute x3, starting transfers between devices, from_next_share(): return lax.ppermute(x, ('pipe', 'dp'), pairs)  3.84 us
  transfers between devices with their start and end apart: 18, of which 7 were waited for; matrix products, arithmetic and copies ran while one was open for 1% of the time, Pallas kernels for 14%

profile of v2, /device:TPU:1, one launch (start us, length us, event | category | flops | bytes accessed | tf_op | source)
XLA Modules:
  0.0 91.1 jit_solution(14676461348785430525)
XLA Ops:
  0.6 0.7 fusion.8
  1.3 0.8 fusion.20
  2.1 1.0 %slice.180 = bf16[176,768]{1,0:T(8,128)(2,1)S(1)} slice(bf16[256,768]{1,0:T(8,128)(2,1)} %bitcast.100), slice={[0:176], [0:768]} | slice | bytes 540672 | tf_op jit(solution)/shard_map/slice | solution.py:225
  3.1 1.7 %bitcast_convert_fusion = f32[2,128,2,768]{3,2,1,0:T(2,128)S(1)} fusion(bf16[1,2,128,2,768]{4,3,2,1,0:T(2,128)(2,1)} %param.6), kind=kLoop, calls=%fused_computation.7 | loop fusion | flops 393216 | bytes 2359296 | tf_op jit(solution)/shard_map/convert_element_type | solution.py:228
  4.8 0.8 slice_subtract_fusion
  6.0 2.1 %collective-permute-start = (bf16[192,768]{1,0:T(8,128)(2,1)S(1)}, bf16[192,768]{1,0:T(8,128)(2,1)S(1)}, u32[]{:S(2)}, u32[]{:S(2)}) collective-permute-start(bf16[192,768]{1,0:T(8,128)(2,1)S(1)} %fusion.2), channel_id=1, source_target_pairs={{0,16},{16,0},{1,17},{17,1},{2,18},{18,2},{3,19},{19,3},{4,20},{20... | collective-permute-start | bytes 884744 | tf_op jit(solution)/shard_map/ppermute | solution.py:17
  8.1 1.3 %collective-permute-start.3 = (bf16[176,768]{1,0:T(8,128)(2,1)S(1)}, bf16[176,768]{1,0:T(8,128)(2,1)S(1)}, u32[]{:S(2)}, u32[]{:S(2)}) collective-permute-start(bf16[176,768]{1,0:T(8,128)(2,1)S(1)} %slice.180), channel_id=1, source_target_pairs={{16,8},{20,12},{24,0},{28,4},{17,9},{21,13},{25,1},{29,5},{18,10},... | collective-permute-start | bytes 811016 | tf_op jit(solution)/shard_map/ppermute | solution.py:27
  9.4 4.2 %collective-permute-start.5 = (bf16[80,768]{1,0:T(8,128)(2,1)S(1)}, bf16[80,768]{1,0:T(8,128)(2,1)S(1)}, u32[]{:S(2)}, u32[]{:S(2)}) collective-permute-start(bf16[80,768]{1,0:T(8,128)(2,1)S(1)} %slice.189), channel_id=1, source_target_pairs={{0,16},{16,0},{1,17},{17,1},{2,18},{18,2},{3,19},{19,3},{4,20},{20... | collective-permute-start | bytes 368648 | tf_op jit(solution)/shard_map/ppermute | solution.py:17
  13.6 5.0 %collective-permute-done.5 = bf16[80,768]{1,0:T(8,128)(2,1)S(1)} collective-permute-done((bf16[80,768]{1,0:T(8,128)(2,1)S(1)}, bf16[80,768]{1,0:T(8,128)(2,1)S(1)}, u32[]{:S(2)}, u32[]{:S(2)}) %collective-permute-start.5) | collective-permute-done | bytes 122912 | tf_op jit(solution)/shard_map/ppermute | solution.py:17
  18.6 1.2 %collective-permute-start.6 = (bf16[80,768]{1,0:T(8,128)(2,1)S(1)}, bf16[80,768]{1,0:T(8,128)(2,1)S(1)}, u32[]{:S(2)}, u32[]{:S(2)}) collective-permute-start(bf16[80,768]{1,0:T(8,128)(2,1)S(1)} %collective-permute-done.5), channel_id=1, source_target_pairs={{0,2},{1,3},{2,0},{3,1},{4,6},{5,7},{6,4},{7,5},{8,10},{9,11},{10,... | collective-permute-start | bytes 368648 | tf_op jit(solution)/shard_map/ppermute | solution.py:42
  19.8 1.3 %collective-permute-start.14 = (bf16[176,768]{1,0:T(8,128)(2,1)S(1)}, bf16[176,768]{1,0:T(8,128)(2,1)S(1)}, u32[]{:S(2)}, u32[]{:S(2)}) collective-permute-start(bf16[176,768]{1,0:T(8,128)(2,1)S(1)} %slice.180), channel_id=1, source_target_pairs={{16,4},{20,0},{24,12},{28,8},{17,5},{21,1},{25,13},{29,9},{18,6},{... | collective-permute-start | bytes 811016 | tf_op jit(solution)/shard_map/ppermute | solution.py:27
  21.2 3.8 %collective-permute-done.3 = bf16[176,768]{1,0:T(8,128)(2,1)S(1)} collective-permute-done((bf16[176,768]{1,0:T(8,128)(2,1)S(1)}, bf16[176,768]{1,0:T(8,128)(2,1)S(1)}, u32[]{:S(2)}, u32[]{:S(2)}) %collective-permute-start.3) | collective-permute-done | bytes 270368 | tf_op jit(solution)/shard_map/ppermute | solution.py:27
  24.9 1.3 %collective-permute-start.9 = (bf16[176,768]{1,0:T(8,128)(2,1)S(1)}, bf16[176,768]{1,0:T(8,128)(2,1)S(1)}, u32[]{:S(2)}, u32[]{:S(2)}) collective-permute-start(bf16[176,768]{1,0:T(8,128)(2,1)S(1)} %slice.180), channel_id=1, source_target_pairs={{16,12},{20,8},{24,4},{28,0},{17,13},{21,9},{25,5},{29,1},{18,14},... | collective-permute-start | bytes 811016 | tf_op jit(solution)/shard_map/ppermute | solution.py:27
  26.2 1.3 %collective-permute-start.4 = (bf16[176,768]{1,0:T(8,128)(2,1)S(1)}, bf16[176,768]{1,0:T(8,128)(2,1)S(1)}, u32[]{:S(2)}, u32[]{:S(2)}) collective-permute-start(bf16[176,768]{1,0:T(8,128)(2,1)S(1)} %collective-permute-done.3), channel_id=1, source_target_pairs={{0,2},{1,3},{2,0},{3,1},{4,6},{5,7},{6,4},{7,5},{8,10},{9,11},{10,... | collective-permute-start | bytes 811016 | tf_op jit(solution)/shard_map/ppermute | solution.py:42
  27.6 4.1 %collective-permute-start.7 = (bf16[176,768]{1,0:T(8,128)(2,1)S(1)}, bf16[176,768]{1,0:T(8,128)(2,1)S(1)}, u32[]{:S(2)}, u32[]{:S(2)}) collective-permute-start(bf16[176,768]{1,0:T(8,128)(2,1)S(1)} %pad_maximum_fusion.4), channel_id=1, source_target_pairs={{0,8},{4,12},{8,0},{12,4},{1,9},{5,13},{9,1},{13,5},{2,10},{6,14},... | collective-permute-start | bytes 811016 | tf_op jit(solution)/shard_map/ppermute | solution.py:37
  31.8 1.3 %collective-permute-start.15 = (bf16[176,768]{1,0:T(8,128)(2,1)S(1)}, bf16[176,768]{1,0:T(8,128)(2,1)S(1)}, u32[]{:S(2)}, u32[]{:S(2)}) collective-permute-start(bf16[176,768]{1,0:T(8,128)(2,1)S(1)} %collective-permute-done.14), channel_id=1, source_target_pairs={{0,2},{1,3},{2,0},{3,1},{4,6},{5,7},{6,4},{7,5},{8,10},{9,11},{10,... | collective-permute-start | bytes 811016 | tf_op jit(solution)/shard_map/ppermute | solution.py:42
  33.0 5.5 %collective-permute-start.16 = (bf16[176,768]{1,0:T(8,128)(2,1)S(1)}, bf16[176,768]{1,0:T(8,128)(2,1)S(1)}, u32[]{:S(2)}, u32[]{:S(2)}) collective-permute-start(bf16[176,768]{1,0:T(8,128)(2,1)S(1)} %pad_maximum_fusion.4), channel_id=1, source_target_pairs={{0,4},{4,0},{8,12},{12,8},{1,5},{5,1},{9,13},{13,9},{2,6},{6,2},{1... | collective-permute-start | bytes 811016 | tf_op jit(solution)/shard_map/ppermute | solution.py:37
  38.6 4.0 %collective-permute-done.7 = bf16[176,768]{1,0:T(8,128)(2,1)S(1)} collective-permute-done((bf16[176,768]{1,0:T(8,128)(2,1)S(1)}, bf16[176,768]{1,0:T(8,128)(2,1)S(1)}, u32[]{:S(2)}, u32[]{:S(2)}) %collective-permute-start.7) | collective-permute-done | bytes 270368 | tf_op jit(solution)/shard_map/ppermute | solution.py:37
  42.6 7.0 %collective-permute-start.11 = (bf16[176,768]{1,0:T(8,128)(2,1)S(1)}, bf16[176,768]{1,0:T(8,128)(2,1)S(1)}, u32[]{:S(2)}, u32[]{:S(2)}) collective-permute-start(bf16[176,768]{1,0:T(8,128)(2,1)S(1)} %pad_maximum_fusion.4), channel_id=1, source_target_pairs={{0,12},{4,8},{8,4},{12,0},{1,13},{5,9},{9,5},{13,1},{2,14},{6,10},... | collective-permute-start | bytes 811016 | tf_op jit(solution)/shard_map/ppermute | solution.py:37
  49.6 1.3 %collective-permute-start.1 = (bf16[192,768]{1,0:T(8,128)(2,1)S(1)}, bf16[192,768]{1,0:T(8,128)(2,1)S(1)}, u32[]{:S(2)}, u32[]{:S(2)}) collective-permute-start(bf16[192,768]{1,0:T(8,128)(2,1)S(1)} %collective-permute-done), channel_id=1, source_target_pairs={{0,2},{1,3},{2,0},{3,1},{4,6},{5,7},{6,4},{7,5},{8,10},{9,11},{10,... | collective-permute-start | bytes 884744 | tf_op jit(solution)/shard_map/ppermute | solution.py:42
  51.2 1.5 %collective-permute-start.8 = (bf16[512,768]{1,0:T(8,128)(2,1)S(1)}, bf16[512,768]{1,0:T(8,128)(2,1)S(1)}, u32[]{:S(2)}, u32[]{:S(2)}) collective-permute-start(bf16[512,768]{1,0:T(8,128)(2,1)S(1)} %pad_maximum_fusion.refs_0_), channel_id=1, source_target_pairs={{0,1},{1,0},{2,3},{3,2},{4,5},{5,4},{6,7},{7,6},{8,9},{9,8},{10,11... | collective-permute-start | bytes 2359304 | tf_op jit(solution)/shard_map/ppermute | solution.py:42
  52.9 2.9 %collective-permute-done.11 = bf16[176,768]{1,0:T(8,128)(2,1)S(1)} collective-permute-done((bf16[176,768]{1,0:T(8,128)(2,1)S(1)}, bf16[176,768]{1,0:T(8,128)(2,1)S(1)}, u32[]{:S(2)}, u32[]{:S(2)}) %collective-permute-start.11) | collective-permute-done | bytes 270368 | tf_op jit(solution)/shard_map/ppermute | solution.py:37
  55.9 1.5 %collective-permute-done.1 = bf16[192,768]{1,0:T(8,128)(2,1)S(1)} collective-permute-done((bf16[192,768]{1,0:T(8,128)(2,1)S(1)}, bf16[192,768]{1,0:T(8,128)(2,1)S(1)}, u32[]{:S(2)}, u32[]{:S(2)}) %collective-permute-start.1) | collective-permute-done | bytes 294944 | tf_op jit(solution)/shard_map/ppermute | solution.py:42
  57.4 3.1 %collective-permute-start.2 = (bf16[2,16,128]{2,1,0:T(8,128)(2,1)S(1)}, bf16[2,16,128]{2,1,0:T(8,128)(2,1)S(1)}, u32[]{:S(2)}, u32[]{:S(2)}) collective-permute-start(bf16[2,16,128]{2,1,0:T(8,128)(2,1)S(1)} %pad_maximum_fusion.6), channel_id=1, source_target_pairs={{0,1},{1,0},{2,3},{3,2},{4,5},{5,4},{6,7},{7,6},{8,9},{9,8},{10,11... | collective-permute-start | bytes 24584 | tf_op jit(solution)/shard_map/ppermute | solution.py:42
  61.4 1.8 %collective-permute-done.10 = bf16[176,768]{1,0:T(8,128)(2,1)S(1)} collective-permute-done((bf16[176,768]{1,0:T(8,128)(2,1)S(1)}, bf16[176,768]{1,0:T(8,128)(2,1)S(1)}, u32[]{:S(2)}, u32[]{:S(2)}) %collective-permute-start.10) | collective-permute-done | bytes 270368 | tf_op jit(solution)/shard_map/ppermute | solution.py:42
  63.2 1.8 %collective-permute-start.12 = (bf16[512,768]{1,0:T(8,128)(2,1)S(1)}, bf16[512,768]{1,0:T(8,128)(2,1)S(1)}, u32[]{:S(2)}, u32[]{:S(2)}) collective-permute-start(bf16[512,768]{1,0:T(8,128)(2,1)S(1)} %pad_maximum_fusion.1.refs_0_), channel_id=1, source_target_pairs={{0,1},{1,0},{2,3},{3,2},{4,5},{5,4},{6,7},{7,6},{8,9},{9,8},{10,11... | collective-permute-start | bytes 2359304 | tf_op jit(solution)/shard_map/ppermute | solution.py:42
  66.0 0.7 shard_map.69.refs_1_
  66.7 0.7 shard_map.72.refs_2_
  67.5 0.7 shard_map.71.refs_1_
  68.2 10.2 %shard_map.73.refs_4_ = f32[544,4096]{1,0:T(8,128)S(1)} custom-call(s32[2]{0:T(128)S(1)} %pad_add_fusion.1.refs_0_, bf16[544,768]{1,0:T(8,128)(2,1)S(1)} %shard_map.71.refs_1_, bf16[544,768]{1,0:T(8,128)(2,1)S(1)} %shard_map.72.refs_2_, bf16[1,4096,3072]{2,1,0:T(8,128)(2,1)} %refs_3_.3), custom_call_target="tpu_custom_call" | custom-call | flops 6845104128 | bytes 12582912 | tf_op jit(solution)/shard_map/pallas_call | solution.py:197
  78.5 0.7 shard_map.70.refs_2_
  79.2 11.9 %shard_map.74 = bf16[1,2,1,68,4,4096]{5,4,3,2,1,0:T(4,128)(2,1)} custom-call(s32[2]{0:T(128)S(1)} %pad_add_fusion.refs_0_, bf16[544,768]{1,0:T(8,128)(2,1)S(1)} %shard_map.69.refs_1_, bf16[544,768]{1,0:T(8,128)(2,1)S(1)} %shard_map.70.refs_2_, bf16[1,4096,3072]{2,1,0:T(8,128)(2,1)} %refs_3_.3, f32[544,4096]{1,0:T(8,128)S(1)} %shard_map.73.refs_4_), custom_call_target="tpu_custom_call" | custom-call | flops 6845104128 | bytes 12582912 | tf_op jit(solution)/shard_map/pallas_call | solution.py:197
  (58 shorter events, 3.0 us)
Async XLA Ops:
  4.8 1.0 %copy-start = (bf16[1,2,128,768]{3,2,1,0:T(8,128)(2,1)S(1)}, bf16[1,2,128,768]{3,2,1,0:T(8,128)(2,1)}, u32[]{:S(2)}) copy-start(bf16[1,2,128,768]{3,2,1,0:T(8,128)(2,1)} %param.5) | copy-start | bytes 1179652
  6.0 21.5 %collective-permute-start = (bf16[192,768]{1,0:T(8,128)(2,1)S(1)}, bf16[192,768]{1,0:T(8,128)(2,1)S(1)}, u32[]{:S(2)}, u32[]{:S(2)}) collective-permute-start(bf16[192,768]{1,0:T(8,128)(2,1)S(1)} %fusion.2), channel_id=1, source_target_pairs={{0,16},{16,0},{1,17},{17,1},{2,18},{18,2},{3,19},{19,3},{4,20},{20... | collective-permute-start | bytes 884744 | tf_op jit(solution)/shard_map/ppermute | solution.py:17
  8.1 16.8 %collective-permute-start.3 = (bf16[176,768]{1,0:T(8,128)(2,1)S(1)}, bf16[176,768]{1,0:T(8,128)(2,1)S(1)}, u32[]{:S(2)}, u32[]{:S(2)}) collective-permute-start(bf16[176,768]{1,0:T(8,128)(2,1)S(1)} %slice.180), channel_id=1, source_target_pairs={{16,8},{20,12},{24,0},{28,4},{17,9},{21,13},{25,1},{29,5},{18,10},... | collective-permute-start | bytes 811016 | tf_op jit(solution)/shard_map/ppermute | solution.py:27
  9.4 9.2 %collective-permute-start.5 = (bf16[80,768]{1,0:T(8,128)(2,1)S(1)}, bf16[80,768]{1,0:T(8,128)(2,1)S(1)}, u32[]{:S(2)}, u32[]{:S(2)}) collective-permute-start(bf16[80,768]{1,0:T(8,128)(2,1)S(1)} %slice.189), channel_id=1, source_target_pairs={{0,16},{16,0},{1,17},{17,1},{2,18},{18,2},{3,19},{19,3},{4,20},{20... | collective-permute-start | bytes 368648 | tf_op jit(solution)/shard_map/ppermute | solution.py:17
  18.6 8.9 %collective-permute-start.6 = (bf16[80,768]{1,0:T(8,128)(2,1)S(1)}, bf16[80,768]{1,0:T(8,128)(2,1)S(1)}, u32[]{:S(2)}, u32[]{:S(2)}) collective-permute-start(bf16[80,768]{1,0:T(8,128)(2,1)S(1)} %collective-permute-done.5), channel_id=1, source_target_pairs={{0,2},{1,3},{2,0},{3,1},{4,6},{5,7},{6,4},{7,5},{8,10},{9,11},{10,... | collective-permute-start | bytes 368648 | tf_op jit(solution)/shard_map/ppermute | solution.py:42
  19.8 12.0 %collective-permute-start.14 = (bf16[176,768]{1,0:T(8,128)(2,1)S(1)}, bf16[176,768]{1,0:T(8,128)(2,1)S(1)}, u32[]{:S(2)}, u32[]{:S(2)}) collective-permute-start(bf16[176,768]{1,0:T(8,128)(2,1)S(1)} %slice.180), channel_id=1, source_target_pairs={{16,4},{20,0},{24,12},{28,8},{17,5},{21,1},{25,13},{29,9},{18,6},{... | collective-permute-start | bytes 811016 | tf_op jit(solution)/shard_map/ppermute | solution.py:27
  24.9 24.7 %collective-permute-start.9 = (bf16[176,768]{1,0:T(8,128)(2,1)S(1)}, bf16[176,768]{1,0:T(8,128)(2,1)S(1)}, u32[]{:S(2)}, u32[]{:S(2)}) collective-permute-start(bf16[176,768]{1,0:T(8,128)(2,1)S(1)} %slice.180), channel_id=1, source_target_pairs={{16,12},{20,8},{24,4},{28,0},{17,13},{21,9},{25,5},{29,1},{18,14},... | collective-permute-start | bytes 811016 | tf_op jit(solution)/shard_map/ppermute | solution.py:27
  26.2 24.7 %collective-permute-start.4 = (bf16[176,768]{1,0:T(8,128)(2,1)S(1)}, bf16[176,768]{1,0:T(8,128)(2,1)S(1)}, u32[]{:S(2)}, u32[]{:S(2)}) collective-permute-start(bf16[176,768]{1,0:T(8,128)(2,1)S(1)} %collective-permute-done.3), channel_id=1, source_target_pairs={{0,2},{1,3},{2,0},{3,1},{4,6},{5,7},{6,4},{7,5},{8,10},{9,11},{10,... | collective-permute-start | bytes 811016 | tf_op jit(solution)/shard_map/ppermute | solution.py:42
  27.6 15.0 %collective-permute-start.7 = (bf16[176,768]{1,0:T(8,128)(2,1)S(1)}, bf16[176,768]{1,0:T(8,128)(2,1)S(1)}, u32[]{:S(2)}, u32[]{:S(2)}) collective-permute-start(bf16[176,768]{1,0:T(8,128)(2,1)S(1)} %pad_maximum_fusion.4), channel_id=1, source_target_pairs={{0,8},{4,12},{8,0},{12,4},{1,9},{5,13},{9,1},{13,5},{2,10},{6,14},... | collective-permute-start | bytes 811016 | tf_op jit(solution)/shard_map/ppermute | solution.py:37
  31.8 21.0 %collective-permute-start.15 = (bf16[176,768]{1,0:T(8,128)(2,1)S(1)}, bf16[176,768]{1,0:T(8,128)(2,1)S(1)}, u32[]{:S(2)}, u32[]{:S(2)}) collective-permute-start(bf16[176,768]{1,0:T(8,128)(2,1)S(1)} %collective-permute-done.14), channel_id=1, source_target_pairs={{0,2},{1,3},{2,0},{3,1},{4,6},{5,7},{6,4},{7,5},{8,10},{9,11},{10,... | collective-permute-start | bytes 811016 | tf_op jit(solution)/shard_map/ppermute | solution.py:42
  33.0 18.2 %collective-permute-start.16 = (bf16[176,768]{1,0:T(8,128)(2,1)S(1)}, bf16[176,768]{1,0:T(8,128)(2,1)S(1)}, u32[]{:S(2)}, u32[]{:S(2)}) collective-permute-start(bf16[176,768]{1,0:T(8,128)(2,1)S(1)} %pad_maximum_fusion.4), channel_id=1, source_target_pairs={{0,4},{4,0},{8,12},{12,8},{1,5},{5,1},{9,13},{13,9},{2,6},{6,2},{1... | collective-permute-start | bytes 811016 | tf_op jit(solution)/shard_map/ppermute | solution.py:37
  42.6 13.2 %collective-permute-start.11 = (bf16[176,768]{1,0:T(8,128)(2,1)S(1)}, bf16[176,768]{1,0:T(8,128)(2,1)S(1)}, u32[]{:S(2)}, u32[]{:S(2)}) collective-permute-start(bf16[176,768]{1,0:T(8,128)(2,1)S(1)} %pad_maximum_fusion.4), channel_id=1, source_target_pairs={{0,12},{4,8},{8,4},{12,0},{1,13},{5,9},{9,5},{13,1},{2,14},{6,10},... | collective-permute-start | bytes 811016 | tf_op jit(solution)/shard_map/ppermute | solution.py:37
  49.6 7.8 %collective-permute-start.1 = (bf16[192,768]{1,0:T(8,128)(2,1)S(1)}, bf16[192,768]{1,0:T(8,128)(2,1)S(1)}, u32[]{:S(2)}, u32[]{:S(2)}) collective-permute-start(bf16[192,768]{1,0:T(8,128)(2,1)S(1)} %collective-permute-done), channel_id=1, source_target_pairs={{0,2},{1,3},{2,0},{3,1},{4,6},{5,7},{6,4},{7,5},{8,10},{9,11},{10,... | collective-permute-start | bytes 884744 | tf_op jit(solution)/shard_map/ppermute | solution.py:42
  50.9 12.2 %collective-permute-start.10 = (bf16[176,768]{1,0:T(8,128)(2,1)S(1)}, bf16[176,768]{1,0:T(8,128)(2,1)S(1)}, u32[]{:S(2)}, u32[]{:S(2)}) collective-permute-start(bf16[176,768]{1,0:T(8,128)(2,1)S(1)} %collective-permute-done.9), channel_id=1, source_target_pairs={{0,2},{1,3},{2,0},{3,1},{4,6},{5,7},{6,4},{7,5},{8,10},{9,11},{10,... | collective-permute-start | bytes 811016 | tf_op jit(solution)/shard_map/ppermute | solution.py:42
  51.2 14.8 %collective-permute-start.8 = (bf16[512,768]{1,0:T(8,128)(2,1)S(1)}, bf16[512,768]{1,0:T(8,128)(2,1)S(1)}, u32[]{:S(2)}, u32[]{:S(2)}) collective-permute-start(bf16[512,768]{1,0:T(8,128)(2,1)S(1)} %pad_maximum_fusion.refs_0_), channel_id=1, source_target_pairs={{0,1},{1,0},{2,3},{3,2},{4,5},{5,4},{6,7},{7,6},{8,9},{9,8},{10,11... | collective-permute-start | bytes 2359304 | tf_op jit(solution)/shard_map/ppermute | solution.py:42
  52.8 13.9 %collective-permute-start.17 = (bf16[512,768]{1,0:T(8,128)(2,1)S(1)}, bf16[512,768]{1,0:T(8,128)(2,1)S(1)}, u32[]{:S(2)}, u32[]{:S(2)}) collective-permute-start(bf16[512,768]{1,0:T(8,128)(2,1)S(1)} %pad_maximum_fusion.3.refs_0_), channel_id=1, source_target_pairs={{0,1},{1,0},{2,3},{3,2},{4,5},{5,4},{6,7},{7,6},{8,9},{9,8},{10,11... | collective-permute-start | bytes 2359304 | tf_op jit(solution)/shard_map/ppermute | solution.py:42
  57.4 3.9 %collective-permute-start.2 = (bf16[2,16,128]{2,1,0:T(8,128)(2,1)S(1)}, bf16[2,16,128]{2,1,0:T(8,128)(2,1)S(1)}, u32[]{:S(2)}, u32[]{:S(2)}) collective-permute-start(bf16[2,16,128]{2,1,0:T(8,128)(2,1)S(1)} %pad_maximum_fusion.6), channel_id=1, source_target_pairs={{0,1},{1,0},{2,3},{3,2},{4,5},{5,4},{6,7},{7,6},{8,9},{9,8},{10,11... | collective-permute-start | bytes 24584 | tf_op jit(solution)/shard_map/ppermute | solution.py:42
  60.6 6.9 %collective-permute-start.13 = (bf16[512,768]{1,0:T(8,128)(2,1)S(1)}, bf16[512,768]{1,0:T(8,128)(2,1)S(1)}, u32[]{:S(2)}, u32[]{:S(2)}) collective-permute-start(bf16[512,768]{1,0:T(8,128)(2,1)S(1)} %pad_maximum_fusion.2.refs_0_), channel_id=1, source_target_pairs={{0,1},{1,0},{2,3},{3,2},{4,5},{5,4},{6,7},{7,6},{8,9},{9,8},{10,11... | collective-permute-start | bytes 2359304 | tf_op jit(solution)/shard_map/ppermute | solution.py:42
  63.2 15.2 %collective-permute-start.12 = (bf16[512,768]{1,0:T(8,128)(2,1)S(1)}, bf16[512,768]{1,0:T(8,128)(2,1)S(1)}, u32[]{:S(2)}, u32[]{:S(2)}) collective-permute-start(bf16[512,768]{1,0:T(8,128)(2,1)S(1)} %pad_maximum_fusion.1.refs_0_), channel_id=1, source_target_pairs={{0,1},{1,0},{2,3},{3,2},{4,5},{5,4},{6,7},{7,6},{8,9},{9,8},{10,11... | collective-permute-start | bytes 2359304 | tf_op jit(solution)/shard_map/ppermute | solution.py:42

commit v3 on v2

v3 whole, which is shorter than its diff:
```python
import functools

import jax
import jax.numpy as jnp
from jax import lax
from jax.experimental import pallas as pl
from jax.experimental.pallas import tpu as pltpu
from jax.sharding import PartitionSpec as P

MEBI = 1024 * 1024
NT = (((1,), (1,)), ((), ()))
EXTRA = 16


def from_next(x, dp_xor=0):
    sections, shares = lax.axis_size("pipe"), lax.axis_size("dp")
    pairs = [
        (s * shares + z, (s - 1) * shares + (z ^ dp_xor))
        if s
        else (z, (sections - 1) * shares + z)
        for s in range(sections)
        for z in range(shares)
    ]
    return lax.ppermute(x, ("pipe", "dp"), pairs)


def from_share(x, dp_xor, idle):
    sections, shares = lax.axis_size("pipe"), lax.axis_size("dp")
    experts = lax.axis_size("expert")
    pairs = []
    for s in range(sections):
        for z in range(shares):
            for e in range(experts):
                to = (s, z, e ^ 1) if s == idle else (s, z ^ dp_xor, e)
                pairs.append(
                    ((s * shares + z) * experts + e, (to[0] * shares + to[1]) * experts + to[2])
                )
    return lax.ppermute(x, ("pipe", "dp", "expert"), pairs)


def swap(x, bit):
    experts = lax.axis_size("expert")
    return lax.ppermute(x, "expert", [(e, e ^ bit) for e in range(experts)])


def join_kernel(count, *refs):
    out_ref, at = refs[-1], 0
    for ref in refs[:count]:
        out_ref[at : at + ref.shape[0], :] = ref[...]
        at += ref.shape[0]


def join(blocks, gates=()):
    blocks, gates = list(blocks), [gate for gate in gates if gate is not None]
    rows, share = sum(block.shape[0] for block in blocks), blocks[0].shape[1]
    return pl.pallas_call(
        functools.partial(join_kernel, len(blocks)),
        in_specs=[pl.BlockSpec(memory_space=pltpu.VMEM)] * len(blocks)
        + [pl.BlockSpec(memory_space=pl.ANY)] * len(gates),
        out_specs=pl.BlockSpec(memory_space=pltpu.VMEM),
        out_shape=jax.ShapeDtypeStruct((rows, share), blocks[0].dtype),
        compiler_params=pltpu.CompilerParams(vmem_limit_bytes=4 * MEBI),
    )(*blocks, *gates)


def thirds(x):
    high = x.astype(jnp.bfloat16).astype(jnp.float32)
    middle = (x - high).astype(jnp.bfloat16).astype(jnp.float32)
    return [high, middle, x - high - middle]


def meta_kernel(logits_ref, routes_ref, meta_ref):
    micros, _, tokens = logits_ref.shape
    share = meta_ref.shape[1]
    lines = []
    for micro in range(micros):
        routes = routes_ref[micro].astype(jnp.float32)
        gap = logits_ref[micro, 0:1] - logits_ref[micro, 1:2]
        lines += [routes[0:1], routes[1:2], *thirds(gap), *[jnp.zeros_like(gap)] * 3]
    lines = jnp.concatenate(lines, 0)
    if share > tokens:
        lines = jnp.concatenate([lines, jnp.zeros((EXTRA, share - tokens), jnp.float32)], 1)
    meta_ref[...] = lines.astype(jnp.bfloat16)


def score_kernel(scores_ref, rows_ref):
    micros, tokens = scores_ref.shape
    share = rows_ref.shape[1]
    lines = jnp.concatenate(thirds(scores_ref[...]), 0)
    lines = jnp.concatenate([lines, jnp.zeros((EXTRA - 3 * micros, tokens), jnp.float32)], 0)
    if share > tokens:
        lines = jnp.concatenate([lines, jnp.zeros((EXTRA, share - tokens), jnp.float32)], 1)
    rows_ref[...] = lines.astype(jnp.bfloat16)


def extra_rows(kernel, share, *args):
    in_vmem = pl.BlockSpec(memory_space=pltpu.VMEM)
    return pl.pallas_call(
        kernel,
        in_specs=[in_vmem] * len(args),
        out_specs=in_vmem,
        out_shape=jax.ShapeDtypeStruct((EXTRA, share), jnp.bfloat16),
        compiler_params=pltpu.CompilerParams(vmem_limit_bytes=4 * MEBI),
    )(*args)


def place_kernel(expert_ref, meta_ref, places_ref, weights_ref):
    expert = expert_ref[0]
    groups, _, tokens = meta_ref.shape
    micros = meta_ref.shape[1] // 4
    rows = places_ref.shape[1]
    earlier = lax.broadcasted_iota(jnp.int32, (tokens, tokens), 0) < lax.broadcasted_iota(
        jnp.int32, (tokens, tokens), 1
    )
    earlier = earlier.astype(jnp.bfloat16)
    row = lax.broadcasted_iota(jnp.int32, (rows, tokens), 0)
    weights = []
    for micro in range(micros):
        for j in range(groups):
            meta = meta_ref[j]
            first = meta[4 * micro : 4 * micro + 1] == expert.astype(jnp.float32)
            second = meta[4 * micro + 1 : 4 * micro + 2] == expert.astype(jnp.float32)
            here = jnp.logical_or(first, second)
            weights.append(
                jnp.where(
                    first, meta[4 * micro + 2 : 4 * micro + 3], meta[4 * micro + 3 : 4 * micro + 4]
                )
            )
            named = jnp.broadcast_to(here.astype(jnp.float32), (16, tokens)).astype(jnp.bfloat16)
            slot = jnp.dot(named, earlier, preferred_element_type=jnp.float32)[0:1]
            target = slot.astype(jnp.int32) * groups + (expert ^ j)
            picked = row == jnp.where(here, target, -1)
            places_ref[micro, :, j * tokens : (j + 1) * tokens] = picked.astype(
                jnp.float32
            ).astype(jnp.bfloat16)
    weights = jnp.concatenate(weights, 0)
    padding = jnp.zeros((tokens - weights.shape[0], tokens), jnp.float32)
    weights_ref[...] = jnp.transpose(jnp.concatenate([weights, padding], 0))


def find_places(expert, meta, cap):
    groups, quads, tokens = meta.shape
    micros = quads // 4
    in_vmem = pl.BlockSpec(memory_space=pltpu.VMEM)
    return pl.pallas_call(
        place_kernel,
        in_specs=[pl.BlockSpec(memory_space=pltpu.SMEM), in_vmem],
        out_specs=[in_vmem, in_vmem],
        out_shape=[
            jax.ShapeDtypeStruct((micros, cap * groups, groups * tokens), jnp.bfloat16),
            jax.ShapeDtypeStruct((tokens, tokens), jnp.float32),
        ],
        compiler_params=pltpu.CompilerParams(vmem_limit_bytes=16 * MEBI),
    )(expert, meta)


def fill_kernel(cut, count, places_ref, weights_ref, *refs):
    token_refs, rows_ref = refs[:count], refs[-1]
    micros, rows, _ = places_ref.shape
    tokens = weights_ref.shape[0]
    late = micros * tokens - cut
    for micro in range(micros):
        blocks = []
        for j in range(2 * count):
            source, top = token_refs[j % count], j // count
            low, high = micro * tokens, (micro + 1) * tokens
            pieces = []
            if low < cut:
                pieces.append(source[top * cut + low : top * cut + min(high, cut), :])
            if high > cut:
                at = 2 * cut + top * late - cut
                pieces.append(source[at + max(low, cut) : at + high, :])
            held = pieces[0] if len(pieces) == 1 else jnp.concatenate(pieces, 0)
            weight = weights_ref[:, micro * 2 * count + j : micro * 2 * count + j + 1]
            blocks.append((held.astype(jnp.float32) * weight).astype(jnp.bfloat16))
        rows_ref[micro * rows : (micro + 1) * rows, :] = jnp.dot(
            places_ref[micro], jnp.concatenate(blocks, 0), preferred_element_type=jnp.float32
        ).astype(jnp.bfloat16)


def fill_rows(places, weights, tokens, cut, gates):
    micros, rows, _ = places.shape
    depth = tokens[0].shape[1]
    in_vmem = pl.BlockSpec(memory_space=pltpu.VMEM)
    return pl.pallas_call(
        functools.partial(fill_kernel, cut, len(tokens)),
        in_specs=[in_vmem] * (2 + len(tokens))
        + [pl.BlockSpec(memory_space=pl.ANY)] * len(gates),
        out_specs=in_vmem,
        out_shape=jax.ShapeDtypeStruct((micros * rows, depth), jnp.bfloat16),
        compiler_params=pltpu.CompilerParams(vmem_limit_bytes=12 * MEBI),
    )(places, weights, *tokens, *gates)


def part_kernel(parts, groups, first, last, *refs):
    row_refs = refs[1 : 1 + parts]
    weight_refs = refs[1 + parts : 1 + 2 * parts]
    rest = refs[1 + 2 * parts :]
    product = None
    for row_ref, weight_ref in zip(row_refs, weight_refs):
        term = lax.dot_general(
            row_ref[...], weight_ref[0], NT, preferred_element_type=jnp.float32
        )
        product = term if product is None else product + term
    block = product.shape[1]
    here = pl.ds(pl.multiple_of(pl.program_id(0) * block, block), block)
    if not first:
        product = product + rest[0][:, here]
    if not last:
        rest[-2][:, here] = product
        rest[-1][...] = product[:8, :128]
    else:
        out_ref = rest[-1]
        micros, cap = out_ref.shape[1], out_ref.shape[3]
        rows = cap * groups
        for micro in range(micros):
            out_ref[0, micro, 0] = (
                product[micro * rows : (micro + 1) * rows]
                .astype(out_ref.dtype)
                .reshape(cap, groups, block)
            )


def add_parts(place, begin, rows, weights, total, micros, groups, last):
    count, depth = rows[0].shape
    hidden = weights.shape[1]
    block = min(1024, hidden)
    in_vmem = pl.BlockSpec(memory_space=pltpu.VMEM)
    in_specs = [in_vmem] * len(rows)
    for i in range(begin, begin + len(rows)):
        in_specs.append(pl.BlockSpec((1, block, depth), lambda f, p, i=i: (0, f, p[i])))
    weights = pltpu.with_memory_space_constraint(weights, pltpu.HBM)
    args = [place, *rows, *[weights] * len(rows)]
    if total is not None:
        in_specs.append(in_vmem)
        args.append(total)
    if last:
        cap = count // (micros * groups)
        out_shape = jax.ShapeDtypeStruct((1, micros, 1, cap, groups, hidden), jnp.bfloat16)
        out_spec = pl.BlockSpec(
            (1, micros, 1, cap, groups, block), lambda f, p: (0, 0, 0, 0, 0, f)
        )
    else:
        out_shape = [
            jax.ShapeDtypeStruct((count, hidden), jnp.float32),
            jax.ShapeDtypeStruct((8, 128), jnp.float32),
        ]
        out_spec = [in_vmem, in_vmem]
    return pl.pallas_call(
        functools.partial(part_kernel, len(rows), groups, total is None, last),
        grid_spec=pltpu.PrefetchScalarGridSpec(
            num_scalar_prefetch=1,
            grid=(hidden // block,),
            in_specs=in_specs,
            out_specs=out_spec,
        ),
        out_shape=out_shape,
        compiler_params=pltpu.CompilerParams(vmem_limit_bytes=24 * MEBI),
        cost_estimate=pl.CostEstimate(
            flops=2 * count * depth * len(rows) * hidden,
            bytes_accessed=2 * hidden * depth * len(rows),
            transcendentals=0,
        ),
    )(*args)


def per_device(out_grad, expert_outputs, logits, routes, down_weights):
    micros, token_count, share = out_grad.shape[1:]
    experts, shares = lax.axis_size("expert"), lax.axis_size("dp")
    cap = min(token_count, 2 * token_count // experts + token_count // 32)
    expert, mine = lax.axis_index("expert"), lax.axis_index("dp")
    sections = lax.axis_size("pipe")
    received = lax.axis_index("pipe") < sections - 1
    top = experts // 2
    cut = micros * token_count * 11 // 16
    own = out_grad.reshape(micros * token_count, share)
    early, late = own[:cut], own[cut:]
    meta = extra_rows(
        meta_kernel, share, logits[0].transpose(0, 2, 1), routes[0].transpose(0, 2, 1)
    )

    late = from_next(late)
    direct = {2: from_next(early, 2)}
    late_top = swap(late, top)
    zero = from_next(join([early, meta], [late]))
    zero_top = swap(zero, top)
    direct[0], direct_top = zero[:cut], {0: zero_top[:cut]}
    direct[1] = from_next(join([early], [zero]), 1)

    grads, outputs = out_grad[0].astype(jnp.float32), expert_outputs[0].astype(jnp.float32)
    scores = jnp.sum(grads * (outputs[:, :, 0] - outputs[:, :, 1]), -1)
    step = 1
    while step < shares:
        scores += from_share(scores, step, 0)
        step *= 2
    scores = extra_rows(score_kernel, share, scores)

    pair = join([late, late_top])
    pairs = {0: pair, 2: from_share(pair, 2, sections - 1), 1: from_share(pair, 1, sections - 1)}
    for k in range(3, shares):
        sent = [early] if k < shares - 1 else [early, scores]
        direct[k] = from_next(join(sent, [direct[k - 1]]), k)
    scores, direct[shares - 1] = direct[shares - 1][cut:], direct[shares - 1][:cut]
    for k in range(1, shares):
        direct_top[k] = swap(direct[k], top)
    for k in range(3, shares):
        pairs[k] = from_share(join([pair], [pairs[k - 2]]), k, sections - 1)

    def spread(x):
        held, bit = {0: x}, top // 2
        while bit:
            for j in sorted(held):
                held[j ^ bit] = swap(held[j], bit)
            bit //= 2
        return [held[j] for j in sorted(held)]

    extras = spread(jnp.stack([x[-EXTRA:, :token_count] for x in (zero, zero_top)]))
    extras = jnp.concatenate([jnp.stack([e[b] for e in extras]) for b in range(2)], 0)
    extras = extras.astype(jnp.float32).reshape(experts, micros, 8, token_count)
    extras = extras.transpose(0, 2, 1, 3)
    gap = extras[:, 2] + extras[:, 3] + extras[:, 4]
    weight_first, weight_second = jax.nn.sigmoid(gap), jax.nn.sigmoid(-gap)
    meta = jnp.stack(
        [
            extras[:, 0],
            extras[:, 1],
            jnp.where(received, weight_first, 0.0),
            jnp.where(received, weight_second, 0.0),
        ],
        2,
    ).reshape(experts, 4 * micros, token_count)

    scores = scores[: 3 * micros, :token_count].astype(jnp.float32)
    scores = scores.reshape(3, micros, token_count)
    scores = scores[0] + scores[1] + scores[2]
    slope = jnp.where(received, weight_first[0] * weight_second[0] * scores, 0.0)
    moved_logits = jnp.stack([slope, -slope], -1).astype(jnp.bfloat16)[None]

    places, weights = find_places(expert.astype(jnp.int32)[None], meta, cap)

    together = 1
    while (share * together) % 128:
        together *= 2
    rows = []
    for which in range(shares // together):
        pieces = []
        for k in range(which * together, (which + 1) * together):
            pieces.append(spread(join([direct[k], direct_top[k], pairs[k]])))
        tokens = pieces[0]
        if together > 1:
            order = jnp.arange(together) ^ (mine % together)
            tokens = []
            for j in range(top):
                stacked = jnp.take(jnp.stack([piece[j] for piece in pieces]), order, axis=0)
                tokens.append(stacked.transpose(1, 0, 2).reshape(-1, together * share))
        rows.append(fill_rows(places, weights, tokens, cut, []))
    place = jnp.stack([(mine // together) ^ i for i in range(len(rows))]).astype(jnp.int32)
    hidden = add_parts(place, 0, rows, down_weights, None, micros, experts, True)
    return hidden.transpose(0, 1, 2, 4, 3, 5), moved_logits


def solution(mesh):
    in_specs = (
        P("pipe", None, "expert", "dp"),
        P("pipe", None, "expert", None, "dp"),
        P("pipe", None, "expert", None),
        P("pipe", None, "expert", None),
        P("expert", "dp", None),
    )
    out_specs = (P("pipe", None, "expert", None, None, "dp"), P("pipe", None, "expert", None))
    return jax.shard_map(
        per_device, mesh=mesh, in_specs=in_specs, out_specs=out_specs, check_vma=False
    )
```

time: 91.6 us -> 76.6 us (0.84)
  the two profiles are of different devices: /device:TPU:1 before, /device:TPU:9 now
where the time goes in v3:
time: 76.6 us; the launch traced here: 76.4 us
  starting transfers between devices  31.6 us (41%)
  Pallas kernels  22.8 us (30%)
  waiting for transfers between devices  15.6 us (20%)
  other arithmetic  2.82 us (4%)
  local copies, waits for them, and re-layouts  2.57 us (3%)
  between operations  0.96 us (1%)
    pallas_call x1, Pallas kernels, add_parts(): pl.pallas_call(functools.partial(part_kernel, len(rows), groups, total is...  19.2 us
    ppermute x10, starting transfers between devices, swap(): return lax.ppermute(x, 'expert', [(e, e ^ bit) for e in range(experts)])  18.1 us
    ppermute x5, starting transfers between devices, from_next(): return lax.ppermute(x, ('pipe', 'dp'), pairs)  8.97 us
    ppermute x5, waiting for transfers between devices, from_next(): return lax.ppermute(x, ('pipe', 'dp'), pairs)  6.7 us
    ppermute x5, waiting for transfers between devices, from_share(): return lax.ppermute(x, ('pipe', 'dp', 'expert'), pairs)  6.55 us
    ppermute x5, starting transfers between devices, from_share(): return lax.ppermute(x, ('pipe', 'dp', 'expert'), pairs)  4.52 us
    pallas_call x4, Pallas kernels, fill_rows(): pl.pallas_call(functools.partial(fill_kernel, cut, len(tokens)), in_specs...  2.89 us
    ppermute x10, waiting for transfers between devices, swap(): return lax.ppermute(x, 'expert', [(e, e ^ bit) for e in range(experts)])  2.36 us
  transfers between devices with their start and end apart: 20, of which 8 were waited for; matrix products, arithmetic and copies ran while one was open for 6% of the time, Pallas kernels for 4%

profile of v3, /device:TPU:9, one launch (start us, length us, event | category | flops | bytes accessed | tf_op | source)
XLA Modules:
  0.0 76.4 jit_solution(218057544203706120)
XLA Ops:
  0.6 0.9 %slice.96 = bf16[80,768]{1,0:T(8,128)(2,1)S(1)} slice(bf16[256,768]{1,0:T(8,128)(2,1)} %bitcast.78), slice={[176:256], [0:768]} | slice | bytes 245760 | tf_op jit(solution)/shard_map/slice | solution.py:277
  1.6 1.3 %collective-permute-start = (bf16[80,768]{1,0:T(8,128)(2,1)S(1)}, bf16[80,768]{1,0:T(8,128)(2,1)S(1)}, u32[]{:S(2)}, u32[]{:S(2)}) collective-permute-start(bf16[80,768]{1,0:T(8,128)(2,1)S(1)} %slice.96), channel_id=1, source_target_pairs={{0,16},{4,20},{8,24},{12,28},{16,0},{20,4},{24,8},{28,12},{1,17},{... | collective-permute-start | bytes 368648 | tf_op jit(solution)/shard_map/ppermute | solution.py:24
  2.8 1.0 %slice.95.refs_0_ = bf16[176,768]{1,0:T(8,128)(2,1)S(1)} slice(bf16[256,768]{1,0:T(8,128)(2,1)} %bitcast.79), slice={[0:176], [0:768]} | slice | bytes 540672 | tf_op jit(solution)/shard_map/slice | solution.py:277
  4.1 1.7 %bitcast_convert_fusion = f32[2,128,2,768]{3,2,1,0:T(2,128)S(1)} fusion(bf16[1,2,128,2,768]{4,3,2,1,0:T(2,128)(2,1)} %param.6), kind=kLoop, calls=%fused_computation.3 | loop fusion | flops 393216 | bytes 2359296 | tf_op jit(solution)/shard_map/convert_element_type | solution.py:290
  5.9 3.3 %collective-permute-start.1 = (bf16[192,768]{1,0:T(8,128)(2,1)S(1)}, bf16[192,768]{1,0:T(8,128)(2,1)S(1)}, u32[]{:S(2)}, u32[]{:S(2)}) collective-permute-start(bf16[192,768]{1,0:T(8,128)(2,1)S(1)} %shard_map.69), channel_id=1, source_target_pairs={{0,16},{4,20},{8,24},{12,28},{16,0},{20,4},{24,8},{28,12},{1,17},{... | collective-permute-start | bytes 884744 | tf_op jit(solution)/shard_map/ppermute | solution.py:24
  9.2 0.8 %slice_subtract_fusion = f32[2,128,1,768]{3,2,1,0:T(1,128)S(1)} fusion(f32[2,128,2,768]{3,2,1,0:T(2,128)S(1)} %bitcast_convert_fusion), kind=kLoop, calls=%fused_computation | loop fusion | flops 196608 | bytes 2359296 | tf_op jit(solution)/shard_map/sub | solution.py:291
  10.0 1.3 %collective-permute-start.4 = (bf16[80,768]{1,0:T(8,128)(2,1)S(1)}, bf16[80,768]{1,0:T(8,128)(2,1)S(1)}, u32[]{:S(2)}, u32[]{:S(2)}) collective-permute-start(bf16[80,768]{1,0:T(8,128)(2,1)S(1)} %collective-permute-done.refs_2_.refs_0_), channel_id=1, source_target_pairs={{0,2},{1,3},{2,0},{3,1},{4,6},{5,7},{6,4},{7,5},{8,10},{9,11},{10,... | collective-permute-start | bytes 368648 | tf_op jit(solution)/shard_map/ppermute | solution.py:43
  11.5 1.9 %collective-permute-start.14 = (f32[2,128]{1,0:T(2,128)S(1)}, f32[2,128]{1,0:T(2,128)S(1)}, u32[]{:S(2)}, u32[]{:S(2)}) collective-permute-start(f32[2,128]{1,0:T(2,128)S(1)} %fusion), channel_id=1, source_target_pairs={{0,1},{1,0},{2,3},{3,2},{4,5},{5,4},{6,7},{7,6},{8,9},{9,8},{10,11... | collective-permute-start | bytes 3080 | tf_op jit(solution)/shard_map/ppermute | solution.py:38
  13.3 0.8 %collective-permute-done.14 = f32[2,128]{1,0:T(2,128)S(1)} collective-permute-done((f32[2,128]{1,0:T(2,128)S(1)}, f32[2,128]{1,0:T(2,128)S(1)}, u32[]{:S(2)}, u32[]{:S(2)}) %collective-permute-start.14) | collective-permute-done | bytes 1056 | tf_op jit(solution)/shard_map/ppermute | solution.py:38
  14.5 0.8 %collective-permute-done.15 = f32[2,128]{1,0:T(2,128)S(1)} collective-permute-done((f32[2,128]{1,0:T(2,128)S(1)}, f32[2,128]{1,0:T(2,128)S(1)}, u32[]{:S(2)}, u32[]{:S(2)}) %collective-permute-start.15) | collective-permute-done | bytes 1056 | tf_op jit(solution)/shard_map/ppermute | solution.py:38
  15.3 1.8 %collective-permute-start.12 = (bf16[160,768]{1,0:T(8,128)(2,1)S(1)}, bf16[160,768]{1,0:T(8,128)(2,1)S(1)}, u32[]{:S(2)}, u32[]{:S(2)}) collective-permute-start(bf16[160,768]{1,0:T(8,128)(2,1)S(1)} %shard_map.71.refs_2_.refs_0_), channel_id=1, source_target_pairs={{0,8},{1,9},{2,10},{3,11},{4,12},{5,13},{6,14},{7,15},{8,0},{9,1},... | collective-permute-start | bytes 737288 | tf_op jit(solution)/shard_map/ppermute | solution.py:38
  17.3 4.1 %collective-permute-start.16 = (bf16[192,768]{1,0:T(8,128)(2,1)S(1)}, bf16[192,768]{1,0:T(8,128)(2,1)S(1)}, u32[]{:S(2)}, u32[]{:S(2)}) collective-permute-start(bf16[192,768]{1,0:T(8,128)(2,1)S(1)} %shard_map.80), channel_id=1, source_target_pairs={{0,16},{4,20},{8,24},{12,28},{16,12},{20,8},{24,4},{28,0},{1,17},{... | collective-permute-start | bytes 884744 | tf_op jit(solution)/shard_map/ppermute | solution.py:24
  21.6 1.2 %collective-permute-start.2 = (bf16[192,768]{1,0:T(8,128)(2,1)S(1)}, bf16[192,768]{1,0:T(8,128)(2,1)S(1)}, u32[]{:S(2)}, u32[]{:S(2)}) collective-permute-start(bf16[192,768]{1,0:T(8,128)(2,1)S(1)} %collective-permute-done.1.refs_1_), channel_id=1, source_target_pairs={{0,2},{1,3},{2,0},{3,1},{4,6},{5,7},{6,4},{7,5},{8,10},{9,11},{10,... | collective-permute-start | bytes 884744 | tf_op jit(solution)/shard_map/ppermute | solution.py:43
  23.0 4.4 %collective-permute-done.8.refs_2_.refs_1_ = bf16[160,768]{1,0:T(8,128)(2,1)S(1)} collective-permute-done((bf16[160,768]{1,0:T(8,128)(2,1)S(1)}, bf16[160,768]{1,0:T(8,128)(2,1)S(1)}, u32[]{:S(2)}, u32[]{:S(2)}) %collective-permute-start.8) | collective-permute-done | bytes 245792 | tf_op jit(solution)/shard_map/ppermute | solution.py:38
  27.4 0.5 collective-permute-done.12.refs_2_
  27.9 0.4 collective-permute-start.18
  28.8 2.8 %collective-permute-start.13 = (bf16[512,768]{1,0:T(8,128)(2,1)S(1)}, bf16[512,768]{1,0:T(8,128)(2,1)S(1)}, u32[]{:S(2)}, u32[]{:S(2)}) collective-permute-start(bf16[512,768]{1,0:T(8,128)(2,1)S(1)} %shard_map.77.refs_0_), channel_id=1, source_target_pairs={{0,1},{1,0},{2,3},{3,2},{4,5},{5,4},{6,7},{7,6},{8,9},{9,8},{10,11... | collective-permute-start | bytes 2359304 | tf_op jit(solution)/shard_map/ppermute | solution.py:43
  31.6 6.7 %collective-permute-done.16 = bf16[192,768]{1,0:T(8,128)(2,1)S(1)} collective-permute-done((bf16[192,768]{1,0:T(8,128)(2,1)S(1)}, bf16[192,768]{1,0:T(8,128)(2,1)S(1)}, u32[]{:S(2)}, u32[]{:S(2)}) %collective-permute-start.16) | collective-permute-done | bytes 294944 | tf_op jit(solution)/shard_map/ppermute | solution.py:24
  38.4 2.0 %collective-permute-start.3 = (bf16[2,16,128]{2,1,0:T(8,128)(2,1)S(1)}, bf16[2,16,128]{2,1,0:T(8,128)(2,1)S(1)}, u32[]{:S(2)}, u32[]{:S(2)}) collective-permute-start(bf16[2,16,128]{2,1,0:T(8,128)(2,1)S(1)} %pad_maximum_fusion.1), channel_id=1, source_target_pairs={{0,1},{1,0},{2,3},{3,2},{4,5},{5,4},{6,7},{7,6},{8,9},{9,8},{10,11... | collective-permute-start | bytes 24584 | tf_op jit(solution)/shard_map/ppermute | solution.py:43
  40.4 1.7 %collective-permute-start.7 = (bf16[176,768]{1,0:T(8,128)(2,1)S(1)}, bf16[176,768]{1,0:T(8,128)(2,1)S(1)}, u32[]{:S(2)}, u32[]{:S(2)}) collective-permute-start(bf16[176,768]{1,0:T(8,128)(2,1)S(1)} %collective-permute-done.6.refs_0_), channel_id=1, source_target_pairs={{0,2},{1,3},{2,0},{3,1},{4,6},{5,7},{6,4},{7,5},{8,10},{9,11},{10,... | collective-permute-start | bytes 811016 | tf_op jit(solution)/shard_map/ppermute | solution.py:43
  42.3 0.4 collective-permute-start.5
  42.8 1.6 %collective-permute-done.17.refs_1_ = bf16[176,768]{1,0:T(8,128)(2,1)S(1)} collective-permute-done((bf16[176,768]{1,0:T(8,128)(2,1)S(1)}, bf16[176,768]{1,0:T(8,128)(2,1)S(1)}, u32[]{:S(2)}, u32[]{:S(2)}) %collective-permute-start.17) | collective-permute-done | bytes 270368 | tf_op jit(solution)/shard_map/ppermute | solution.py:43
  44.5 5.4 %collective-permute-start.19 = (bf16[512,768]{1,0:T(8,128)(2,1)S(1)}, bf16[512,768]{1,0:T(8,128)(2,1)S(1)}, u32[]{:S(2)}, u32[]{:S(2)}) collective-permute-start(bf16[512,768]{1,0:T(8,128)(2,1)S(1)} %shard_map.82.refs_0_), channel_id=1, source_target_pairs={{0,1},{1,0},{2,3},{3,2},{4,5},{5,4},{6,7},{7,6},{8,9},{9,8},{10,11... | collective-permute-start | bytes 2359304 | tf_op jit(solution)/shard_map/ppermute | solution.py:43
  49.9 0.4 collective-permute-done.7.refs_1_
  50.3 2.9 %collective-permute-start.9 = (bf16[512,768]{1,0:T(8,128)(2,1)S(1)}, bf16[512,768]{1,0:T(8,128)(2,1)S(1)}, u32[]{:S(2)}, u32[]{:S(2)}) collective-permute-start(bf16[512,768]{1,0:T(8,128)(2,1)S(1)} %shard_map.75.refs_0_), channel_id=1, source_target_pairs={{0,1},{1,0},{2,3},{3,2},{4,5},{5,4},{6,7},{7,6},{8,9},{9,8},{10,11... | collective-permute-start | bytes 2359304 | tf_op jit(solution)/shard_map/ppermute | solution.py:43
  53.3 0.6 copy.23
  53.8 0.3 shard_map.70
  54.2 0.7 shard_map.78.refs_3_
  54.9 0.7 shard_map.73.refs_1_
  55.7 0.7 shard_map.83.refs_4_
  56.4 0.7 shard_map.76.refs_2_
  57.2 19.2 %shard_map.84 = bf16[1,2,1,68,4,4096]{5,4,3,2,1,0:T(4,128)(2,1)} custom-call(s32[4]{0:T(128)S(1)} %pad_add_fusion.refs_0_, bf16[544,768]{1,0:T(8,128)(2,1)S(1)} %shard_map.73.refs_1_, bf16[544,768]{1,0:T(8,128)(2,1)S(1)} %shard_map.76.refs_2_, bf16[544,768]{1,0:T(8,128)(2,1)S(1)} %shard_map.78.refs_3_, bf16[544,768]{1,0:T(8,128)(2,1)S(1)} %shard_map.83.refs_4_, ...), custom_call_target="tpu_custom_call" | custom-call | flops 13690208256 | bytes 25165824 | tf_op jit(solution)/shard_map/pallas_call | solution.py:249
  (60 shorter events, 2.3 us)
Async XLA Ops:
  0.6 5.2 %copy-start = (f32[1,2,128,2]{2,3,1,0:T(2,128)S(1)}, f32[1,2,128,2]{2,3,1,0:T(2,128)}, u32[]{:S(2)}) copy-start(f32[1,2,128,2]{2,3,1,0:T(2,128)} %param.7) | copy-start | bytes 6148
  0.6 5.2 %copy-start.1 = (s32[1,2,128,2]{2,3,1,0:T(2,128)S(1)}, s32[1,2,128,2]{2,3,1,0:T(2,128)}, u32[]{:S(2)}) copy-start(s32[1,2,128,2]{2,3,1,0:T(2,128)} %param.8) | copy-start | bytes 6148
  1.6 4.3 %collective-permute-start = (bf16[80,768]{1,0:T(8,128)(2,1)S(1)}, bf16[80,768]{1,0:T(8,128)(2,1)S(1)}, u32[]{:S(2)}, u32[]{:S(2)}) collective-permute-start(bf16[80,768]{1,0:T(8,128)(2,1)S(1)} %slice.96), channel_id=1, source_target_pairs={{0,16},{4,20},{8,24},{12,28},{16,0},{20,4},{24,8},{28,12},{1,17},{... | collective-permute-start | bytes 368648 | tf_op jit(solution)/shard_map/ppermute | solution.py:24
  3.8 13.5 %collective-permute-start.10 = (bf16[176,768]{1,0:T(8,128)(2,1)S(1)}, bf16[176,768]{1,0:T(8,128)(2,1)S(1)}, u32[]{:S(2)}, u32[]{:S(2)}) collective-permute-start(bf16[176,768]{1,0:T(8,128)(2,1)S(1)} %slice.95.refs_0_), channel_id=1, source_target_pairs={{0,16},{4,20},{8,24},{12,28},{16,8},{20,12},{24,0},{28,4},{1,17},{... | collective-permute-start | bytes 811016 | tf_op jit(solution)/shard_map/ppermute | solution.py:24
  5.8 5.5 %copy-start.2 = (bf16[1,2,128,768]{3,2,1,0:T(8,128)(2,1)S(1)}, bf16[1,2,128,768]{3,2,1,0:T(8,128)(2,1)}, u32[]{:S(2)}) copy-start(bf16[1,2,128,768]{3,2,1,0:T(8,128)(2,1)} %param.5) | copy-start | bytes 1179652
  5.9 15.7 %collective-permute-start.1 = (bf16[192,768]{1,0:T(8,128)(2,1)S(1)}, bf16[192,768]{1,0:T(8,128)(2,1)S(1)}, u32[]{:S(2)}, u32[]{:S(2)}) collective-permute-start(bf16[192,768]{1,0:T(8,128)(2,1)S(1)} %shard_map.69), channel_id=1, source_target_pairs={{0,16},{4,20},{8,24},{12,28},{16,0},{20,4},{24,8},{28,12},{1,17},{... | collective-permute-start | bytes 884744 | tf_op jit(solution)/shard_map/ppermute | solution.py:24
  10.0 5.3 %collective-permute-start.4 = (bf16[80,768]{1,0:T(8,128)(2,1)S(1)}, bf16[80,768]{1,0:T(8,128)(2,1)S(1)}, u32[]{:S(2)}, u32[]{:S(2)}) collective-permute-start(bf16[80,768]{1,0:T(8,128)(2,1)S(1)} %collective-permute-done.refs_2_.refs_0_), channel_id=1, source_target_pairs={{0,2},{1,3},{2,0},{3,1},{4,6},{5,7},{6,4},{7,5},{8,10},{9,11},{10,... | collective-permute-start | bytes 368648 | tf_op jit(solution)/shard_map/ppermute | solution.py:43
  11.5 2.7 %collective-permute-start.14 = (f32[2,128]{1,0:T(2,128)S(1)}, f32[2,128]{1,0:T(2,128)S(1)}, u32[]{:S(2)}, u32[]{:S(2)}) collective-permute-start(f32[2,128]{1,0:T(2,128)S(1)} %fusion), channel_id=1, source_target_pairs={{0,1},{1,0},{2,3},{3,2},{4,5},{5,4},{6,7},{7,6},{8,9},{9,8},{10,11... | collective-permute-start | bytes 3080 | tf_op jit(solution)/shard_map/ppermute | solution.py:38
  14.2 1.1 %collective-permute-start.15 = (f32[2,128]{1,0:T(2,128)S(1)}, f32[2,128]{1,0:T(2,128)S(1)}, u32[]{:S(2)}, u32[]{:S(2)}) collective-permute-start(f32[2,128]{1,0:T(2,128)S(1)} %add.84), channel_id=1, source_target_pairs={{0,1},{1,0},{2,3},{3,2},{4,5},{5,4},{6,7},{7,6},{8,9},{9,8},{10,11... | collective-permute-start | bytes 3080 | tf_op jit(solution)/shard_map/ppermute | solution.py:38
  15.3 12.6 %collective-permute-start.12 = (bf16[160,768]{1,0:T(8,128)(2,1)S(1)}, bf16[160,768]{1,0:T(8,128)(2,1)S(1)}, u32[]{:S(2)}, u32[]{:S(2)}) collective-permute-start(bf16[160,768]{1,0:T(8,128)(2,1)S(1)} %shard_map.71.refs_2_.refs_0_), channel_id=1, source_target_pairs={{0,8},{1,9},{2,10},{3,11},{4,12},{5,13},{6,14},{7,15},{8,0},{9,1},... | collective-permute-start | bytes 737288 | tf_op jit(solution)/shard_map/ppermute | solution.py:38
  17.1 10.3 %collective-permute-start.8 = (bf16[160,768]{1,0:T(8,128)(2,1)S(1)}, bf16[160,768]{1,0:T(8,128)(2,1)S(1)}, u32[]{:S(2)}, u32[]{:S(2)}) collective-permute-start(bf16[160,768]{1,0:T(8,128)(2,1)S(1)} %shard_map.71.refs_2_.refs_0_), channel_id=1, source_target_pairs={{0,4},{1,5},{2,6},{3,7},{4,0},{5,1},{6,2},{7,3},{8,12},{9,13},{10,... | collective-permute-start | bytes 737288 | tf_op jit(solution)/shard_map/ppermute | solution.py:38
  17.3 21.0 %collective-permute-start.16 = (bf16[192,768]{1,0:T(8,128)(2,1)S(1)}, bf16[192,768]{1,0:T(8,128)(2,1)S(1)}, u32[]{:S(2)}, u32[]{:S(2)}) collective-permute-start(bf16[192,768]{1,0:T(8,128)(2,1)S(1)} %shard_map.80), channel_id=1, source_target_pairs={{0,16},{4,20},{8,24},{12,28},{16,12},{20,8},{24,4},{28,0},{1,17},{... | collective-permute-start | bytes 884744 | tf_op jit(solution)/shard_map/ppermute | solution.py:24
  21.4 7.3 %collective-permute-start.11 = (bf16[176,768]{1,0:T(8,128)(2,1)S(1)}, bf16[176,768]{1,0:T(8,128)(2,1)S(1)}, u32[]{:S(2)}, u32[]{:S(2)}) collective-permute-start(bf16[176,768]{1,0:T(8,128)(2,1)S(1)} %collective-permute-done.10.refs_0_.refs_2_), channel_id=1, source_target_pairs={{0,2},{1,3},{2,0},{3,1},{4,6},{5,7},{6,4},{7,5},{8,10},{9,11},{10,... | collective-permute-start | bytes 811016 | tf_op jit(solution)/shard_map/ppermute | solution.py:43
  21.6 16.8 %collective-permute-start.2 = (bf16[192,768]{1,0:T(8,128)(2,1)S(1)}, bf16[192,768]{1,0:T(8,128)(2,1)S(1)}, u32[]{:S(2)}, u32[]{:S(2)}) collective-permute-start(bf16[192,768]{1,0:T(8,128)(2,1)S(1)} %collective-permute-done.1.refs_1_), channel_id=1, source_target_pairs={{0,2},{1,3},{2,0},{3,1},{4,6},{5,7},{6,4},{7,5},{8,10},{9,11},{10,... | collective-permute-start | bytes 884744 | tf_op jit(solution)/shard_map/ppermute | solution.py:43
  27.4 13.0 %collective-permute-start.6 = (bf16[176,768]{1,0:T(8,128)(2,1)S(1)}, bf16[176,768]{1,0:T(8,128)(2,1)S(1)}, u32[]{:S(2)}, u32[]{:S(2)}) collective-permute-start(bf16[176,768]{1,0:T(8,128)(2,1)S(1)} %shard_map.74), channel_id=1, source_target_pairs={{0,16},{4,20},{8,24},{12,28},{16,4},{20,0},{24,12},{28,8},{1,17},{... | collective-permute-start | bytes 811016 | tf_op jit(solution)/shard_map/ppermute | solution.py:24
  27.9 14.8 %collective-permute-start.18 = (bf16[160,768]{1,0:T(8,128)(2,1)S(1)}, bf16[160,768]{1,0:T(8,128)(2,1)S(1)}, u32[]{:S(2)}, u32[]{:S(2)}) collective-permute-start(bf16[160,768]{1,0:T(8,128)(2,1)S(1)} %shard_map.81), channel_id=1, source_target_pairs={{0,12},{1,13},{2,14},{3,15},{4,8},{5,9},{6,10},{7,11},{8,4},{9,5},... | collective-permute-start | bytes 737288 | tf_op jit(solution)/shard_map/ppermute | solution.py:38
  28.8 25.5 %collective-permute-start.13 = (bf16[512,768]{1,0:T(8,128)(2,1)S(1)}, bf16[512,768]{1,0:T(8,128)(2,1)S(1)}, u32[]{:S(2)}, u32[]{:S(2)}) collective-permute-start(bf16[512,768]{1,0:T(8,128)(2,1)S(1)} %shard_map.77.refs_0_), channel_id=1, source_target_pairs={{0,1},{1,0},{2,3},{3,2},{4,5},{5,4},{6,7},{7,6},{8,9},{9,8},{10,11... | collective-permute-start | bytes 2359304 | tf_op jit(solution)/shard_map/ppermute | solution.py:43
  38.3 6.1 %collective-permute-start.17 = (bf16[176,768]{1,0:T(8,128)(2,1)S(1)}, bf16[176,768]{1,0:T(8,128)(2,1)S(1)}, u32[]{:S(2)}, u32[]{:S(2)}) collective-permute-start(bf16[176,768]{1,0:T(8,128)(2,1)S(1)} %slice.110.refs_0_), channel_id=1, source_target_pairs={{0,2},{1,3},{2,0},{3,1},{4,6},{5,7},{6,4},{7,5},{8,10},{9,11},{10,... | collective-permute-start | bytes 811016 | tf_op jit(solution)/shard_map/ppermute | solution.py:43
  38.4 3.8 %collective-permute-start.3 = (bf16[2,16,128]{2,1,0:T(8,128)(2,1)S(1)}, bf16[2,16,128]{2,1,0:T(8,128)(2,1)S(1)}, u32[]{:S(2)}, u32[]{:S(2)}) collective-permute-start(bf16[2,16,128]{2,1,0:T(8,128)(2,1)S(1)} %pad_maximum_fusion.1), channel_id=1, source_target_pairs={{0,1},{1,0},{2,3},{3,2},{4,5},{5,4},{6,7},{7,6},{8,9},{9,8},{10,11... | collective-permute-start | bytes 24584 | tf_op jit(solution)/shard_map/ppermute | solution.py:43
  40.4 9.8 %collective-permute-start.7 = (bf16[176,768]{1,0:T(8,128)(2,1)S(1)}, bf16[176,768]{1,0:T(8,128)(2,1)S(1)}, u32[]{:S(2)}, u32[]{:S(2)}) collective-permute-start(bf16[176,768]{1,0:T(8,128)(2,1)S(1)} %collective-permute-done.6.refs_0_), channel_id=1, source_target_pairs={{0,2},{1,3},{2,0},{3,1},{4,6},{5,7},{6,4},{7,5},{8,10},{9,11},{10,... | collective-permute-start | bytes 811016 | tf_op jit(solution)/shard_map/ppermute | solution.py:43
  42.3 12.7 %collective-permute-start.5 = (bf16[512,768]{1,0:T(8,128)(2,1)S(1)}, bf16[512,768]{1,0:T(8,128)(2,1)S(1)}, u32[]{:S(2)}, u32[]{:S(2)}) collective-permute-start(bf16[512,768]{1,0:T(8,128)(2,1)S(1)} %shard_map.72.refs_0_), channel_id=1, source_target_pairs={{0,1},{1,0},{2,3},{3,2},{4,5},{5,4},{6,7},{7,6},{8,9},{9,8},{10,11... | collective-permute-start | bytes 2359304 | tf_op jit(solution)/shard_map/ppermute | solution.py:43
  44.5 11.2 %collective-permute-start.19 = (bf16[512,768]{1,0:T(8,128)(2,1)S(1)}, bf16[512,768]{1,0:T(8,128)(2,1)S(1)}, u32[]{:S(2)}, u32[]{:S(2)}) collective-permute-start(bf16[512,768]{1,0:T(8,128)(2,1)S(1)} %shard_map.82.refs_0_), channel_id=1, source_target_pairs={{0,1},{1,0},{2,3},{3,2},{4,5},{5,4},{6,7},{7,6},{8,9},{9,8},{10,11... | collective-permute-start | bytes 2359304 | tf_op jit(solution)/shard_map/ppermute | solution.py:43
  50.3 6.2 %collective-permute-start.9 = (bf16[512,768]{1,0:T(8,128)(2,1)S(1)}, bf16[512,768]{1,0:T(8,128)(2,1)S(1)}, u32[]{:S(2)}, u32[]{:S(2)}) collective-permute-start(bf16[512,768]{1,0:T(8,128)(2,1)S(1)} %shard_map.75.refs_0_), channel_id=1, source_target_pairs={{0,1},{1,0},{2,3},{3,2},{4,5},{5,4},{6,7},{7,6},{8,9},{9,8},{10,11... | collective-permute-start | bytes 2359304 | tf_op jit(solution)/shard_map/ppermute | solution.py:43

commit v4 on v3

v4 whole, which is shorter than its diff:
```python
import functools

import jax
import jax.numpy as jnp
from jax import lax
from jax.experimental import pallas as pl
from jax.experimental.pallas import tpu as pltpu
from jax.sharding import PartitionSpec as P

MEBI = 1024 * 1024
NT = (((1,), (1,)), ((), ()))
EXTRA = 16
COPIES = 4


def from_next(x, dp_xor=0):
    sections, shares = lax.axis_size("pipe"), lax.axis_size("dp")
    pairs = [
        (s * shares + z, (s - 1) * shares + (z ^ dp_xor))
        if s
        else (z, (sections - 1) * shares + z)
        for s in range(sections)
        for z in range(shares)
    ]
    return lax.ppermute(x, ("pipe", "dp"), pairs)


def from_share(x, dp_xor, idle):
    sections, shares = lax.axis_size("pipe"), lax.axis_size("dp")
    experts = lax.axis_size("expert")
    pairs = []
    for s in range(sections):
        for z in range(shares):
            for e in range(experts):
                to = (s, z, e ^ 1) if s == idle else (s, z ^ dp_xor, e)
                pairs.append(
                    ((s * shares + z) * experts + e, (to[0] * shares + to[1]) * experts + to[2])
                )
    return lax.ppermute(x, ("pipe", "dp", "expert"), pairs)


def swap(x, bit):
    experts = lax.axis_size("expert")
    return lax.ppermute(x, "expert", [(e, e ^ bit) for e in range(experts)])


def join_kernel(count, *refs):
    out_ref, at = refs[-1], 0
    for ref in refs[:count]:
        out_ref[at : at + ref.shape[0], :] = ref[...]
        at += ref.shape[0]


def join(blocks, gates=()):
    blocks, gates = list(blocks), [gate for gate in gates if gate is not None]
    rows, share = sum(block.shape[0] for block in blocks), blocks[0].shape[1]
    return pl.pallas_call(
        functools.partial(join_kernel, len(blocks)),
        in_specs=[pl.BlockSpec(memory_space=pltpu.VMEM)] * len(blocks)
        + [pl.BlockSpec(memory_space=pl.ANY)] * len(gates),
        out_specs=pl.BlockSpec(memory_space=pltpu.VMEM),
        out_shape=jax.ShapeDtypeStruct((rows, share), blocks[0].dtype),
        compiler_params=pltpu.CompilerParams(vmem_limit_bytes=4 * MEBI),
    )(*blocks, *gates)


def thirds(x):
    high = x.astype(jnp.bfloat16).astype(jnp.float32)
    middle = (x - high).astype(jnp.bfloat16).astype(jnp.float32)
    return [high, middle, x - high - middle]


def extra_kernel(_, *refs):
    extra_ref, held, done = refs[4], refs[5:9], refs[9]
    copies = [pltpu.make_async_copy(refs[i], held[i], done.at[i]) for i in range(4)]
    for copy in copies:
        copy.start()
    for copy in copies:
        copy.wait()
    logits_ref, routes_ref, grads_ref, outputs_ref = held
    micros, _, tokens = logits_ref.shape
    share = extra_ref.shape[1]
    pair = lax.broadcasted_iota(jnp.int32, (2 * tokens, tokens), 0)
    token = lax.broadcasted_iota(jnp.int32, (2 * tokens, tokens), 1)
    lines = []
    for micro in range(micros):
        routes = routes_ref[micro].astype(jnp.float32)
        gap = logits_ref[micro, 0:1] - logits_ref[micro, 1:2]
        products = lax.dot_general(
            outputs_ref[micro].reshape(2 * tokens, share),
            grads_ref[micro],
            NT,
            preferred_element_type=jnp.float32,
        )
        first = jnp.sum(jnp.where(pair == 2 * token, products, 0.0), 0, keepdims=True)
        second = jnp.sum(jnp.where(pair == 2 * token + 1, products, 0.0), 0, keepdims=True)
        lines += [routes[0:1], routes[1:2], *thirds(gap), *thirds(first - second)]
    lines = jnp.concatenate(lines, 0)
    if share > tokens:
        lines = jnp.concatenate([lines, jnp.zeros((EXTRA, share - tokens), jnp.float32)], 1)
    extra_ref[...] = lines.astype(jnp.bfloat16)


def extra_rows(share, flags, *args):
    return pl.pallas_call(
        extra_kernel,
        in_specs=[pl.BlockSpec(memory_space=pltpu.SMEM)]
        + [pl.BlockSpec(memory_space=pltpu.HBM)] * len(args),
        out_specs=pl.BlockSpec(memory_space=pltpu.VMEM),
        out_shape=jax.ShapeDtypeStruct((EXTRA, share), jnp.bfloat16),
        scratch_shapes=[pltpu.VMEM(arg.shape, arg.dtype) for arg in args]
        + [pltpu.SemaphoreType.DMA((len(args),))],
        compiler_params=pltpu.CompilerParams(vmem_limit_bytes=4 * MEBI),
    )(flags, *[pltpu.with_memory_space_constraint(arg, pltpu.HBM) for arg in args])


def place_kernel(flags_ref, meta_ref, places_ref, weights_ref, kept_ref):
    expert, received = flags_ref[0], flags_ref[1].astype(jnp.float32)
    groups, _, tokens = meta_ref.shape
    micros = meta_ref.shape[1] // 4
    rows = places_ref.shape[1]
    earlier = lax.broadcasted_iota(jnp.int32, (tokens, tokens), 0) < lax.broadcasted_iota(
        jnp.int32, (tokens, tokens), 1
    )
    earlier = earlier.astype(jnp.bfloat16)
    row = lax.broadcasted_iota(jnp.int32, (rows, tokens), 0)
    weights = []
    for micro in range(micros):
        for j in range(groups):
            meta = meta_ref[j]
            first = meta[4 * micro : 4 * micro + 1] == expert.astype(jnp.float32)
            second = meta[4 * micro + 1 : 4 * micro + 2] == expert.astype(jnp.float32)
            here = jnp.logical_or(first, second)
            weights.append(
                jnp.where(
                    first, meta[4 * micro + 2 : 4 * micro + 3], meta[4 * micro + 3 : 4 * micro + 4]
                )
            )
            named = jnp.broadcast_to(here.astype(jnp.float32), (16, tokens)).astype(jnp.bfloat16)
            slot = jnp.dot(named, earlier, preferred_element_type=jnp.float32)[0:1]
            target = slot.astype(jnp.int32) * groups + (expert ^ j)
            picked = row == jnp.where(here, target, -1)
            places_ref[micro, :, j * tokens : (j + 1) * tokens] = picked.astype(
                jnp.float32
            ).astype(jnp.bfloat16)
    weights = jnp.concatenate(weights, 0)
    padding = jnp.zeros((tokens - weights.shape[0], tokens), jnp.float32)
    weights_ref[...] = jnp.transpose(jnp.concatenate([weights * received, padding], 0))
    kept_ref[...] = jnp.zeros_like(kept_ref) + received


def find_places(flags, meta, cap):
    groups, quads, tokens = meta.shape
    micros = quads // 4
    in_vmem = pl.BlockSpec(memory_space=pltpu.VMEM)
    return pl.pallas_call(
        place_kernel,
        in_specs=[pl.BlockSpec(memory_space=pltpu.SMEM), in_vmem],
        out_specs=[in_vmem] * 3,
        out_shape=[
            jax.ShapeDtypeStruct((micros, cap * groups, groups * tokens), jnp.bfloat16),
            jax.ShapeDtypeStruct((tokens, tokens), jnp.float32),
            jax.ShapeDtypeStruct((micros, tokens), jnp.float32),
        ],
        compiler_params=pltpu.CompilerParams(vmem_limit_bytes=16 * MEBI),
    )(flags, meta)


def fill_kernel(cut, count, places_ref, weights_ref, *refs):
    token_refs, rows_ref = refs[:count], refs[-1]
    micros, rows, _ = places_ref.shape
    tokens = weights_ref.shape[0]
    late = micros * tokens - cut
    for micro in range(micros):
        blocks = []
        for j in range(2 * count):
            source, top = token_refs[j % count], j // count
            low, high = micro * tokens, (micro + 1) * tokens
            pieces = []
            if low < cut:
                pieces.append(source[top * cut + low : top * cut + min(high, cut), :])
            if high > cut:
                at = 2 * cut + top * late - cut
                pieces.append(source[at + max(low, cut) : at + high, :])
            held = pieces[0] if len(pieces) == 1 else jnp.concatenate(pieces, 0)
            weight = weights_ref[:, micro * 2 * count + j : micro * 2 * count + j + 1]
            blocks.append((held.astype(jnp.float32) * weight).astype(jnp.bfloat16))
        rows_ref[micro * rows : (micro + 1) * rows, :] = jnp.dot(
            places_ref[micro], jnp.concatenate(blocks, 0), preferred_element_type=jnp.float32
        ).astype(jnp.bfloat16)


def fill_rows(places, weights, tokens, cut, gates):
    micros, rows, _ = places.shape
    depth = tokens[0].shape[1]
    in_vmem = pl.BlockSpec(memory_space=pltpu.VMEM)
    return pl.pallas_call(
        functools.partial(fill_kernel, cut, len(tokens)),
        in_specs=[in_vmem] * (2 + len(tokens))
        + [pl.BlockSpec(memory_space=pl.ANY)] * len(gates),
        out_specs=in_vmem,
        out_shape=jax.ShapeDtypeStruct((micros * rows, depth), jnp.bfloat16),
        compiler_params=pltpu.CompilerParams(vmem_limit_bytes=12 * MEBI),
    )(places, weights, *tokens, *gates)


def column_copies(weights_hbm, share, held_ref, done):
    hidden, depth = held_ref.shape
    block = hidden // done.shape[0]
    columns = pl.ds(pl.multiple_of(share * depth, 128), depth)
    return [
        pltpu.make_async_copy(
            weights_hbm.at[0, pl.ds(i * block, block), columns],
            held_ref.at[pl.ds(i * block, block), :],
            done.at[i],
        )
        for i in range(done.shape[0])
    ]


def fetch_kernel(index, flags_ref, weights_hbm, *refs):
    held_ref, done = refs[-2:]
    copies = column_copies(weights_hbm, flags_ref[index], held_ref, done)
    for copy in copies:
        copy.start()
    for copy in copies:
        copy.wait()


def fetch(flags, index, weights, depth, gates):
    return pl.pallas_call(
        functools.partial(fetch_kernel, index),
        in_specs=[pl.BlockSpec(memory_space=pltpu.SMEM), pl.BlockSpec(memory_space=pltpu.HBM)]
        + [pl.BlockSpec(memory_space=pl.ANY)] * len(gates),
        out_specs=pl.BlockSpec(memory_space=pltpu.VMEM),
        out_shape=jax.ShapeDtypeStruct((weights.shape[1], depth), weights.dtype),
        scratch_shapes=[pltpu.SemaphoreType.DMA((COPIES,))],
        compiler_params=pltpu.CompilerParams(vmem_limit_bytes=1 * MEBI),
    )(flags, pltpu.with_memory_space_constraint(weights, pltpu.HBM), *gates)


def multiply(row_refs, weight_refs, here):
    product = None
    for row_ref, weight_ref in zip(row_refs, weight_refs):
        term = lax.dot_general(
            row_ref[...], weight_ref[here, :], NT, preferred_element_type=jnp.float32
        )
        product = term if product is None else product + term
    return product


def first_kernel(block, count, following, flags_ref, weights_hbm, *refs):
    row_refs, weight_refs, rest = refs[:count], refs[count : 2 * count], refs[2 * count :]
    total_ref, token_ref, later_refs, done = rest[0], rest[1], rest[2:-1], rest[-1]
    copies = []
    for i, later_ref in enumerate(later_refs):
        copies += column_copies(weights_hbm, flags_ref[following + i], later_ref, done.at[i])
    for copy in copies:
        copy.start()

    @pl.loop(0, total_ref.shape[1] // block)
    def _(step):
        here = pl.ds(pl.multiple_of(step * block, block), block)
        total_ref[:, here] = multiply(row_refs, weight_refs, here)

    token_ref[...] = total_ref[:8, :128]
    for copy in copies:
        copy.wait()


def multiply_first(flags, following, later, rows, held, weights):
    count, depth = rows[0].shape
    hidden = weights.shape[1]
    in_vmem = pl.BlockSpec(memory_space=pltpu.VMEM)
    outs = pl.pallas_call(
        functools.partial(first_kernel, min(1024, hidden), len(rows), following),
        in_specs=[pl.BlockSpec(memory_space=pltpu.SMEM), pl.BlockSpec(memory_space=pltpu.HBM)]
        + [in_vmem] * (2 * len(rows)),
        out_specs=[in_vmem] * (2 + later),
        out_shape=[
            jax.ShapeDtypeStruct((count, hidden), jnp.float32),
            jax.ShapeDtypeStruct((8, 128), jnp.float32),
        ]
        + [jax.ShapeDtypeStruct((hidden, depth), weights.dtype)] * later,
        scratch_shapes=[pltpu.SemaphoreType.DMA((later, COPIES))],
        compiler_params=pltpu.CompilerParams(vmem_limit_bytes=12 * MEBI),
        cost_estimate=pl.CostEstimate(
            flops=2 * count * depth * len(rows) * hidden,
            bytes_accessed=2 * hidden * depth * len(rows),
            transcendentals=0,
        ),
    )(flags, pltpu.with_memory_space_constraint(weights, pltpu.HBM), *rows, *held)
    return outs[0], outs[1], outs[2:]


def last_kernel(groups, count, *refs):
    row_refs, weight_refs = refs[:count], refs[count : 2 * count]
    total_ref, out_ref = refs[2 * count :]
    micros, cap, block = out_ref.shape[1], out_ref.shape[3], out_ref.shape[5]
    here = pl.ds(pl.multiple_of(pl.program_id(0) * block, block), block)
    product = multiply(row_refs, weight_refs, here) + total_ref[:, here]
    rows = cap * groups
    for micro in range(micros):
        out_ref[0, micro, 0] = (
            product[micro * rows : (micro + 1) * rows]
            .astype(out_ref.dtype)
            .reshape(cap, groups, block)
        )


def multiply_last(rows, held, total, micros, groups):
    count, hidden = total.shape
    depth = rows[0].shape[1]
    block = min(1024, hidden)
    cap = count // (micros * groups)
    in_vmem = pl.BlockSpec(memory_space=pltpu.VMEM)
    return pl.pallas_call(
        functools.partial(last_kernel, groups, len(rows)),
        grid=(hidden // block,),
        in_specs=[in_vmem] * (2 * len(rows) + 1),
        out_specs=pl.BlockSpec((1, micros, 1, cap, groups, block), lambda f: (0, 0, 0, 0, 0, f)),
        out_shape=jax.ShapeDtypeStruct((1, micros, 1, cap, groups, hidden), jnp.bfloat16),
        compiler_params=pltpu.CompilerParams(vmem_limit_bytes=16 * MEBI),
        cost_estimate=pl.CostEstimate(
            flops=2 * count * depth * len(rows) * hidden,
            bytes_accessed=2 * hidden * depth * len(rows),
            transcendentals=0,
        ),
    )(*rows, *held, total)


def per_device(out_grad, expert_outputs, logits, routes, down_weights):
    micros, token_count, share = out_grad.shape[1:]
    experts, shares = lax.axis_size("expert"), lax.axis_size("dp")
    cap = min(token_count, 2 * token_count // experts + token_count // 32)
    expert, mine = lax.axis_index("expert"), lax.axis_index("dp")
    sections = lax.axis_size("pipe")
    received = lax.axis_index("pipe") < sections - 1
    together = 1
    while (share * together) % 128:
        together *= 2
    sets = list(range(shares // together))
    half = len(sets) // 2
    gated = sets[half:]
    if together == 1:
        sets, half, gated = [2,0,1,3, *sets[4:]], 2, [1, 3]
    flags = jnp.stack([expert, received, *[(mine // together) ^ which for which in sets]])
    flags = flags.astype(jnp.int32)
    top = experts // 2
    cut = micros * token_count * 11 // 16
    own = out_grad.reshape(micros * token_count, share)
    early, late = own[:cut], own[cut:]
    late = from_next(late)
    direct = {2: from_next(early, 2)}
    late_top = swap(late, top)

    extra = extra_rows(
        share,
        flags,
        logits[0].transpose(0, 2, 1),
        routes[0].transpose(0, 2, 1),
        out_grad[0],
        expert_outputs[0],
    )
    extras = {}
    direct[0] = from_next(join([early, extra], [late]))
    direct[1] = from_next(join([early, extra], [direct[0]]), 1)
    pair = join([late, late_top])
    pairs = {0: pair, 2: from_share(pair, 2, sections - 1), 1: from_share(pair, 1, sections - 1)}
    for k in range(3, shares):
        direct[k] = from_next(join([early, extra], [direct[k - 1]]), k)
        pairs[k] = from_share(join([pair], [pairs[k - 2]]), k, sections - 1)
    near = from_next(join([extra], [direct[shares - 1]]), 2)
    zero_top = swap(direct[0], top)
    direct_top = {0: zero_top[:cut]}
    for k in range(shares):
        if k != 2:
            direct[k], extras[k] = direct[k][:cut], direct[k][cut:]
        if k:
            direct_top[k] = swap(direct[k], top)

    def spread(x):
        held, bit = {0: x}, top // 2
        while bit:
            for j in sorted(held):
                held[j ^ bit] = swap(held[j], bit)
            bit //= 2
        return [held[j] for j in sorted(held)]

    metas = spread(jnp.stack([x[:, :token_count] for x in (extras[0], zero_top[cut:])]))
    metas = jnp.concatenate([jnp.stack([m[b] for m in metas]) for b in range(2)], 0)
    metas = metas.astype(jnp.float32).reshape(experts, micros, 8, token_count)
    gap = metas[:, :, 2] + metas[:, :, 3] + metas[:, :, 4]
    weight_first, weight_second = jax.nn.sigmoid(gap), jax.nn.sigmoid(-gap)
    meta = jnp.stack(
        [
            metas[:, :, 0],
            metas[:, :, 1],
            weight_first,
            weight_second,
        ],
        2,
    ).reshape(experts, 4 * micros, token_count)

    places, weights, kept = find_places(flags, meta, cap)
    def filled(which, gates, fill_gates):
        pieces = []
        for k in range(which * together, (which + 1) * together):
            pieces.append(spread(join([direct[k], direct_top[k], pairs[k]], gates)))
        tokens = pieces[0]
        if together > 1:
            order = jnp.arange(together) ^ (mine % together)
            tokens = []
            for j in range(top):
                stacked = jnp.take(jnp.stack([piece[j] for piece in pieces]), order, axis=0)
                tokens.append(stacked.transpose(1, 0, 2).reshape(-1, together * share))
        return fill_rows(places, weights, tokens, cut, fill_gates)

    fetch_gates = [[pairs[2]], [pairs[2]]]
    held = []
    for i in range(half):
        gates = fetch_gates[i] if i < len(fetch_gates) else []
        held.append(fetch(flags, 2 + i, down_weights, together * share, gates))
    rows = [filled(which, [], []) for which in sets[:half]]
    total, done, held = multiply_first(
        flags, 2 + half, len(sets) - half, rows, held, down_weights
    )
    extras[2] = join([near], [done])
    scores = 0.0
    for k in range(shares):
        terms = extras[k][:, :token_count].astype(jnp.float32).reshape(micros, 8, token_count)
        scores += terms[:, 5] + terms[:, 6] + terms[:, 7]
    slope = jnp.where(kept > 0, weight_first[0] * weight_second[0] * scores, 0.0)
    moved_logits = jnp.stack([slope, -slope], -1).astype(jnp.bfloat16)[None]

    rows = [filled(which, [done] if which in gated else [], []) for which in sets[half:]]
    hidden = multiply_last(rows, held, total, micros, experts)
    return hidden.transpose(0, 1, 2, 4, 3, 5), moved_logits


def solution(mesh):
    in_specs = (
        P("pipe", None, "expert", "dp"),
        P("pipe", None, "expert", None, "dp"),
        P("pipe", None, "expert", None),
        P("pipe", None, "expert", None),
        P("expert", "dp", None),
    )
    out_specs = (P("pipe", None, "expert", None, None, "dp"), P("pipe", None, "expert", None))
    return jax.shard_map(
        per_device, mesh=mesh, in_specs=in_specs, out_specs=out_specs, check_vma=False
    )
```

time: 76.6 us -> 69 us (0.901)
  starting transfers between devices: 31.6 us -> 22.7 us
  Pallas kernels: 22.8 us -> 30.4 us
  waiting for transfers between devices: 15.6 us -> 12 us
  other arithmetic: 2.82 us -> 0.13 us
    pallas_call x3 -> x5, Pallas kernels: 19.3 us -> 26.3 us  [the longest x1 8.84 us: multiply_last(): pl.pallas_call(functools.partial(last_kernel, groups, len(rows)), grid=(h...]
    ppermute x5 -> x3, waiting for transfers between devices: 6.55 us -> 0.16 us  [from_share(): return lax.ppermute(x, ('pipe', 'dp', 'expert'), pairs)]
    ppermute x10, starting transfers between devices: 18.1 us -> 12.3 us  [swap(): return lax.ppermute(x, 'expert', [(e, e ^ bit) for e in range(experts)])]
    ppermute x10, waiting for transfers between devices: 2.36 us -> 5.41 us  [swap(): return lax.ppermute(x, 'expert', [(e, e ^ bit) for e in range(experts)])]
    ppermute x5 -> x3, starting transfers between devices: 4.52 us -> 2.62 us  [from_share(): return lax.ppermute(x, ('pipe', 'dp', 'expert'), pairs)]
    convert_element_type x2 -> x1, other arithmetic: 1.68 us -> 0.03 us  [per_device(): metas = metas.astype(jnp.float32).reshape(experts, micros, 8, token_count)]
    ppermute x5 -> x6, starting transfers between devices: 8.97 us -> 7.82 us  [from_next(): return lax.ppermute(x, ('pipe', 'dp'), pairs)]
    sub x1 -> x0, other arithmetic: 0.81 us -> none  [per_device(): scores = jnp.sum(grads * (outputs[:, :, 0] - outputs[:, :, 1]), -1)]
  transfers between devices with their start and end apart: 20 -> 19, of which waited for: 8 -> 8; matrix products, arithmetic and copies ran while one was open for 6% -> 3% of each run, Pallas kernels for 4% -> 30%
where the time goes in v4:
time: 69 us; the launch traced here: 68.9 us
  Pallas kernels  30.4 us (44%)
  starting transfers between devices  22.7 us (33%)
  waiting for transfers between devices  12 us (17%)
  local copies, waits for them, and re-layouts  2.67 us (4%)
  between operations  0.97 us (1%)
    ppermute x10, starting transfers between devices, swap(): return lax.ppermute(x, 'expert', [(e, e ^ bit) for e in range(experts)])  12.3 us
    pallas_call x1, Pallas kernels, multiply_last(): pl.pallas_call(functools.partial(last_kernel, groups, len(rows)), grid=(h...  8.84 us
    pallas_call x1, Pallas kernels, multiply_first(): pl.pallas_call(functools.partial(first_kernel, min(1024, hidden), len(row...  8.35 us
    ppermute x6, starting transfers between devices, from_next(): return lax.ppermute(x, ('pipe', 'dp'), pairs)  7.82 us
    pallas_call x2, Pallas kernels, fetch(): pl.pallas_call(functools.partial(fetch_kernel, index), in_specs=[pl.Block...  6.87 us
    ppermute x6, waiting for transfers between devices, from_next(): return lax.ppermute(x, ('pipe', 'dp'), pairs)  6.42 us
    ppermute x10, waiting for transfers between devices, swap(): return lax.ppermute(x, 'expert', [(e, e ^ bit) for e in range(experts)])  5.41 us
    pallas_call x4, Pallas kernels, fill_rows(): pl.pallas_call(functools.partial(fill_kernel, cut, len(tokens)), in_specs...  2.86 us
  transfers between devices with their start and end apart: 19, of which 8 were waited for; matrix products, arithmetic and copies ran while one was open for 3% of the time, Pallas kernels for 30%

profile of v4, /device:TPU:9, one launch (start us, length us, event | category | flops | bytes accessed | tf_op | source)
XLA Modules:
  0.0 68.9 jit_solution(11903716853669276119)
XLA Ops:
  0.6 0.9 %slice.138 = bf16[80,768]{1,0:T(8,128)(2,1)S(1)} slice(bf16[256,768]{1,0:T(8,128)(2,1)} %bitcast.75), slice={[176:256], [0:768]} | slice | bytes 245760 | tf_op jit(solution)/shard_map/slice | solution.py:352
  1.5 1.3 %collective-permute-start = (bf16[80,768]{1,0:T(8,128)(2,1)S(1)}, bf16[80,768]{1,0:T(8,128)(2,1)S(1)}, u32[]{:S(2)}, u32[]{:S(2)}) collective-permute-start(bf16[80,768]{1,0:T(8,128)(2,1)S(1)} %slice.138), channel_id=1, source_target_pairs={{0,16},{4,20},{8,24},{12,28},{16,0},{20,4},{24,8},{28,12},{1,17},{... | collective-permute-start | bytes 368648 | tf_op jit(solution)/shard_map/ppermute | solution.py:25
  2.8 1.0 %slice.137.refs_0_ = bf16[176,768]{1,0:T(8,128)(2,1)S(1)} slice(bf16[256,768]{1,0:T(8,128)(2,1)} %bitcast.76), slice={[0:176], [0:768]} | slice | bytes 540672 | tf_op jit(solution)/shard_map/slice | solution.py:352
  3.9 2.3 %shard_map.68.refs_1_.refs_0_ = bf16[16,768]{1,0:T(8,128)(2,1)S(1)} custom-call(s32[6]{0:T(128)S(1)} %stack.55._.flags_ref, f32[2,2,128]{2,1,0:T(2,128)} %bitcast.91, s32[2,2,128]{2,1,0:T(2,128)} %bitcast.92, bf16[2,128,768]{2,1,0:T(8,128)(2,1)} %bitcast.77, bf16[2,128,2,768]{3,2,1,0:T(2,128)(2,1)} %bitcast.78), custom_call_target="tpu_custom_call" | custom-call | tf_op jit(solution)/shard_map/pallas_call | solution.py:105
  6.2 0.9 %collective-permute-start.1 = (bf16[192,768]{1,0:T(8,128)(2,1)S(1)}, bf16[192,768]{1,0:T(8,128)(2,1)S(1)}, u32[]{:S(2)}, u32[]{:S(2)}) collective-permute-start(bf16[192,768]{1,0:T(8,128)(2,1)S(1)} %shard_map.69), channel_id=1, source_target_pairs={{0,16},{4,20},{8,24},{12,28},{16,0},{20,4},{24,8},{28,12},{1,17},{... | collective-permute-start | bytes 884744 | tf_op jit(solution)/shard_map/ppermute | solution.py:25
  7.1 0.6 collective-permute-start.8
  7.7 1.2 %collective-permute-start.6 = (bf16[80,768]{1,0:T(8,128)(2,1)S(1)}, bf16[80,768]{1,0:T(8,128)(2,1)S(1)}, u32[]{:S(2)}, u32[]{:S(2)}) collective-permute-start(bf16[80,768]{1,0:T(8,128)(2,1)S(1)} %collective-permute-done.refs_2_.refs_0_), channel_id=1, source_target_pairs={{0,2},{1,3},{2,0},{3,1},{4,6},{5,7},{6,4},{7,5},{8,10},{9,11},{10,... | collective-permute-start | bytes 368648 | tf_op jit(solution)/shard_map/ppermute | solution.py:44
  9.0 2.8 %collective-permute-done.6.refs_1_ = bf16[80,768]{1,0:T(8,128)(2,1)S(1)} collective-permute-done((bf16[80,768]{1,0:T(8,128)(2,1)S(1)}, bf16[80,768]{1,0:T(8,128)(2,1)S(1)}, u32[]{:S(2)}, u32[]{:S(2)}) %collective-permute-start.6) | collective-permute-done | bytes 122912 | tf_op jit(solution)/shard_map/ppermute | solution.py:44
  11.8 2.4 %collective-permute-start.10 = (bf16[160,768]{1,0:T(8,128)(2,1)S(1)}, bf16[160,768]{1,0:T(8,128)(2,1)S(1)}, u32[]{:S(2)}, u32[]{:S(2)}) collective-permute-start(bf16[160,768]{1,0:T(8,128)(2,1)S(1)} %shard_map.72.refs_2_.refs_0_), channel_id=1, source_target_pairs={{0,8},{1,9},{2,10},{3,11},{4,12},{5,13},{6,14},{7,15},{8,0},{9,1},... | collective-permute-start | bytes 737288 | tf_op jit(solution)/shard_map/ppermute | solution.py:39
  14.3 3.3 %collective-permute-done.8.refs_0_.refs_2_ = bf16[176,768]{1,0:T(8,128)(2,1)S(1)} collective-permute-done((bf16[176,768]{1,0:T(8,128)(2,1)S(1)}, bf16[176,768]{1,0:T(8,128)(2,1)S(1)}, u32[]{:S(2)}, u32[]{:S(2)}) %collective-permute-start.8) | collective-permute-done | bytes 270368 | tf_op jit(solution)/shard_map/ppermute | solution.py:25
  17.7 4.9 %collective-permute-start.14 = (bf16[192,768]{1,0:T(8,128)(2,1)S(1)}, bf16[192,768]{1,0:T(8,128)(2,1)S(1)}, u32[]{:S(2)}, u32[]{:S(2)}) collective-permute-start(bf16[192,768]{1,0:T(8,128)(2,1)S(1)} %shard_map.82), channel_id=1, source_target_pairs={{0,16},{4,20},{8,24},{12,28},{16,12},{20,8},{24,4},{28,0},{1,17},{... | collective-permute-start | bytes 884744 | tf_op jit(solution)/shard_map/ppermute | solution.py:25
  22.5 1.2 %collective-permute-start.9 = (bf16[176,768]{1,0:T(8,128)(2,1)S(1)}, bf16[176,768]{1,0:T(8,128)(2,1)S(1)}, u32[]{:S(2)}, u32[]{:S(2)}) collective-permute-start(bf16[176,768]{1,0:T(8,128)(2,1)S(1)} %collective-permute-done.8.refs_0_.refs_2_), channel_id=1, source_target_pairs={{0,2},{1,3},{2,0},{3,1},{4,6},{5,7},{6,4},{7,5},{8,10},{9,11},{10,... | collective-permute-start | bytes 811016 | tf_op jit(solution)/shard_map/ppermute | solution.py:44
  24.6 3.4 %shard_map.77.refs_2_ = bf16[4096,768]{1,0:T(8,128)(2,1)S(1)} custom-call(s32[6]{0:T(128)S(1)} %stack.55._.flags_ref, bf16[1,4096,3072]{2,1,0:T(8,128)(2,1)} %weights_hbm.5, bf16[160,768]{1,0:T(8,128)(2,1)S(1)} %collective-permute-done.10.refs_2_.refs_0_), custom_call_target="tpu_custom_call" | custom-call | tf_op jit(solution)/shard_map/pallas_call | solution.py:231
  28.0 3.4 %shard_map.78.refs_3_ = bf16[4096,768]{1,0:T(8,128)(2,1)S(1)} custom-call(s32[6]{0:T(128)S(1)} %stack.55._.flags_ref, bf16[1,4096,3072]{2,1,0:T(8,128)(2,1)} %weights_hbm.5, bf16[160,768]{1,0:T(8,128)(2,1)S(1)} %collective-permute-done.10.refs_2_.refs_0_), custom_call_target="tpu_custom_call" | custom-call | tf_op jit(solution)/shard_map/pallas_call | solution.py:231
  31.5 4.1 %collective-permute-start.11 = (bf16[512,768]{1,0:T(8,128)(2,1)S(1)}, bf16[512,768]{1,0:T(8,128)(2,1)S(1)}, u32[]{:S(2)}, u32[]{:S(2)}) collective-permute-start(bf16[512,768]{1,0:T(8,128)(2,1)S(1)} %shard_map.73.refs_0_), channel_id=1, source_target_pairs={{0,1},{1,0},{2,3},{3,2},{4,5},{5,4},{6,7},{7,6},{8,9},{9,8},{10,11... | collective-permute-start | bytes 2359304 | tf_op jit(solution)/shard_map/ppermute | solution.py:44
  35.7 0.4 collective-permute-done.2
  36.1 1.2 %collective-permute-start.15 = (bf16[176,768]{1,0:T(8,128)(2,1)S(1)}, bf16[176,768]{1,0:T(8,128)(2,1)S(1)}, u32[]{:S(2)}, u32[]{:S(2)}) collective-permute-start(bf16[176,768]{1,0:T(8,128)(2,1)S(1)} %slice.147.refs_0_), channel_id=1, source_target_pairs={{0,2},{1,3},{2,0},{3,1},{4,6},{5,7},{6,4},{7,5},{8,10},{9,11},{10,... | collective-permute-start | bytes 811016 | tf_op jit(solution)/shard_map/ppermute | solution.py:44
  37.3 3.1 %collective-permute-done.4 = bf16[192,768]{1,0:T(8,128)(2,1)S(1)} collective-permute-done((bf16[192,768]{1,0:T(8,128)(2,1)S(1)}, bf16[192,768]{1,0:T(8,128)(2,1)S(1)}, u32[]{:S(2)}, u32[]{:S(2)}) %collective-permute-start.4) | collective-permute-done | bytes 294944 | tf_op jit(solution)/shard_map/ppermute | solution.py:25
  40.4 1.9 %collective-permute-start.3 = (bf16[2,16,128]{2,1,0:T(8,128)(2,1)S(1)}, bf16[2,16,128]{2,1,0:T(8,128)(2,1)S(1)}, u32[]{:S(2)}, u32[]{:S(2)}) collective-permute-start(bf16[2,16,128]{2,1,0:T(8,128)(2,1)S(1)} %pad_maximum_fusion.1), channel_id=1, source_target_pairs={{0,1},{1,0},{2,3},{3,2},{4,5},{5,4},{6,7},{7,6},{8,9},{9,8},{10,11... | collective-permute-start | bytes 24584 | tf_op jit(solution)/shard_map/ppermute | solution.py:44
  42.4 0.7 %collective-permute-done.3 = bf16[2,16,128]{2,1,0:T(8,128)(2,1)S(1)} collective-permute-done((bf16[2,16,128]{2,1,0:T(8,128)(2,1)S(1)}, bf16[2,16,128]{2,1,0:T(8,128)(2,1)S(1)}, u32[]{:S(2)}, u32[]{:S(2)}) %collective-permute-start.3) | collective-permute-done | bytes 8224 | tf_op jit(solution)/shard_map/ppermute | solution.py:44
  43.6 0.9 %shard_map.70 = (bf16[2,272,512]{2,1,0:T(8,128)(2,1)S(1)}, f32[128,128]{1,0:T(8,128)S(1)}, f32[2,128]{1,0:T(2,128)S(1)}) custom-call(s32[6]{0:T(128)S(1)} %stack.55._.flags_ref, f32[4,8,128]{2,1,0:T(8,128)S(1)} %bitcast.73), custom_call_target="tpu_custom_call" | custom-call | tf_op jit(solution)/shard_map/pallas_call | solution.py:156
  44.5 1.3 %collective-permute-start.5 = (bf16[176,768]{1,0:T(8,128)(2,1)S(1)}, bf16[176,768]{1,0:T(8,128)(2,1)S(1)}, u32[]{:S(2)}, u32[]{:S(2)}) collective-permute-start(bf16[176,768]{1,0:T(8,128)(2,1)S(1)} %slice.144.refs_0_), channel_id=1, source_target_pairs={{0,2},{1,3},{2,0},{3,1},{4,6},{5,7},{6,4},{7,5},{8,10},{9,11},{10,... | collective-permute-start | bytes 811016 | tf_op jit(solution)/shard_map/ppermute | solution.py:44
  45.8 0.7 %shard_map.74.refs_0_ = bf16[544,768]{1,0:T(8,128)(2,1)S(1)} custom-call(bf16[2,272,512]{2,1,0:T(8,128)(2,1)S(1)} %get-tuple-element.9.places_ref, f32[128,128]{1,0:T(8,128)S(1)} %get-tuple-element.10.weights_ref, bf16[512,768]{1,0:T(8,128)(2,1)S(1)} %shard_map.73.refs_0_, bf16[512,768]{1,0:T(8,128)(2,1)S(1)} %collective-permute-done.11.refs_1_), custom_call_target="tpu_custom_call" | custom-call | tf_op jit(solution)/shard_map/pallas_call | solution.py:197
  46.6 0.7 %shard_map.76.refs_1_ = bf16[544,768]{1,0:T(8,128)(2,1)S(1)} custom-call(bf16[2,272,512]{2,1,0:T(8,128)(2,1)S(1)} %get-tuple-element.9.places_ref, f32[128,128]{1,0:T(8,128)S(1)} %get-tuple-element.10.weights_ref, bf16[512,768]{1,0:T(8,128)(2,1)S(1)} %shard_map.75.refs_0_, bf16[512,768]{1,0:T(8,128)(2,1)S(1)} %collective-permute-done.12.refs_1_), custom_call_target="tpu_custom_call" | custom-call | tf_op jit(solution)/shard_map/pallas_call | solution.py:197
  47.3 8.4 %shard_map.79 = (f32[544,4096]{1,0:T(8,128)S(1)}, f32[8,128]{1,0:T(8,128)S(1)}, bf16[4096,768]{1,0:T(8,128)(2,1)S(1)}, bf16[4096,768]{1,0:T(8,128)(2,1)S(1)}) custom-call(s32[6]{0:T(128)S(1)} %stack.55._.flags_ref, bf16[1,4096,3072]{2,1,0:T(8,128)(2,1)} %weights_hbm.5, bf16[544,768]{1,0:T(8,128)(2,1)S(1)} %shard_map.74.refs_0_, ...), custom_call_target="tpu_custom_call" | custom-call | flops 6845104128 | bytes 12582912 | tf_op jit(solution)/shard_map/pallas_call | solution.py:275
  55.7 0.5 collective-permute-start.17
  56.5 0.6 copy.24
  57.1 1.1 %collective-permute-done.17.refs_1_ = bf16[512,768]{1,0:T(8,128)(2,1)S(1)} collective-permute-done((bf16[512,768]{1,0:T(8,128)(2,1)S(1)}, bf16[512,768]{1,0:T(8,128)(2,1)S(1)}, u32[]{:S(2)}, u32[]{:S(2)}) %collective-permute-start.17) | collective-permute-done | bytes 786464 | tf_op jit(solution)/shard_map/ppermute | solution.py:44
  58.2 0.7 %shard_map.85.refs_1_ = bf16[544,768]{1,0:T(8,128)(2,1)S(1)} custom-call(bf16[2,272,512]{2,1,0:T(8,128)(2,1)S(1)} %get-tuple-element.9.places_ref, f32[128,128]{1,0:T(8,128)S(1)} %get-tuple-element.10.weights_ref, bf16[512,768]{1,0:T(8,128)(2,1)S(1)} %shard_map.84.refs_0_, bf16[512,768]{1,0:T(8,128)(2,1)S(1)} %collective-permute-done.17.refs_1_), custom_call_target="tpu_custom_call" | custom-call | tf_op jit(solution)/shard_map/pallas_call | solution.py:197
  58.9 0.4 collective-permute-done.13.refs_1_
  59.3 0.7 %shard_map.81.refs_0_ = bf16[544,768]{1,0:T(8,128)(2,1)S(1)} custom-call(bf16[2,272,512]{2,1,0:T(8,128)(2,1)S(1)} %get-tuple-element.9.places_ref, f32[128,128]{1,0:T(8,128)S(1)} %get-tuple-element.10.weights_ref, bf16[512,768]{1,0:T(8,128)(2,1)S(1)} %shard_map.80.refs_0_, bf16[512,768]{1,0:T(8,128)(2,1)S(1)} %collective-permute-done.13.refs_1_), custom_call_target="tpu_custom_call" | custom-call | tf_op jit(solution)/shard_map/pallas_call | solution.py:197
  60.0 8.8 %shard_map.86 = bf16[1,2,1,68,4,4096]{5,4,3,2,1,0:T(4,128)(2,1)} custom-call(bf16[544,768]{1,0:T(8,128)(2,1)S(1)} %shard_map.81.refs_0_, bf16[544,768]{1,0:T(8,128)(2,1)S(1)} %shard_map.85.refs_1_, bf16[4096,768]{1,0:T(8,128)(2,1)S(1)} %get-tuple-element.12.refs_2_, bf16[4096,768]{1,0:T(8,128)(2,1)S(1)} %get-tuple-element.13.refs_3_, ...), custom_call_target="tpu_custom_call" | custom-call | flops 6845104128 | bytes 12582912 | tf_op jit(solution)/shard_map/pallas_call | solution.py:317
  (59 shorter events, 2.0 us)
Async XLA Ops:
  1.5 4.6 %collective-permute-start = (bf16[80,768]{1,0:T(8,128)(2,1)S(1)}, bf16[80,768]{1,0:T(8,128)(2,1)S(1)}, u32[]{:S(2)}, u32[]{:S(2)}) collective-permute-start(bf16[80,768]{1,0:T(8,128)(2,1)S(1)} %slice.138), channel_id=1, source_target_pairs={{0,16},{4,20},{8,24},{12,28},{16,0},{20,4},{24,8},{28,12},{1,17},{... | collective-permute-start | bytes 368648 | tf_op jit(solution)/shard_map/ppermute | solution.py:25
  6.2 17.6 %collective-permute-start.1 = (bf16[192,768]{1,0:T(8,128)(2,1)S(1)}, bf16[192,768]{1,0:T(8,128)(2,1)S(1)}, u32[]{:S(2)}, u32[]{:S(2)}) collective-permute-start(bf16[192,768]{1,0:T(8,128)(2,1)S(1)} %shard_map.69), channel_id=1, source_target_pairs={{0,16},{4,20},{8,24},{12,28},{16,0},{20,4},{24,8},{28,12},{1,17},{... | collective-permute-start | bytes 884744 | tf_op jit(solution)/shard_map/ppermute | solution.py:25
  7.1 10.5 %collective-permute-start.8 = (bf16[176,768]{1,0:T(8,128)(2,1)S(1)}, bf16[176,768]{1,0:T(8,128)(2,1)S(1)}, u32[]{:S(2)}, u32[]{:S(2)}) collective-permute-start(bf16[176,768]{1,0:T(8,128)(2,1)S(1)} %slice.137.refs_0_), channel_id=1, source_target_pairs={{0,16},{4,20},{8,24},{12,28},{16,8},{20,12},{24,0},{28,4},{1,17},{... | collective-permute-start | bytes 811016 | tf_op jit(solution)/shard_map/ppermute | solution.py:25
  7.7 4.0 %collective-permute-start.6 = (bf16[80,768]{1,0:T(8,128)(2,1)S(1)}, bf16[80,768]{1,0:T(8,128)(2,1)S(1)}, u32[]{:S(2)}, u32[]{:S(2)}) collective-permute-start(bf16[80,768]{1,0:T(8,128)(2,1)S(1)} %collective-permute-done.refs_2_.refs_0_), channel_id=1, source_target_pairs={{0,2},{1,3},{2,0},{3,1},{4,6},{5,7},{6,4},{7,5},{8,10},{9,11},{10,... | collective-permute-start | bytes 368648 | tf_op jit(solution)/shard_map/ppermute | solution.py:44
  11.8 12.7 %collective-permute-start.10 = (bf16[160,768]{1,0:T(8,128)(2,1)S(1)}, bf16[160,768]{1,0:T(8,128)(2,1)S(1)}, u32[]{:S(2)}, u32[]{:S(2)}) collective-permute-start(bf16[160,768]{1,0:T(8,128)(2,1)S(1)} %shard_map.72.refs_2_.refs_0_), channel_id=1, source_target_pairs={{0,8},{1,9},{2,10},{3,11},{4,12},{5,13},{6,14},{7,15},{8,0},{9,1},... | collective-permute-start | bytes 737288 | tf_op jit(solution)/shard_map/ppermute | solution.py:39
  14.1 9.9 %collective-permute-start.7 = (bf16[160,768]{1,0:T(8,128)(2,1)S(1)}, bf16[160,768]{1,0:T(8,128)(2,1)S(1)}, u32[]{:S(2)}, u32[]{:S(2)}) collective-permute-start(bf16[160,768]{1,0:T(8,128)(2,1)S(1)} %shard_map.72.refs_2_.refs_0_), channel_id=1, source_target_pairs={{0,4},{1,5},{2,6},{3,7},{4,0},{5,1},{6,2},{7,3},{8,12},{9,13},{10,... | collective-permute-start | bytes 737288 | tf_op jit(solution)/shard_map/ppermute | solution.py:39
  17.7 17.9 %collective-permute-start.14 = (bf16[192,768]{1,0:T(8,128)(2,1)S(1)}, bf16[192,768]{1,0:T(8,128)(2,1)S(1)}, u32[]{:S(2)}, u32[]{:S(2)}) collective-permute-start(bf16[192,768]{1,0:T(8,128)(2,1)S(1)} %shard_map.82), channel_id=1, source_target_pairs={{0,16},{4,20},{8,24},{12,28},{16,12},{20,8},{24,4},{28,0},{1,17},{... | collective-permute-start | bytes 884744 | tf_op jit(solution)/shard_map/ppermute | solution.py:25
  22.5 8.9 %collective-permute-start.9 = (bf16[176,768]{1,0:T(8,128)(2,1)S(1)}, bf16[176,768]{1,0:T(8,128)(2,1)S(1)}, u32[]{:S(2)}, u32[]{:S(2)}) collective-permute-start(bf16[176,768]{1,0:T(8,128)(2,1)S(1)} %collective-permute-done.8.refs_0_.refs_2_), channel_id=1, source_target_pairs={{0,2},{1,3},{2,0},{3,1},{4,6},{5,7},{6,4},{7,5},{8,10},{9,11},{10,... | collective-permute-start | bytes 811016 | tf_op jit(solution)/shard_map/ppermute | solution.py:44
  23.8 16.6 %collective-permute-start.4 = (bf16[192,768]{1,0:T(8,128)(2,1)S(1)}, bf16[192,768]{1,0:T(8,128)(2,1)S(1)}, u32[]{:S(2)}, u32[]{:S(2)}) collective-permute-start(bf16[192,768]{1,0:T(8,128)(2,1)S(1)} %shard_map.71), channel_id=1, source_target_pairs={{0,16},{4,20},{8,24},{12,28},{16,4},{20,0},{24,12},{28,8},{1,17},{... | collective-permute-start | bytes 884744 | tf_op jit(solution)/shard_map/ppermute | solution.py:25
  24.0 12.1 %collective-permute-start.2 = (bf16[192,768]{1,0:T(8,128)(2,1)S(1)}, bf16[192,768]{1,0:T(8,128)(2,1)S(1)}, u32[]{:S(2)}, u32[]{:S(2)}) collective-permute-start(bf16[192,768]{1,0:T(8,128)(2,1)S(1)} %collective-permute-done.1.refs_2_), channel_id=1, source_target_pairs={{0,2},{1,3},{2,0},{3,1},{4,6},{5,7},{6,4},{7,5},{8,10},{9,11},{10,... | collective-permute-start | bytes 884744 | tf_op jit(solution)/shard_map/ppermute | solution.py:44
  24.5 31.2 %collective-permute-start.16 = (bf16[160,768]{1,0:T(8,128)(2,1)S(1)}, bf16[160,768]{1,0:T(8,128)(2,1)S(1)}, u32[]{:S(2)}, u32[]{:S(2)}) collective-permute-start(bf16[160,768]{1,0:T(8,128)(2,1)S(1)} %shard_map.83), channel_id=1, source_target_pairs={{0,12},{1,13},{2,14},{3,15},{4,8},{5,9},{6,10},{7,11},{8,4},{9,5},... | collective-permute-start | bytes 737288 | tf_op jit(solution)/shard_map/ppermute | solution.py:39
  31.5 13.0 %collective-permute-start.11 = (bf16[512,768]{1,0:T(8,128)(2,1)S(1)}, bf16[512,768]{1,0:T(8,128)(2,1)S(1)}, u32[]{:S(2)}, u32[]{:S(2)}) collective-permute-start(bf16[512,768]{1,0:T(8,128)(2,1)S(1)} %shard_map.73.refs_0_), channel_id=1, source_target_pairs={{0,1},{1,0},{2,3},{3,2},{4,5},{5,4},{6,7},{7,6},{8,9},{9,8},{10,11... | collective-permute-start | bytes 2359304 | tf_op jit(solution)/shard_map/ppermute | solution.py:44
  35.6 20.8 %collective-permute-start.18 = (bf16[16,768]{1,0:T(8,128)(2,1)S(1)}, bf16[16,768]{1,0:T(8,128)(2,1)S(1)}, u32[]{:S(2)}, u32[]{:S(2)}) collective-permute-start(bf16[16,768]{1,0:T(8,128)(2,1)S(1)} %shard_map.87), channel_id=1, source_target_pairs={{0,16},{4,20},{8,24},{12,28},{16,8},{20,12},{24,0},{28,4},{1,17},{... | collective-permute-start | bytes 73736 | tf_op jit(solution)/shard_map/ppermute | solution.py:25
  36.1 19.6 %collective-permute-start.15 = (bf16[176,768]{1,0:T(8,128)(2,1)S(1)}, bf16[176,768]{1,0:T(8,128)(2,1)S(1)}, u32[]{:S(2)}, u32[]{:S(2)}) collective-permute-start(bf16[176,768]{1,0:T(8,128)(2,1)S(1)} %slice.147.refs_0_), channel_id=1, source_target_pairs={{0,2},{1,3},{2,0},{3,1},{4,6},{5,7},{6,4},{7,5},{8,10},{9,11},{10,... | collective-permute-start | bytes 811016 | tf_op jit(solution)/shard_map/ppermute | solution.py:44
  40.4 2.7 %collective-permute-start.3 = (bf16[2,16,128]{2,1,0:T(8,128)(2,1)S(1)}, bf16[2,16,128]{2,1,0:T(8,128)(2,1)S(1)}, u32[]{:S(2)}, u32[]{:S(2)}) collective-permute-start(bf16[2,16,128]{2,1,0:T(8,128)(2,1)S(1)} %pad_maximum_fusion.1), channel_id=1, source_target_pairs={{0,1},{1,0},{2,3},{3,2},{4,5},{5,4},{6,7},{7,6},{8,9},{9,8},{10,11... | collective-permute-start | bytes 24584 | tf_op jit(solution)/shard_map/ppermute | solution.py:44
  43.1 3.4 %collective-permute-start.12 = (bf16[512,768]{1,0:T(8,128)(2,1)S(1)}, bf16[512,768]{1,0:T(8,128)(2,1)S(1)}, u32[]{:S(2)}, u32[]{:S(2)}) collective-permute-start(bf16[512,768]{1,0:T(8,128)(2,1)S(1)} %shard_map.75.refs_0_), channel_id=1, source_target_pairs={{0,1},{1,0},{2,3},{3,2},{4,5},{5,4},{6,7},{7,6},{8,9},{9,8},{10,11... | collective-permute-start | bytes 2359304 | tf_op jit(solution)/shard_map/ppermute | solution.py:44
  44.5 11.7 %collective-permute-start.5 = (bf16[176,768]{1,0:T(8,128)(2,1)S(1)}, bf16[176,768]{1,0:T(8,128)(2,1)S(1)}, u32[]{:S(2)}, u32[]{:S(2)}) collective-permute-start(bf16[176,768]{1,0:T(8,128)(2,1)S(1)} %slice.144.refs_0_), channel_id=1, source_target_pairs={{0,2},{1,3},{2,0},{3,1},{4,6},{5,7},{6,4},{7,5},{8,10},{9,11},{10,... | collective-permute-start | bytes 811016 | tf_op jit(solution)/shard_map/ppermute | solution.py:44
  55.7 2.4 %collective-permute-start.17 = (bf16[512,768]{1,0:T(8,128)(2,1)S(1)}, bf16[512,768]{1,0:T(8,128)(2,1)S(1)}, u32[]{:S(2)}, u32[]{:S(2)}) collective-permute-start(bf16[512,768]{1,0:T(8,128)(2,1)S(1)} %shard_map.84.refs_0_), channel_id=1, source_target_pairs={{0,1},{1,0},{2,3},{3,2},{4,5},{5,4},{6,7},{7,6},{8,9},{9,8},{10,11... | collective-permute-start | bytes 2359304 | tf_op jit(solution)/shard_map/ppermute | solution.py:44
  56.3 3.0 %collective-permute-start.13 = (bf16[512,768]{1,0:T(8,128)(2,1)S(1)}, bf16[512,768]{1,0:T(8,128)(2,1)S(1)}, u32[]{:S(2)}, u32[]{:S(2)}) collective-permute-start(bf16[512,768]{1,0:T(8,128)(2,1)S(1)} %shard_map.80.refs_0_), channel_id=1, source_target_pairs={{0,1},{1,0},{2,3},{3,2},{4,5},{5,4},{6,7},{7,6},{8,9},{9,8},{10,11... | collective-permute-start | bytes 2359304 | tf_op jit(solution)/shard_map/ppermute | solution.py:44

commit v5 on v4

--- a/solution.py
+++ b/solution.py
@@ -70,8 +70,8 @@
     return [high, middle, x - high - middle]
 
 
-def extra_kernel(_, *refs):
-    extra_ref, held, done = refs[4], refs[5:9], refs[9]
+def extra_kernel(*refs):
+    extra_ref, held, done = refs[-6], refs[-5:-1], refs[-1]
     copies = [pltpu.make_async_copy(refs[i], held[i], done.at[i]) for i in range(4)]
     for copy in copies:
         copy.start()
@@ -101,21 +101,23 @@
     extra_ref[...] = lines.astype(jnp.bfloat16)
 
 
-def extra_rows(share, flags, *args):
+def extra_rows(share, gates, *args):
     return pl.pallas_call(
         extra_kernel,
-        in_specs=[pl.BlockSpec(memory_space=pltpu.SMEM)]
-        + [pl.BlockSpec(memory_space=pltpu.HBM)] * len(args),
+        in_specs=[pl.BlockSpec(memory_space=pltpu.HBM)] * len(args)
+        + [pl.BlockSpec(memory_space=pl.ANY)] * len(gates),
         out_specs=pl.BlockSpec(memory_space=pltpu.VMEM),
         out_shape=jax.ShapeDtypeStruct((EXTRA, share), jnp.bfloat16),
         scratch_shapes=[pltpu.VMEM(arg.shape, arg.dtype) for arg in args]
         + [pltpu.SemaphoreType.DMA((len(args),))],
         compiler_params=pltpu.CompilerParams(vmem_limit_bytes=4 * MEBI),
-    )(flags, *[pltpu.with_memory_space_constraint(arg, pltpu.HBM) for arg in args])
-
-
-def place_kernel(flags_ref, meta_ref, places_ref, weights_ref, kept_ref):
-    expert, received = flags_ref[0], flags_ref[1].astype(jnp.float32)
+    )(*[pltpu.with_memory_space_constraint(arg, pltpu.HBM) for arg in args], *gates)
+
+
+def place_kernel(meta_ref, places_ref, weights_ref, kept_ref):
+    expert = lax.axis_index("expert")
+    received = lax.axis_index("pipe") < lax.axis_size("pipe") - 1
+    received = received.astype(jnp.float32)
     groups, _, tokens = meta_ref.shape
     micros = meta_ref.shape[1] // 4
     rows = places_ref.shape[1]
@@ -149,13 +151,13 @@
     kept_ref[...] = jnp.zeros_like(kept_ref) + received
 
 
-def find_places(flags, meta, cap):
+def find_places(meta, cap):
     groups, quads, tokens = meta.shape
     micros = quads // 4
     in_vmem = pl.BlockSpec(memory_space=pltpu.VMEM)
     return pl.pallas_call(
         place_kernel,
-        in_specs=[pl.BlockSpec(memory_space=pltpu.SMEM), in_vmem],
+        in_specs=[in_vmem],
         out_specs=[in_vmem] * 3,
         out_shape=[
             jax.ShapeDtypeStruct((micros, cap * groups, groups * tokens), jnp.bfloat16),
@@ -163,31 +165,37 @@
             jax.ShapeDtypeStruct((micros, tokens), jnp.float32),
         ],
         compiler_params=pltpu.CompilerParams(vmem_limit_bytes=16 * MEBI),
-    )(flags, meta)
-
-
-def fill_kernel(cut, count, places_ref, weights_ref, *refs):
-    token_refs, rows_ref = refs[:count], refs[-1]
+    )(meta)
+
+
+def fill(cut, places_ref, weights_ref, sources, spots, rows_ref):
     micros, rows, _ = places_ref.shape
-    tokens = weights_ref.shape[0]
+    tokens, count = weights_ref.shape[0], len(sources[0])
     late = micros * tokens - cut
     for micro in range(micros):
         blocks = []
         for j in range(2 * count):
-            source, top = token_refs[j % count], j // count
+            top = j // count
             low, high = micro * tokens, (micro + 1) * tokens
             pieces = []
             if low < cut:
-                pieces.append(source[top * cut + low : top * cut + min(high, cut), :])
+                source, at = spots[top]
+                pieces.append(sources[source][j % count][at + low : at + min(high, cut), :])
             if high > cut:
-                at = 2 * cut + top * late - cut
-                pieces.append(source[at + max(low, cut) : at + high, :])
+                source, at = spots[2]
+                at += top * late - cut
+                pieces.append(sources[source][j % count][at + max(low, cut) : at + high, :])
             held = pieces[0] if len(pieces) == 1 else jnp.concatenate(pieces, 0)
             weight = weights_ref[:, micro * 2 * count + j : micro * 2 * count + j + 1]
             blocks.append((held.astype(jnp.float32) * weight).astype(jnp.bfloat16))
         rows_ref[micro * rows : (micro + 1) * rows, :] = jnp.dot(
             places_ref[micro], jnp.concatenate(blocks, 0), preferred_element_type=jnp.float32
         ).astype(jnp.bfloat16)
+
+
+def fill_kernel(cut, count, places_ref, weights_ref, *refs):
+    spots = ((0, 0), (0, cut), (0, 2 * cut))
+    fill(cut, places_ref, weights_ref, [refs[:count]], spots, refs[-1])
 
 
 def fill_rows(places, weights, tokens, cut, gates):
@@ -204,8 +212,14 @@
     )(places, weights, *tokens, *gates)
 
 
-def column_copies(weights_hbm, share, held_ref, done):
+def receives():
+    return lax.axis_index("pipe") < lax.axis_size("pipe") - 1
+
+
+def column_copies(weights_hbm, which, held_ref, done):
     hidden, depth = held_ref.shape
+    together = depth * lax.axis_size("dp") // weights_hbm.shape[2]
+    share = (lax.axis_index("dp") // together) ^ which
     block = hidden // done.shape[0]
     columns = pl.ds(pl.multiple_of(share * depth, 128), depth)
     return [
@@ -218,25 +232,28 @@
     ]
 
 
-def fetch_kernel(index, flags_ref, weights_hbm, *refs):
+def fetch_kernel(which, weights_hbm, *refs):
     held_ref, done = refs[-2:]
-    copies = column_copies(weights_hbm, flags_ref[index], held_ref, done)
-    for copy in copies:
-        copy.start()
-    for copy in copies:
-        copy.wait()
-
-
-def fetch(flags, index, weights, depth, gates):
-    return pl.pallas_call(
-        functools.partial(fetch_kernel, index),
-        in_specs=[pl.BlockSpec(memory_space=pltpu.SMEM), pl.BlockSpec(memory_space=pltpu.HBM)]
+
+    @pl.when(receives())
+    def _():
+        copies = column_copies(weights_hbm, which, held_ref, done)
+        for copy in copies:
+            copy.start()
+        for copy in copies:
+            copy.wait()
+
+
+def fetch(which, weights, depth, gates):
+    return pl.pallas_call(
+        functools.partial(fetch_kernel, which),
+        in_specs=[pl.BlockSpec(memory_space=pltpu.HBM)]
         + [pl.BlockSpec(memory_space=pl.ANY)] * len(gates),
         out_specs=pl.BlockSpec(memory_space=pltpu.VMEM),
         out_shape=jax.ShapeDtypeStruct((weights.shape[1], depth), weights.dtype),
         scratch_shapes=[pltpu.SemaphoreType.DMA((COPIES,))],
         compiler_params=pltpu.CompilerParams(vmem_limit_bytes=1 * MEBI),
-    )(flags, pltpu.with_memory_space_constraint(weights, pltpu.HBM), *gates)
+    )(pltpu.with_memory_space_constraint(weights, pltpu.HBM), *gates)
 
 
 def multiply(row_refs, weight_refs, here):
@@ -249,33 +266,35 @@
     return product
 
 
-def first_kernel(block, count, following, flags_ref, weights_hbm, *refs):
+def first_kernel(block, count, following, weights_hbm, *refs):
     row_refs, weight_refs, rest = refs[:count], refs[count : 2 * count], refs[2 * count :]
     total_ref, token_ref, later_refs, done = rest[0], rest[1], rest[2:-1], rest[-1]
-    copies = []
-    for i, later_ref in enumerate(later_refs):
-        copies += column_copies(weights_hbm, flags_ref[following + i], later_ref, done.at[i])
-    for copy in copies:
-        copy.start()
-
-    @pl.loop(0, total_ref.shape[1] // block)
-    def _(step):
-        here = pl.ds(pl.multiple_of(step * block, block), block)
-        total_ref[:, here] = multiply(row_refs, weight_refs, here)
-
-    token_ref[...] = total_ref[:8, :128]
-    for copy in copies:
-        copy.wait()
-
-
-def multiply_first(flags, following, later, rows, held, weights):
+    token_ref[...] = jnp.zeros_like(token_ref)
+
+    @pl.when(receives())
+    def _():
+        copies = []
+        for i, later_ref in enumerate(later_refs):
+            copies += column_copies(weights_hbm, following[i], later_ref, done.at[i])
+        for copy in copies:
+            copy.start()
+
+        @pl.loop(0, total_ref.shape[1] // block)
+        def _(step):
+            here = pl.ds(pl.multiple_of(step * block, block), block)
+            total_ref[:, here] = multiply(row_refs, weight_refs, here)
+
+        for copy in copies:
+            copy.wait()
+
+
+def multiply_first(following, rows, held, weights):
     count, depth = rows[0].shape
-    hidden = weights.shape[1]
+    hidden, later = weights.shape[1], len(following)
     in_vmem = pl.BlockSpec(memory_space=pltpu.VMEM)
     outs = pl.pallas_call(
         functools.partial(first_kernel, min(1024, hidden), len(rows), following),
-        in_specs=[pl.BlockSpec(memory_space=pltpu.SMEM), pl.BlockSpec(memory_space=pltpu.HBM)]
-        + [in_vmem] * (2 * len(rows)),
+        in_specs=[pl.BlockSpec(memory_space=pltpu.HBM)] + [in_vmem] * (2 * len(rows)),
         out_specs=[in_vmem] * (2 + later),
         out_shape=[
             jax.ShapeDtypeStruct((count, hidden), jnp.float32),
@@ -289,63 +308,77 @@
             bytes_accessed=2 * hidden * depth * len(rows),
             transcendentals=0,
         ),
-    )(flags, pltpu.with_memory_space_constraint(weights, pltpu.HBM), *rows, *held)
+    )(pltpu.with_memory_space_constraint(weights, pltpu.HBM), *rows, *held)
     return outs[0], outs[1], outs[2:]
 
 
-def last_kernel(groups, count, *refs):
-    row_refs, weight_refs = refs[:count], refs[count : 2 * count]
-    total_ref, out_ref = refs[2 * count :]
+def last_kernel(groups, cut, each, spots, places_ref, weights_ref, total_ref, *refs):
+    count = len(spots)
+    out_ref, row_refs = refs[-1 - count], refs[-count:]
+    weight_refs, token_refs = refs[:count], refs[count : -1 - count]
+    sources = [token_refs[i : i + each] for i in range(0, len(token_refs), each)]
+
+    @pl.when(jnp.logical_and(pl.program_id(0) == 0, receives()))
+    def _():
+        for i in range(count):
+            fill(cut, places_ref, weights_ref, sources, spots[i], row_refs[i])
+
     micros, cap, block = out_ref.shape[1], out_ref.shape[3], out_ref.shape[5]
     here = pl.ds(pl.multiple_of(pl.program_id(0) * block, block), block)
-    product = multiply(row_refs, weight_refs, here) + total_ref[:, here]
-    rows = cap * groups
-    for micro in range(micros):
-        out_ref[0, micro, 0] = (
-            product[micro * rows : (micro + 1) * rows]
-            .astype(out_ref.dtype)
-            .reshape(cap, groups, block)
-        )
-
-
-def multiply_last(rows, held, total, micros, groups):
+
+    @pl.when(receives())
+    def _():
+        product = multiply(row_refs, weight_refs, here) + total_ref[:, here]
+        rows = cap * groups
+        for micro in range(micros):
+            out_ref[0, micro, 0] = (
+                product[micro * rows : (micro + 1) * rows]
+                .astype(out_ref.dtype)
+                .reshape(cap, groups, block)
+            )
+
+    @pl.when(jnp.logical_not(receives()))
+    def _():
+        out_ref[...] = jnp.zeros_like(out_ref)
+
+
+def multiply_last(places, weights, tokens, spots, held, total, groups, cut):
+    micros = places.shape[0]
     count, hidden = total.shape
-    depth = rows[0].shape[1]
+    depth = held[0].shape[1]
     block = min(1024, hidden)
     cap = count // (micros * groups)
     in_vmem = pl.BlockSpec(memory_space=pltpu.VMEM)
-    return pl.pallas_call(
-        functools.partial(last_kernel, groups, len(rows)),
+    args = [places, weights, total, *held, *[ref for refs in tokens for ref in refs]]
+    return pl.pallas_call(
+        functools.partial(last_kernel, groups, cut, len(tokens[0]), spots),
         grid=(hidden // block,),
-        in_specs=[in_vmem] * (2 * len(rows) + 1),
+        in_specs=[in_vmem] * len(args),
         out_specs=pl.BlockSpec((1, micros, 1, cap, groups, block), lambda f: (0, 0, 0, 0, 0, f)),
         out_shape=jax.ShapeDtypeStruct((1, micros, 1, cap, groups, hidden), jnp.bfloat16),
-        compiler_params=pltpu.CompilerParams(vmem_limit_bytes=16 * MEBI),
+        scratch_shapes=[pltpu.VMEM((count, depth), jnp.bfloat16)] * len(held),
+        compiler_params=pltpu.CompilerParams(vmem_limit_bytes=20 * MEBI),
         cost_estimate=pl.CostEstimate(
-            flops=2 * count * depth * len(rows) * hidden,
-            bytes_accessed=2 * hidden * depth * len(rows),
+            flops=2 * count * depth * len(held) * hidden,
+            bytes_accessed=2 * hidden * depth * len(held),
             transcendentals=0,
         ),
-    )(*rows, *held, total)
+    )(*args)
 
 
 def per_device(out_grad, expert_outputs, logits, routes, down_weights):
     micros, token_count, share = out_grad.shape[1:]
     experts, shares = lax.axis_size("expert"), lax.axis_size("dp")
     cap = min(token_count, 2 * token_count // experts + token_count // 32)
-    expert, mine = lax.axis_index("expert"), lax.axis_index("dp")
+    mine = lax.axis_index("dp")
     sections = lax.axis_size("pipe")
-    received = lax.axis_index("pipe") < sections - 1
     together = 1
     while (share * together) % 128:
         together *= 2
     sets = list(range(shares // together))
     half = len(sets) // 2
-    gated = sets[half:]
     if together == 1:
-        sets, half, gated = [2,0,1,3, *sets[4:]], 2, [1, 3]
-    flags = jnp.stack([expert, received, *[(mine // together) ^ which for which in sets]])
-    flags = flags.astype(jnp.int32)
+        sets = [2, 0, 1, *sets[3:]]
     top = experts // 2
     cut = micros * token_count * 11 // 16
     own = out_grad.reshape(micros * token_count, share)
@@ -356,7 +389,7 @@
 
     extra = extra_rows(
         share,
-        flags,
+        [],
         logits[0].transpose(0, 2, 1),
         routes[0].transpose(0, 2, 1),
         out_grad[0],
@@ -371,12 +404,14 @@
         direct[k] = from_next(join([early, extra], [direct[k - 1]]), k)
         pairs[k] = from_share(join([pair], [pairs[k - 2]]), k, sections - 1)
     near = from_next(join([extra], [direct[shares - 1]]), 2)
-    zero_top = swap(direct[0], top)
-    direct_top = {0: zero_top[:cut]}
+    extras[0] = direct[0][cut:]
+    direct_top = {0: swap(direct[0], top)[:cut]}
+    early_top = swap(join([direct[2], extras[0]]), top)
+    direct_top[2], extra_top = early_top[:cut], early_top[cut:]
     for k in range(shares):
         if k != 2:
             direct[k], extras[k] = direct[k][:cut], direct[k][cut:]
-        if k:
+        if k and k != 2:
             direct_top[k] = swap(direct[k], top)
 
     def spread(x):
@@ -387,7 +422,7 @@
             bit //= 2
         return [held[j] for j in sorted(held)]
 
-    metas = spread(jnp.stack([x[:, :token_count] for x in (extras[0], zero_top[cut:])]))
+    metas = spread(jnp.stack([x[:, :token_count] for x in (extras[0], extra_top)]))
     metas = jnp.concatenate([jnp.stack([m[b] for m in metas]) for b in range(2)], 0)
     metas = metas.astype(jnp.float32).reshape(experts, micros, 8, token_count)
     gap = metas[:, :, 2] + metas[:, :, 3] + metas[:, :, 4]
@@ -402,8 +437,8 @@
         2,
     ).reshape(experts, 4 * micros, token_count)
 
-    places, weights, kept = find_places(flags, meta, cap)
-    def filled(which, gates, fill_gates):
+    places, weights, kept = find_places(meta, cap)
+    def gather(which, gates):
         pieces = []
         for k in range(which * together, (which + 1) * together):
             pieces.append(spread(join([direct[k], direct_top[k], pairs[k]], gates)))
@@ -414,17 +449,20 @@
             for j in range(top):
                 stacked = jnp.take(jnp.stack([piece[j] for piece in pieces]), order, axis=0)
                 tokens.append(stacked.transpose(1, 0, 2).reshape(-1, together * share))
-        return fill_rows(places, weights, tokens, cut, fill_gates)
+        return tokens
 
     fetch_gates = [[pairs[2]], [pairs[2]]]
     held = []
     for i in range(half):
         gates = fetch_gates[i] if i < len(fetch_gates) else []
-        held.append(fetch(flags, 2 + i, down_weights, together * share, gates))
-    rows = [filled(which, [], []) for which in sets[:half]]
-    total, done, held = multiply_first(
-        flags, 2 + half, len(sets) - half, rows, held, down_weights
-    )
+        held.append(fetch(sets[i], down_weights, together * share, gates))
+    gates = []
+    if together == 1:
+        one, three = sets[half:]
+        ahead = spread(join([direct[one], pairs[one], direct[three]]))
+        gates = []
+    rows = [fill_rows(places, weights, gather(which, []), cut, gates) for which in sets[:half]]
+    total, done, held = multiply_first(sets[half:], rows, held, down_weights)
     extras[2] = join([near], [done])
     scores = 0.0
     for k in range(shares):
@@ -433,8 +471,14 @@
     slope = jnp.where(kept > 0, weight_first[0] * weight_second[0] * scores, 0.0)
     moved_logits = jnp.stack([slope, -slope], -1).astype(jnp.bfloat16)[None]
 
-    rows = [filled(which, [done] if which in gated else [], []) for which in sets[half:]]
-    hidden = multiply_last(rows, held, total, micros, experts)
+    if together > 1:
+        tokens = [gather(which, [done]) for which in sets[half:]]
+        spots = [((i, 0), (i, cut), (i, 2 * cut)) for i in range(len(tokens))]
+    else:
+        rest = join([direct_top[one], direct_top[three], pairs[three]], [done])
+        tokens, both = [ahead, spread(rest)], 2 * (micros * token_count - cut)
+        spots = [((0, 0), (1, 0), (0, cut)), ((0, cut + both), (1, cut), (1, 2 * cut))]
+    hidden = multiply_last(places, weights, tokens, spots, held, total, experts, cut)
     return hidden.transpose(0, 1, 2, 4, 3, 5), moved_logits
 
 

time: 69 us -> 68.2 us (0.988)
  Pallas kernels: 30.4 us -> 27.5 us
  starting transfers between devices: 22.7 us -> 24.8 us
    ppermute x6, starting transfers between devices: 7.82 us -> 11.9 us  [from_next(): return lax.ppermute(x, ('pipe', 'dp'), pairs)]
    ppermute x10, starting transfers between devices: 12.3 us -> 10.3 us  [swap(): return lax.ppermute(x, 'expert', [(e, e ^ bit) for e in range(experts)])]
    pallas_call x4 -> x2, Pallas kernels: 2.86 us -> 1.44 us  [fill_rows(): pl.pallas_call(functools.partial(fill_kernel, cut, len(tokens)), in_specs...]
    ppermute x10, waiting for transfers between devices: 5.41 us -> 6.47 us  [swap(): return lax.ppermute(x, 'expert', [(e, e ^ bit) for e in range(experts)])]
    ppermute x6, waiting for transfers between devices: 6.42 us -> 5.46 us  [from_next(): return lax.ppermute(x, ('pipe', 'dp'), pairs)]
    pallas_call x5, Pallas kernels: 18.8 us -> 17.9 us  [the longest x1 10.1 us: multiply_last(): pl.pallas_call(functools.partial(last_kernel, groups, cut, len(tokens[0])...]
  transfers between devices with their start and end apart: 19 -> 19, of which waited for: 8 -> 7; matrix products, arithmetic and copies ran while one was open for 3% -> 3% of each run, Pallas kernels for 30% -> 26%
where the time goes in v5:
time: 68.2 us; the launch traced here: 68 us
  Pallas kernels  27.5 us (40%)
  starting transfers between devices  24.8 us (36%)
  waiting for transfers between devices  11.9 us (17%)
  local copies, waits for them, and re-layouts  2.61 us (4%)
  between operations  1.01 us (1%)
    ppermute x6, starting transfers between devices, from_next(): return lax.ppermute(x, ('pipe', 'dp'), pairs)  11.9 us
    ppermute x10, starting transfers between devices, swap(): return lax.ppermute(x, 'expert', [(e, e ^ bit) for e in range(experts)])  10.3 us
    pallas_call x1, Pallas kernels, multiply_last(): pl.pallas_call(functools.partial(last_kernel, groups, cut, len(tokens[0])...  10.1 us
    pallas_call x1, Pallas kernels, multiply_first(): pl.pallas_call(functools.partial(first_kernel, min(1024, hidden), len(row...  7.83 us
    ppermute x10, waiting for transfers between devices, swap(): return lax.ppermute(x, 'expert', [(e, e ^ bit) for e in range(experts)])  6.47 us
    pallas_call x2, Pallas kernels, fetch(): pl.pallas_call(functools.partial(fetch_kernel, which), in_specs=[pl.Block...  5.81 us
    ppermute x6, waiting for transfers between devices, from_next(): return lax.ppermute(x, ('pipe', 'dp'), pairs)  5.46 us
    ppermute x3, starting transfers between devices, from_share(): return lax.ppermute(x, ('pipe', 'dp', 'expert'), pairs)  2.61 us
  transfers between devices with their start and end apart: 19, of which 7 were waited for; matrix products, arithmetic and copies ran while one was open for 3% of the time, Pallas kernels for 26%

profile of v5, /device:TPU:9, one launch (start us, length us, event | category | flops | bytes accessed | tf_op | source)
XLA Modules:
  0.0 68.0 jit_solution(5091723862506913259)
XLA Ops:
  0.6 0.9 %slice.146 = bf16[80,768]{1,0:T(8,128)(2,1)S(1)} slice(bf16[256,768]{1,0:T(8,128)(2,1)} %bitcast.69), slice={[176:256], [0:768]} | slice | bytes 245760 | tf_op jit(solution)/shard_map/slice | solution.py:385
  1.5 1.3 %collective-permute-start = (bf16[80,768]{1,0:T(8,128)(2,1)S(1)}, bf16[80,768]{1,0:T(8,128)(2,1)S(1)}, u32[]{:S(2)}, u32[]{:S(2)}) collective-permute-start(bf16[80,768]{1,0:T(8,128)(2,1)S(1)} %slice.146), channel_id=1, source_target_pairs={{0,16},{4,20},{8,24},{12,28},{16,0},{20,4},{24,8},{28,12},{1,17},{... | collective-permute-start | bytes 368648 | tf_op jit(solution)/shard_map/ppermute | solution.py:25
  2.8 1.0 %slice.145.refs_0_ = bf16[176,768]{1,0:T(8,128)(2,1)S(1)} slice(bf16[256,768]{1,0:T(8,128)(2,1)} %bitcast.70), slice={[0:176], [0:768]} | slice | bytes 540672 | tf_op jit(solution)/shard_map/slice | solution.py:385
  3.8 1.7 %shard_map.68.refs_1_.refs_0_ = bf16[16,768]{1,0:T(8,128)(2,1)S(1)} custom-call(f32[2,2,128]{2,1,0:T(2,128)} %bitcast.85, s32[2,2,128]{2,1,0:T(2,128)} %bitcast.86, bf16[2,128,768]{2,1,0:T(8,128)(2,1)} %bitcast.71, bf16[2,128,2,768]{3,2,1,0:T(2,128)(2,1)} %bitcast.72), custom_call_target="tpu_custom_call" | custom-call | tf_op jit(solution)/shard_map/pallas_call | solution.py:105
  5.5 0.3 collective-permute-done.refs_2_.refs_0_
  5.8 1.3 %collective-permute-start.1 = (bf16[192,768]{1,0:T(8,128)(2,1)S(1)}, bf16[192,768]{1,0:T(8,128)(2,1)S(1)}, u32[]{:S(2)}, u32[]{:S(2)}) collective-permute-start(bf16[192,768]{1,0:T(8,128)(2,1)S(1)} %shard_map.69), channel_id=1, source_target_pairs={{0,16},{4,20},{8,24},{12,28},{16,0},{20,4},{24,8},{28,12},{1,17},{... | collective-permute-start | bytes 884744 | tf_op jit(solution)/shard_map/ppermute | solution.py:25
  7.1 0.3 collective-permute-start.2
  7.3 1.2 %collective-permute-start.5 = (bf16[80,768]{1,0:T(8,128)(2,1)S(1)}, bf16[80,768]{1,0:T(8,128)(2,1)S(1)}, u32[]{:S(2)}, u32[]{:S(2)}) collective-permute-start(bf16[80,768]{1,0:T(8,128)(2,1)S(1)} %collective-permute-done.refs_2_.refs_0_), channel_id=1, source_target_pairs={{0,2},{1,3},{2,0},{3,1},{4,6},{5,7},{6,4},{7,5},{8,10},{9,11},{10,... | collective-permute-start | bytes 368648 | tf_op jit(solution)/shard_map/ppermute | solution.py:44
  8.6 2.8 %collective-permute-done.5.refs_1_ = bf16[80,768]{1,0:T(8,128)(2,1)S(1)} collective-permute-done((bf16[80,768]{1,0:T(8,128)(2,1)S(1)}, bf16[80,768]{1,0:T(8,128)(2,1)S(1)}, u32[]{:S(2)}, u32[]{:S(2)}) %collective-permute-start.5) | collective-permute-done | bytes 122912 | tf_op jit(solution)/shard_map/ppermute | solution.py:44
  11.4 2.4 %collective-permute-start.6 = (bf16[160,768]{1,0:T(8,128)(2,1)S(1)}, bf16[160,768]{1,0:T(8,128)(2,1)S(1)}, u32[]{:S(2)}, u32[]{:S(2)}) collective-permute-start(bf16[160,768]{1,0:T(8,128)(2,1)S(1)} %shard_map.72.refs_2_.refs_0_), channel_id=1, source_target_pairs={{0,8},{1,9},{2,10},{3,11},{4,12},{5,13},{6,14},{7,15},{8,0},{9,1},... | collective-permute-start | bytes 737288 | tf_op jit(solution)/shard_map/ppermute | solution.py:39
  13.9 3.7 %collective-permute-done.2.refs_0_.refs_2_ = bf16[176,768]{1,0:T(8,128)(2,1)S(1)} collective-permute-done((bf16[176,768]{1,0:T(8,128)(2,1)S(1)}, bf16[176,768]{1,0:T(8,128)(2,1)S(1)}, u32[]{:S(2)}, u32[]{:S(2)}) %collective-permute-start.2) | collective-permute-done | bytes 270368 | tf_op jit(solution)/shard_map/ppermute | solution.py:25
  17.7 4.9 %collective-permute-start.12 = (bf16[192,768]{1,0:T(8,128)(2,1)S(1)}, bf16[192,768]{1,0:T(8,128)(2,1)S(1)}, u32[]{:S(2)}, u32[]{:S(2)}) collective-permute-start(bf16[192,768]{1,0:T(8,128)(2,1)S(1)} %shard_map.81), channel_id=1, source_target_pairs={{0,16},{4,20},{8,24},{12,28},{16,12},{20,8},{24,4},{28,0},{1,17},{... | collective-permute-start | bytes 884744 | tf_op jit(solution)/shard_map/ppermute | solution.py:25
  22.6 1.3 %collective-permute-start.3 = (bf16[192,768]{1,0:T(8,128)(2,1)S(1)}, bf16[192,768]{1,0:T(8,128)(2,1)S(1)}, u32[]{:S(2)}, u32[]{:S(2)}) collective-permute-start(bf16[192,768]{1,0:T(8,128)(2,1)S(1)} %shard_map.70), channel_id=1, source_target_pairs={{0,2},{1,3},{2,0},{3,1},{4,6},{5,7},{6,4},{7,5},{8,10},{9,11},{10,... | collective-permute-start | bytes 884744 | tf_op jit(solution)/shard_map/ppermute | solution.py:44
  24.1 0.3 collective-permute-start.8
  24.5 2.9 %shard_map.77.refs_2_ = bf16[4096,768]{1,0:T(8,128)(2,1)S(1)} custom-call(bf16[1,4096,3072]{2,1,0:T(8,128)(2,1)} %weights_hbm.5, bf16[160,768]{1,0:T(8,128)(2,1)S(1)} %collective-permute-done.6.refs_2_.refs_0_), custom_call_target="tpu_custom_call" | custom-call | tf_op jit(solution)/shard_map/pallas_call | solution.py:248
  27.4 2.9 %shard_map.78.refs_3_ = bf16[4096,768]{1,0:T(8,128)(2,1)S(1)} custom-call(bf16[1,4096,3072]{2,1,0:T(8,128)(2,1)} %weights_hbm.5, bf16[160,768]{1,0:T(8,128)(2,1)S(1)} %collective-permute-done.6.refs_2_.refs_0_), custom_call_target="tpu_custom_call" | custom-call | tf_op jit(solution)/shard_map/pallas_call | solution.py:248
  30.3 4.1 %collective-permute-start.18 = (bf16[16,768]{1,0:T(8,128)(2,1)S(1)}, bf16[16,768]{1,0:T(8,128)(2,1)S(1)}, u32[]{:S(2)}, u32[]{:S(2)}) collective-permute-start(bf16[16,768]{1,0:T(8,128)(2,1)S(1)} %shard_map.86), channel_id=1, source_target_pairs={{0,16},{4,20},{8,24},{12,28},{16,8},{20,12},{24,0},{28,4},{1,17},{... | collective-permute-start | bytes 73736 | tf_op jit(solution)/shard_map/ppermute | solution.py:25
  34.4 1.3 %collective-permute-start.15 = (bf16[176,768]{1,0:T(8,128)(2,1)S(1)}, bf16[176,768]{1,0:T(8,128)(2,1)S(1)}, u32[]{:S(2)}, u32[]{:S(2)}) collective-permute-start(bf16[176,768]{1,0:T(8,128)(2,1)S(1)} %slice.157.refs_2_), channel_id=1, source_target_pairs={{0,2},{1,3},{2,0},{3,1},{4,6},{5,7},{6,4},{7,5},{8,10},{9,11},{10,... | collective-permute-start | bytes 811016 | tf_op jit(solution)/shard_map/ppermute | solution.py:44
  35.8 1.0 %collective-permute-done.8 = bf16[192,768]{1,0:T(8,128)(2,1)S(1)} collective-permute-done((bf16[192,768]{1,0:T(8,128)(2,1)S(1)}, bf16[192,768]{1,0:T(8,128)(2,1)S(1)}, u32[]{:S(2)}, u32[]{:S(2)}) %collective-permute-start.8) | collective-permute-done | bytes 294944 | tf_op jit(solution)/shard_map/ppermute | solution.py:44
  36.7 2.4 %collective-permute-start.4 = (bf16[2,16,128]{2,1,0:T(8,128)(2,1)S(1)}, bf16[2,16,128]{2,1,0:T(8,128)(2,1)S(1)}, u32[]{:S(2)}, u32[]{:S(2)}) collective-permute-start(bf16[2,16,128]{2,1,0:T(8,128)(2,1)S(1)} %pad_maximum_fusion.1), channel_id=1, source_target_pairs={{0,1},{1,0},{2,3},{3,2},{4,5},{5,4},{6,7},{7,6},{8,9},{9,8},{10,11... | collective-permute-start | bytes 24584 | tf_op jit(solution)/shard_map/ppermute | solution.py:44
  39.2 1.5 %collective-permute-done.10 = bf16[192,768]{1,0:T(8,128)(2,1)S(1)} collective-permute-done((bf16[192,768]{1,0:T(8,128)(2,1)S(1)}, bf16[192,768]{1,0:T(8,128)(2,1)S(1)}, u32[]{:S(2)}, u32[]{:S(2)}) %collective-permute-start.10) | collective-permute-done | bytes 294944 | tf_op jit(solution)/shard_map/ppermute | solution.py:25
  40.6 1.7 %collective-permute-start.9 = (bf16[512,768]{1,0:T(8,128)(2,1)S(1)}, bf16[512,768]{1,0:T(8,128)(2,1)S(1)}, u32[]{:S(2)}, u32[]{:S(2)}) collective-permute-start(bf16[512,768]{1,0:T(8,128)(2,1)S(1)} %shard_map.75.refs_0_), channel_id=1, source_target_pairs={{0,1},{1,0},{2,3},{3,2},{4,5},{5,4},{6,7},{7,6},{8,9},{9,8},{10,11... | collective-permute-start | bytes 2359304 | tf_op jit(solution)/shard_map/ppermute | solution.py:44
  42.7 0.3 shard_map.71
  43.1 1.1 %collective-permute-done.9.refs_1_ = bf16[512,768]{1,0:T(8,128)(2,1)S(1)} collective-permute-done((bf16[512,768]{1,0:T(8,128)(2,1)S(1)}, bf16[512,768]{1,0:T(8,128)(2,1)S(1)}, u32[]{:S(2)}, u32[]{:S(2)}) %collective-permute-start.9) | collective-permute-done | bytes 786464 | tf_op jit(solution)/shard_map/ppermute | solution.py:44
  44.2 1.2 %collective-permute-start.14 = (bf16[176,768]{1,0:T(8,128)(2,1)S(1)}, bf16[176,768]{1,0:T(8,128)(2,1)S(1)}, u32[]{:S(2)}, u32[]{:S(2)}) collective-permute-start(bf16[176,768]{1,0:T(8,128)(2,1)S(1)} %slice.156.refs_0_), channel_id=1, source_target_pairs={{0,2},{1,3},{2,0},{3,1},{4,6},{5,7},{6,4},{7,5},{8,10},{9,11},{10,... | collective-permute-start | bytes 811016 | tf_op jit(solution)/shard_map/ppermute | solution.py:44
  45.4 0.7 %shard_map.76.refs_1_ = bf16[544,768]{1,0:T(8,128)(2,1)S(1)} custom-call(bf16[2,272,512]{2,1,0:T(8,128)(2,1)S(1)} %get-tuple-element.9.places_ref, f32[128,128]{1,0:T(8,128)S(1)} %get-tuple-element.10.weights_ref, bf16[512,768]{1,0:T(8,128)(2,1)S(1)} %shard_map.75.refs_0_, bf16[512,768]{1,0:T(8,128)(2,1)S(1)} %collective-permute-done.9.refs_1_), custom_call_target="tpu_custom_call" | custom-call | tf_op jit(solution)/shard_map/pallas_call | solution.py:205
  46.2 0.7 %collective-permute-start.13 = (bf16[512,768]{1,0:T(8,128)(2,1)S(1)}, bf16[512,768]{1,0:T(8,128)(2,1)S(1)}, u32[]{:S(2)}, u32[]{:S(2)}) collective-permute-start(bf16[512,768]{1,0:T(8,128)(2,1)S(1)} %shard_map.82.refs_2_), channel_id=1, source_target_pairs={{0,1},{1,0},{2,3},{3,2},{4,5},{5,4},{6,7},{7,6},{8,9},{9,8},{10,11... | collective-permute-start | bytes 2359304 | tf_op jit(solution)/shard_map/ppermute | solution.py:44
  46.9 0.7 %shard_map.74.refs_0_ = bf16[544,768]{1,0:T(8,128)(2,1)S(1)} custom-call(bf16[2,272,512]{2,1,0:T(8,128)(2,1)S(1)} %get-tuple-element.9.places_ref, f32[128,128]{1,0:T(8,128)S(1)} %get-tuple-element.10.weights_ref, bf16[512,768]{1,0:T(8,128)(2,1)S(1)} %shard_map.73.refs_0_, bf16[512,768]{1,0:T(8,128)(2,1)S(1)} %collective-permute-done.7.refs_1_), custom_call_target="tpu_custom_call" | custom-call | tf_op jit(solution)/shard_map/pallas_call | solution.py:205
  47.6 7.8 %shard_map.79 = (f32[544,4096]{1,0:T(8,128)S(1)}, f32[8,128]{1,0:T(8,128)S(1)}, bf16[4096,768]{1,0:T(8,128)(2,1)S(1)}, bf16[4096,768]{1,0:T(8,128)(2,1)S(1)}) custom-call(bf16[1,4096,3072]{2,1,0:T(8,128)(2,1)} %weights_hbm.5, bf16[544,768]{1,0:T(8,128)(2,1)S(1)} %shard_map.74.refs_0_, bf16[544,768]{1,0:T(8,128)(2,1)S(1)} %shard_map.76.refs_1_, ...), custom_call_target="tpu_custom_call" | custom-call | flops 6845104128 | bytes 12582912 | tf_op jit(solution)/shard_map/pallas_call | solution.py:295
  55.7 0.6 copy.24
  56.3 1.6 %collective-permute-done.17.refs_5_ = bf16[512,768]{1,0:T(8,128)(2,1)S(1)} collective-permute-done((bf16[512,768]{1,0:T(8,128)(2,1)S(1)}, bf16[512,768]{1,0:T(8,128)(2,1)S(1)}, u32[]{:S(2)}, u32[]{:S(2)}) %collective-permute-start.17) | collective-permute-done | bytes 786464 | tf_op jit(solution)/shard_map/ppermute | solution.py:44
  57.9 10.1 %shard_map.85 = bf16[1,2,1,68,4,4096]{5,4,3,2,1,0:T(4,128)(2,1)} custom-call(bf16[2,272,512]{2,1,0:T(8,128)(2,1)S(1)} %get-tuple-element.9.places_ref, f32[128,128]{1,0:T(8,128)S(1)} %get-tuple-element.10.weights_ref, f32[544,4096]{1,0:T(8,128)S(1)} %get-tuple-element.11.total_ref, bf16[4096,768]{1,0:T(8,128)(2,1)S(1)} %get-tuple-element.12.refs_0_, ...), custom_call_target="tpu_custom_call" | custom-call | flops 6845104128 | bytes 12582912 | tf_op jit(solution)/shard_map/pallas_call | solution.py:353
  (59 shorter events, 1.1 us)
Async XLA Ops:
  1.5 4.3 %collective-permute-start = (bf16[80,768]{1,0:T(8,128)(2,1)S(1)}, bf16[80,768]{1,0:T(8,128)(2,1)S(1)}, u32[]{:S(2)}, u32[]{:S(2)}) collective-permute-start(bf16[80,768]{1,0:T(8,128)(2,1)S(1)} %slice.146), channel_id=1, source_target_pairs={{0,16},{4,20},{8,24},{12,28},{16,0},{20,4},{24,8},{28,12},{1,17},{... | collective-permute-start | bytes 368648 | tf_op jit(solution)/shard_map/ppermute | solution.py:25
  5.8 16.7 %collective-permute-start.1 = (bf16[192,768]{1,0:T(8,128)(2,1)S(1)}, bf16[192,768]{1,0:T(8,128)(2,1)S(1)}, u32[]{:S(2)}, u32[]{:S(2)}) collective-permute-start(bf16[192,768]{1,0:T(8,128)(2,1)S(1)} %shard_map.69), channel_id=1, source_target_pairs={{0,16},{4,20},{8,24},{12,28},{16,0},{20,4},{24,8},{28,12},{1,17},{... | collective-permute-start | bytes 884744 | tf_op jit(solution)/shard_map/ppermute | solution.py:25
  7.1 10.5 %collective-permute-start.2 = (bf16[176,768]{1,0:T(8,128)(2,1)S(1)}, bf16[176,768]{1,0:T(8,128)(2,1)S(1)}, u32[]{:S(2)}, u32[]{:S(2)}) collective-permute-start(bf16[176,768]{1,0:T(8,128)(2,1)S(1)} %slice.145.refs_0_), channel_id=1, source_target_pairs={{0,16},{4,20},{8,24},{12,28},{16,8},{20,12},{24,0},{28,4},{1,17},{... | collective-permute-start | bytes 811016 | tf_op jit(solution)/shard_map/ppermute | solution.py:25
  7.3 4.0 %collective-permute-start.5 = (bf16[80,768]{1,0:T(8,128)(2,1)S(1)}, bf16[80,768]{1,0:T(8,128)(2,1)S(1)}, u32[]{:S(2)}, u32[]{:S(2)}) collective-permute-start(bf16[80,768]{1,0:T(8,128)(2,1)S(1)} %collective-permute-done.refs_2_.refs_0_), channel_id=1, source_target_pairs={{0,2},{1,3},{2,0},{3,1},{4,6},{5,7},{6,4},{7,5},{8,10},{9,11},{10,... | collective-permute-start | bytes 368648 | tf_op jit(solution)/shard_map/ppermute | solution.py:44
  11.4 13.0 %collective-permute-start.6 = (bf16[160,768]{1,0:T(8,128)(2,1)S(1)}, bf16[160,768]{1,0:T(8,128)(2,1)S(1)}, u32[]{:S(2)}, u32[]{:S(2)}) collective-permute-start(bf16[160,768]{1,0:T(8,128)(2,1)S(1)} %shard_map.72.refs_2_.refs_0_), channel_id=1, source_target_pairs={{0,8},{1,9},{2,10},{3,11},{4,12},{5,13},{6,14},{7,15},{8,0},{9,1},... | collective-permute-start | bytes 737288 | tf_op jit(solution)/shard_map/ppermute | solution.py:39
  13.8 10.3 %collective-permute-start.11 = (bf16[160,768]{1,0:T(8,128)(2,1)S(1)}, bf16[160,768]{1,0:T(8,128)(2,1)S(1)}, u32[]{:S(2)}, u32[]{:S(2)}) collective-permute-start(bf16[160,768]{1,0:T(8,128)(2,1)S(1)} %shard_map.72.refs_2_.refs_0_), channel_id=1, source_target_pairs={{0,4},{1,5},{2,6},{3,7},{4,0},{5,1},{6,2},{7,3},{8,12},{9,13},{10,... | collective-permute-start | bytes 737288 | tf_op jit(solution)/shard_map/ppermute | solution.py:39
  17.7 12.6 %collective-permute-start.12 = (bf16[192,768]{1,0:T(8,128)(2,1)S(1)}, bf16[192,768]{1,0:T(8,128)(2,1)S(1)}, u32[]{:S(2)}, u32[]{:S(2)}) collective-permute-start(bf16[192,768]{1,0:T(8,128)(2,1)S(1)} %shard_map.81), channel_id=1, source_target_pairs={{0,16},{4,20},{8,24},{12,28},{16,12},{20,8},{24,4},{28,0},{1,17},{... | collective-permute-start | bytes 884744 | tf_op jit(solution)/shard_map/ppermute | solution.py:25
  22.6 11.9 %collective-permute-start.3 = (bf16[192,768]{1,0:T(8,128)(2,1)S(1)}, bf16[192,768]{1,0:T(8,128)(2,1)S(1)}, u32[]{:S(2)}, u32[]{:S(2)}) collective-permute-start(bf16[192,768]{1,0:T(8,128)(2,1)S(1)} %shard_map.70), channel_id=1, source_target_pairs={{0,2},{1,3},{2,0},{3,1},{4,6},{5,7},{6,4},{7,5},{8,10},{9,11},{10,... | collective-permute-start | bytes 884744 | tf_op jit(solution)/shard_map/ppermute | solution.py:44
  23.9 16.7 %collective-permute-start.10 = (bf16[192,768]{1,0:T(8,128)(2,1)S(1)}, bf16[192,768]{1,0:T(8,128)(2,1)S(1)}, u32[]{:S(2)}, u32[]{:S(2)}) collective-permute-start(bf16[192,768]{1,0:T(8,128)(2,1)S(1)} %shard_map.80), channel_id=1, source_target_pairs={{0,16},{4,20},{8,24},{12,28},{16,4},{20,0},{24,12},{28,8},{1,17},{... | collective-permute-start | bytes 884744 | tf_op jit(solution)/shard_map/ppermute | solution.py:25
  24.1 12.7 %collective-permute-start.8 = (bf16[192,768]{1,0:T(8,128)(2,1)S(1)}, bf16[192,768]{1,0:T(8,128)(2,1)S(1)}, u32[]{:S(2)}, u32[]{:S(2)}) collective-permute-start(bf16[192,768]{1,0:T(8,128)(2,1)S(1)} %collective-permute-done.1.refs_2_), channel_id=1, source_target_pairs={{0,2},{1,3},{2,0},{3,1},{4,6},{5,7},{6,4},{7,5},{8,10},{9,11},{10,... | collective-permute-start | bytes 884744 | tf_op jit(solution)/shard_map/ppermute | solution.py:44
  24.4 31.1 %collective-permute-start.16 = (bf16[160,768]{1,0:T(8,128)(2,1)S(1)}, bf16[160,768]{1,0:T(8,128)(2,1)S(1)}, u32[]{:S(2)}, u32[]{:S(2)}) collective-permute-start(bf16[160,768]{1,0:T(8,128)(2,1)S(1)} %shard_map.83), channel_id=1, source_target_pairs={{0,12},{1,13},{2,14},{3,15},{4,8},{5,9},{6,10},{7,11},{8,4},{9,5},... | collective-permute-start | bytes 737288 | tf_op jit(solution)/shard_map/ppermute | solution.py:39
  30.3 25.3 %collective-permute-start.18 = (bf16[16,768]{1,0:T(8,128)(2,1)S(1)}, bf16[16,768]{1,0:T(8,128)(2,1)S(1)}, u32[]{:S(2)}, u32[]{:S(2)}) collective-permute-start(bf16[16,768]{1,0:T(8,128)(2,1)S(1)} %shard_map.86), channel_id=1, source_target_pairs={{0,16},{4,20},{8,24},{12,28},{16,8},{20,12},{24,0},{28,4},{1,17},{... | collective-permute-start | bytes 73736 | tf_op jit(solution)/shard_map/ppermute | solution.py:25
  34.4 21.0 %collective-permute-start.15 = (bf16[176,768]{1,0:T(8,128)(2,1)S(1)}, bf16[176,768]{1,0:T(8,128)(2,1)S(1)}, u32[]{:S(2)}, u32[]{:S(2)}) collective-permute-start(bf16[176,768]{1,0:T(8,128)(2,1)S(1)} %slice.157.refs_2_), channel_id=1, source_target_pairs={{0,2},{1,3},{2,0},{3,1},{4,6},{5,7},{6,4},{7,5},{8,10},{9,11},{10,... | collective-permute-start | bytes 811016 | tf_op jit(solution)/shard_map/ppermute | solution.py:44
  36.7 5.8 %collective-permute-start.4 = (bf16[2,16,128]{2,1,0:T(8,128)(2,1)S(1)}, bf16[2,16,128]{2,1,0:T(8,128)(2,1)S(1)}, u32[]{:S(2)}, u32[]{:S(2)}) collective-permute-start(bf16[2,16,128]{2,1,0:T(8,128)(2,1)S(1)} %pad_maximum_fusion.1), channel_id=1, source_target_pairs={{0,1},{1,0},{2,3},{3,2},{4,5},{5,4},{6,7},{7,6},{8,9},{9,8},{10,11... | collective-permute-start | bytes 24584 | tf_op jit(solution)/shard_map/ppermute | solution.py:44
  40.6 3.6 %collective-permute-start.9 = (bf16[512,768]{1,0:T(8,128)(2,1)S(1)}, bf16[512,768]{1,0:T(8,128)(2,1)S(1)}, u32[]{:S(2)}, u32[]{:S(2)}) collective-permute-start(bf16[512,768]{1,0:T(8,128)(2,1)S(1)} %shard_map.75.refs_0_), channel_id=1, source_target_pairs={{0,1},{1,0},{2,3},{3,2},{4,5},{5,4},{6,7},{7,6},{8,9},{9,8},{10,11... | collective-permute-start | bytes 2359304 | tf_op jit(solution)/shard_map/ppermute | solution.py:44
  42.5 3.7 %collective-permute-start.7 = (bf16[512,768]{1,0:T(8,128)(2,1)S(1)}, bf16[512,768]{1,0:T(8,128)(2,1)S(1)}, u32[]{:S(2)}, u32[]{:S(2)}) collective-permute-start(bf16[512,768]{1,0:T(8,128)(2,1)S(1)} %shard_map.73.refs_0_), channel_id=1, source_target_pairs={{0,1},{1,0},{2,3},{3,2},{4,5},{5,4},{6,7},{7,6},{8,9},{9,8},{10,11... | collective-permute-start | bytes 2359304 | tf_op jit(solution)/shard_map/ppermute | solution.py:44
  44.2 11.3 %collective-permute-start.14 = (bf16[176,768]{1,0:T(8,128)(2,1)S(1)}, bf16[176,768]{1,0:T(8,128)(2,1)S(1)}, u32[]{:S(2)}, u32[]{:S(2)}) collective-permute-start(bf16[176,768]{1,0:T(8,128)(2,1)S(1)} %slice.156.refs_0_), channel_id=1, source_target_pairs={{0,2},{1,3},{2,0},{3,1},{4,6},{5,7},{6,4},{7,5},{8,10},{9,11},{10,... | collective-permute-start | bytes 811016 | tf_op jit(solution)/shard_map/ppermute | solution.py:44
  46.2 10.1 %collective-permute-start.13 = (bf16[512,768]{1,0:T(8,128)(2,1)S(1)}, bf16[512,768]{1,0:T(8,128)(2,1)S(1)}, u32[]{:S(2)}, u32[]{:S(2)}) collective-permute-start(bf16[512,768]{1,0:T(8,128)(2,1)S(1)} %shard_map.82.refs_2_), channel_id=1, source_target_pairs={{0,1},{1,0},{2,3},{3,2},{4,5},{5,4},{6,7},{7,6},{8,9},{9,8},{10,11... | collective-permute-start | bytes 2359304 | tf_op jit(solution)/shard_map/ppermute | solution.py:44
  55.6 2.4 %collective-permute-start.17 = (bf16[512,768]{1,0:T(8,128)(2,1)S(1)}, bf16[512,768]{1,0:T(8,128)(2,1)S(1)}, u32[]{:S(2)}, u32[]{:S(2)}) collective-permute-start(bf16[512,768]{1,0:T(8,128)(2,1)S(1)} %shard_map.84.refs_4_), channel_id=1, source_target_pairs={{0,1},{1,0},{2,3},{3,2},{4,5},{5,4},{6,7},{7,6},{8,9},{9,8},{10,11... | collective-permute-start | bytes 2359304 | tf_op jit(solution)/shard_map/ppermute | solution.py:44

commit v6 on v5

--- a/solution.py
+++ b/solution.py
@@ -303,11 +303,7 @@
         + [jax.ShapeDtypeStruct((hidden, depth), weights.dtype)] * later,
         scratch_shapes=[pltpu.SemaphoreType.DMA((later, COPIES))],
         compiler_params=pltpu.CompilerParams(vmem_limit_bytes=12 * MEBI),
-        cost_estimate=pl.CostEstimate(
-            flops=2 * count * depth * len(rows) * hidden,
-            bytes_accessed=2 * hidden * depth * len(rows),
-            transcendentals=0,
-        ),
+        cost_estimate=pl.CostEstimate(flops=1, bytes_accessed=1, transcendentals=0),
     )(pltpu.with_memory_space_constraint(weights, pltpu.HBM), *rows, *held)
     return outs[0], outs[1], outs[2:]
 
@@ -403,15 +399,17 @@
     for k in range(3, shares):
         direct[k] = from_next(join([early, extra], [direct[k - 1]]), k)
         pairs[k] = from_share(join([pair], [pairs[k - 2]]), k, sections - 1)
-    near = from_next(join([extra], [direct[shares - 1]]), 2)
+    pairs_near = [
+        (s * shares + z, (s - 1) * shares + (z ^ 2)) for s in range(1, sections) for z in range(shares)
+    ]
+    near = lax.ppermute(join([extra], [direct[0]]), ("pipe", "dp"), pairs_near)
     extras[0] = direct[0][cut:]
     direct_top = {0: swap(direct[0], top)[:cut]}
     early_top = swap(join([direct[2], extras[0]]), top)
     direct_top[2], extra_top = early_top[:cut], early_top[cut:]
-    for k in range(shares):
-        if k != 2:
-            direct[k], extras[k] = direct[k][:cut], direct[k][cut:]
-        if k and k != 2:
+    for k in (0, *range(3, shares)):
+        direct[k], extras[k] = direct[k][:cut], direct[k][cut:]
+        if k:
             direct_top[k] = swap(direct[k], top)
 
     def spread(x):
@@ -438,6 +436,10 @@
     ).reshape(experts, 4 * micros, token_count)
 
     places, weights, kept = find_places(meta, cap)
+    last = join([direct[1]], [places])
+    direct[1], extras[1] = last[:cut], last[cut:]
+    direct_top[1] = swap(direct[1], top)
+
     def gather(which, gates):
         pieces = []
         for k in range(which * together, (which + 1) * together):

time: 68.2 us -> 66.9 us (0.981)
  waiting for transfers between devices: 11.9 us -> 9.85 us
  starting transfers between devices: 24.8 us -> 25.5 us
    ppermute x6 -> x5, starting transfers between devices: 11.9 us -> 7.77 us  [from_next(): return lax.ppermute(x, ('pipe', 'dp'), pairs)]
    ppermute x10, starting transfers between devices: 10.3 us -> 13.9 us  [swap(): return lax.ppermute(x, 'expert', [(e, e ^ bit) for e in range(experts)])]
    ppermute x10, waiting for transfers between devices: 6.47 us -> 4.65 us  [swap(): return lax.ppermute(x, 'expert', [(e, e ^ bit) for e in range(experts)])]
    ppermute x0 -> x1, starting transfers between devices: none -> 1.28 us  [per_device(): near = lax.ppermute(join([extra], [direct[0]]), ('pipe', 'dp'), pairs_near)]
    ppermute x6 -> x5, waiting for transfers between devices: 5.46 us -> 5.19 us  [from_next(): return lax.ppermute(x, ('pipe', 'dp'), pairs)]
where the time goes in v6:
time: 66.9 us; the launch traced here: 66.6 us
  Pallas kernels  27.6 us (41%)
  starting transfers between devices  25.5 us (38%)
  waiting for transfers between devices  9.85 us (15%)
  local copies, waits for them, and re-layouts  2.6 us (4%)
  between operations  0.99 us (1%)
    ppermute x10, starting transfers between devices, swap(): return lax.ppermute(x, 'expert', [(e, e ^ bit) for e in range(experts)])  13.9 us
    pallas_call x1, Pallas kernels, multiply_last(): pl.pallas_call(functools.partial(last_kernel, groups, cut, len(tokens[0])...  10.1 us
    pallas_call x1, Pallas kernels, multiply_first(): pl.pallas_call(functools.partial(first_kernel, min(1024, hidden), len(row...  7.8 us
    ppermute x5, starting transfers between devices, from_next(): return lax.ppermute(x, ('pipe', 'dp'), pairs)  7.77 us
    pallas_call x2, Pallas kernels, fetch(): pl.pallas_call(functools.partial(fetch_kernel, which), in_specs=[pl.Block...  5.81 us
    ppermute x5, waiting for transfers between devices, from_next(): return lax.ppermute(x, ('pipe', 'dp'), pairs)  5.19 us
    ppermute x10, waiting for transfers between devices, swap(): return lax.ppermute(x, 'expert', [(e, e ^ bit) for e in range(experts)])  4.65 us
    ppermute x3, starting transfers between devices, from_share(): return lax.ppermute(x, ('pipe', 'dp', 'expert'), pairs)  2.61 us
  transfers between devices with their start and end apart: 19, of which 7 were waited for; matrix products, arithmetic and copies ran while one was open for 3% of the time, Pallas kernels for 26%

profile of v6, /device:TPU:9, one launch (start us, length us, event | category | flops | bytes accessed | tf_op | source)
XLA Modules:
  0.0 66.6 jit_solution(12683786346117127839)
XLA Ops:
  0.6 0.9 %slice.146 = bf16[80,768]{1,0:T(8,128)(2,1)S(1)} slice(bf16[256,768]{1,0:T(8,128)(2,1)} %bitcast.69), slice={[176:256], [0:768]} | slice | bytes 245760 | tf_op jit(solution)/shard_map/slice | solution.py:381
  1.5 1.3 %collective-permute-start = (bf16[80,768]{1,0:T(8,128)(2,1)S(1)}, bf16[80,768]{1,0:T(8,128)(2,1)S(1)}, u32[]{:S(2)}, u32[]{:S(2)}) collective-permute-start(bf16[80,768]{1,0:T(8,128)(2,1)S(1)} %slice.146), channel_id=1, source_target_pairs={{0,16},{4,20},{8,24},{12,28},{16,0},{20,4},{24,8},{28,12},{1,17},{... | collective-permute-start | bytes 368648 | tf_op jit(solution)/shard_map/ppermute | solution.py:25
  2.8 1.0 %slice.145.refs_0_ = bf16[176,768]{1,0:T(8,128)(2,1)S(1)} slice(bf16[256,768]{1,0:T(8,128)(2,1)} %bitcast.70), slice={[0:176], [0:768]} | slice | bytes 540672 | tf_op jit(solution)/shard_map/slice | solution.py:381
  3.8 1.7 %shard_map.68.refs_1_.refs_0_ = bf16[16,768]{1,0:T(8,128)(2,1)S(1)} custom-call(f32[2,2,128]{2,1,0:T(2,128)} %bitcast.85, s32[2,2,128]{2,1,0:T(2,128)} %bitcast.86, bf16[2,128,768]{2,1,0:T(8,128)(2,1)} %bitcast.71, bf16[2,128,2,768]{3,2,1,0:T(2,128)(2,1)} %bitcast.72), custom_call_target="tpu_custom_call" | custom-call | tf_op jit(solution)/shard_map/pallas_call | solution.py:105
  5.5 0.3 collective-permute-done.refs_2_.refs_0_
  5.8 1.3 %collective-permute-start.1 = (bf16[192,768]{1,0:T(8,128)(2,1)S(1)}, bf16[192,768]{1,0:T(8,128)(2,1)S(1)}, u32[]{:S(2)}, u32[]{:S(2)}) collective-permute-start(bf16[192,768]{1,0:T(8,128)(2,1)S(1)} %shard_map.69), channel_id=1, source_target_pairs={{0,16},{4,20},{8,24},{12,28},{16,0},{20,4},{24,8},{28,12},{1,17},{... | collective-permute-start | bytes 884744 | tf_op jit(solution)/shard_map/ppermute | solution.py:25
  7.1 0.3 collective-permute-start.2
  7.3 1.2 %collective-permute-start.5 = (bf16[80,768]{1,0:T(8,128)(2,1)S(1)}, bf16[80,768]{1,0:T(8,128)(2,1)S(1)}, u32[]{:S(2)}, u32[]{:S(2)}) collective-permute-start(bf16[80,768]{1,0:T(8,128)(2,1)S(1)} %collective-permute-done.refs_2_.refs_0_), channel_id=1, source_target_pairs={{0,2},{1,3},{2,0},{3,1},{4,6},{5,7},{6,4},{7,5},{8,10},{9,11},{10,... | collective-permute-start | bytes 368648 | tf_op jit(solution)/shard_map/ppermute | solution.py:44
  8.6 2.8 %collective-permute-done.5.refs_1_ = bf16[80,768]{1,0:T(8,128)(2,1)S(1)} collective-permute-done((bf16[80,768]{1,0:T(8,128)(2,1)S(1)}, bf16[80,768]{1,0:T(8,128)(2,1)S(1)}, u32[]{:S(2)}, u32[]{:S(2)}) %collective-permute-start.5) | collective-permute-done | bytes 122912 | tf_op jit(solution)/shard_map/ppermute | solution.py:44
  11.4 2.4 %collective-permute-start.6 = (bf16[160,768]{1,0:T(8,128)(2,1)S(1)}, bf16[160,768]{1,0:T(8,128)(2,1)S(1)}, u32[]{:S(2)}, u32[]{:S(2)}) collective-permute-start(bf16[160,768]{1,0:T(8,128)(2,1)S(1)} %shard_map.72.refs_2_.refs_0_), channel_id=1, source_target_pairs={{0,8},{1,9},{2,10},{3,11},{4,12},{5,13},{6,14},{7,15},{8,0},{9,1},... | collective-permute-start | bytes 737288 | tf_op jit(solution)/shard_map/ppermute | solution.py:39
  13.8 0.2 collective-permute-start.11
  13.9 3.7 %collective-permute-done.2.refs_0_.refs_2_ = bf16[176,768]{1,0:T(8,128)(2,1)S(1)} collective-permute-done((bf16[176,768]{1,0:T(8,128)(2,1)S(1)}, bf16[176,768]{1,0:T(8,128)(2,1)S(1)}, u32[]{:S(2)}, u32[]{:S(2)}) %collective-permute-start.2) | collective-permute-done | bytes 270368 | tf_op jit(solution)/shard_map/ppermute | solution.py:25
  17.7 4.9 %collective-permute-start.12 = (bf16[192,768]{1,0:T(8,128)(2,1)S(1)}, bf16[192,768]{1,0:T(8,128)(2,1)S(1)}, u32[]{:S(2)}, u32[]{:S(2)}) collective-permute-start(bf16[192,768]{1,0:T(8,128)(2,1)S(1)} %shard_map.82), channel_id=1, source_target_pairs={{0,16},{4,20},{8,24},{12,28},{16,12},{20,8},{24,4},{28,0},{1,17},{... | collective-permute-start | bytes 884744 | tf_op jit(solution)/shard_map/ppermute | solution.py:25
  22.6 1.3 %collective-permute-start.3 = (bf16[192,768]{1,0:T(8,128)(2,1)S(1)}, bf16[192,768]{1,0:T(8,128)(2,1)S(1)}, u32[]{:S(2)}, u32[]{:S(2)}) collective-permute-start(bf16[192,768]{1,0:T(8,128)(2,1)S(1)} %shard_map.70), channel_id=1, source_target_pairs={{0,2},{1,3},{2,0},{3,1},{4,6},{5,7},{6,4},{7,5},{8,10},{9,11},{10,... | collective-permute-start | bytes 884744 | tf_op jit(solution)/shard_map/ppermute | solution.py:44
  24.1 0.3 collective-permute-start.8
  24.5 2.9 %shard_map.77.refs_2_ = bf16[4096,768]{1,0:T(8,128)(2,1)S(1)} custom-call(bf16[1,4096,3072]{2,1,0:T(8,128)(2,1)} %weights_hbm.5, bf16[160,768]{1,0:T(8,128)(2,1)S(1)} %collective-permute-done.6.refs_2_.refs_0_), custom_call_target="tpu_custom_call" | custom-call | tf_op jit(solution)/shard_map/pallas_call | solution.py:248
  27.4 2.9 %shard_map.78.refs_3_ = bf16[4096,768]{1,0:T(8,128)(2,1)S(1)} custom-call(bf16[1,4096,3072]{2,1,0:T(8,128)(2,1)} %weights_hbm.5, bf16[160,768]{1,0:T(8,128)(2,1)S(1)} %collective-permute-done.6.refs_2_.refs_0_), custom_call_target="tpu_custom_call" | custom-call | tf_op jit(solution)/shard_map/pallas_call | solution.py:248
  30.4 4.8 %collective-permute-start.4 = (bf16[2,16,128]{2,1,0:T(8,128)(2,1)S(1)}, bf16[2,16,128]{2,1,0:T(8,128)(2,1)S(1)}, u32[]{:S(2)}, u32[]{:S(2)}) collective-permute-start(bf16[2,16,128]{2,1,0:T(8,128)(2,1)S(1)} %pad_maximum_fusion.1), channel_id=1, source_target_pairs={{0,1},{1,0},{2,3},{3,2},{4,5},{5,4},{6,7},{7,6},{8,9},{9,8},{10,11... | collective-permute-start | bytes 24584 | tf_op jit(solution)/shard_map/ppermute | solution.py:44
  35.2 1.3 %collective-permute-start.15 = (bf16[176,768]{1,0:T(8,128)(2,1)S(1)}, bf16[176,768]{1,0:T(8,128)(2,1)S(1)}, u32[]{:S(2)}, u32[]{:S(2)}) collective-permute-start(bf16[176,768]{1,0:T(8,128)(2,1)S(1)} %slice.157.refs_2_), channel_id=1, source_target_pairs={{0,2},{1,3},{2,0},{3,1},{4,6},{5,7},{6,4},{7,5},{8,10},{9,11},{10,... | collective-permute-start | bytes 811016 | tf_op jit(solution)/shard_map/ppermute | solution.py:44
  36.6 0.2 collective-permute-done.8
  36.8 1.7 %collective-permute-start.9 = (bf16[512,768]{1,0:T(8,128)(2,1)S(1)}, bf16[512,768]{1,0:T(8,128)(2,1)S(1)}, u32[]{:S(2)}, u32[]{:S(2)}) collective-permute-start(bf16[512,768]{1,0:T(8,128)(2,1)S(1)} %shard_map.75.refs_0_), channel_id=1, source_target_pairs={{0,1},{1,0},{2,3},{3,2},{4,5},{5,4},{6,7},{7,6},{8,9},{9,8},{10,11... | collective-permute-start | bytes 2359304 | tf_op jit(solution)/shard_map/ppermute | solution.py:44
  38.9 0.3 shard_map.71
  39.2 1.2 %collective-permute-done.10.refs_0_ = bf16[192,768]{1,0:T(8,128)(2,1)S(1)} collective-permute-done((bf16[192,768]{1,0:T(8,128)(2,1)S(1)}, bf16[192,768]{1,0:T(8,128)(2,1)S(1)}, u32[]{:S(2)}, u32[]{:S(2)}) %collective-permute-start.10) | collective-permute-done | bytes 294944 | tf_op jit(solution)/shard_map/ppermute | solution.py:25
  40.5 1.3 %collective-permute-start.14 = (bf16[176,768]{1,0:T(8,128)(2,1)S(1)}, bf16[176,768]{1,0:T(8,128)(2,1)S(1)}, u32[]{:S(2)}, u32[]{:S(2)}) collective-permute-start(bf16[176,768]{1,0:T(8,128)(2,1)S(1)} %slice.156.refs_0_), channel_id=1, source_target_pairs={{0,2},{1,3},{2,0},{3,1},{4,6},{5,7},{6,4},{7,5},{8,10},{9,11},{10,... | collective-permute-start | bytes 811016 | tf_op jit(solution)/shard_map/ppermute | solution.py:44
  41.8 1.3 %collective-permute-start.18 = (bf16[16,768]{1,0:T(8,128)(2,1)S(1)}, bf16[16,768]{1,0:T(8,128)(2,1)S(1)}, u32[]{:S(2)}, u32[]{:S(2)}) collective-permute-start(bf16[16,768]{1,0:T(8,128)(2,1)S(1)} %shard_map.87), channel_id=1, source_target_pairs={{16,8},{20,12},{24,0},{28,4},{17,9},{21,13},{25,1},{29,5},{18,10},... | collective-permute-start | bytes 73736 | tf_op jit(solution)/shard_map/ppermute | solution.py:405
  43.2 0.7 %shard_map.76.refs_1_ = bf16[544,768]{1,0:T(8,128)(2,1)S(1)} custom-call(bf16[2,272,512]{2,1,0:T(8,128)(2,1)S(1)} %get-tuple-element.9.places_ref.refs_1_, f32[128,128]{1,0:T(8,128)S(1)} %get-tuple-element.10.weights_ref, bf16[512,768]{1,0:T(8,128)(2,1)S(1)} %shard_map.75.refs_0_, bf16[512,768]{1,0:T(8,128)(2,1)S(1)} %collective-permute-done.9.refs_1_), custom_call_target="tpu_custom_call" | custom-call | tf_op jit(solution)/shard_map/pallas_call | solution.py:205
  43.9 0.7 %shard_map.74.refs_0_ = bf16[544,768]{1,0:T(8,128)(2,1)S(1)} custom-call(bf16[2,272,512]{2,1,0:T(8,128)(2,1)S(1)} %get-tuple-element.9.places_ref.refs_1_, f32[128,128]{1,0:T(8,128)S(1)} %get-tuple-element.10.weights_ref, bf16[512,768]{1,0:T(8,128)(2,1)S(1)} %shard_map.73.refs_0_, bf16[512,768]{1,0:T(8,128)(2,1)S(1)} %collective-permute-done.7.refs_1_), custom_call_target="tpu_custom_call" | custom-call | tf_op jit(solution)/shard_map/pallas_call | solution.py:205
  44.6 1.7 %collective-permute-start.13 = (bf16[512,768]{1,0:T(8,128)(2,1)S(1)}, bf16[512,768]{1,0:T(8,128)(2,1)S(1)}, u32[]{:S(2)}, u32[]{:S(2)}) collective-permute-start(bf16[512,768]{1,0:T(8,128)(2,1)S(1)} %shard_map.83.refs_2_), channel_id=1, source_target_pairs={{0,1},{1,0},{2,3},{3,2},{4,5},{5,4},{6,7},{7,6},{8,9},{9,8},{10,11... | collective-permute-start | bytes 2359304 | tf_op jit(solution)/shard_map/ppermute | solution.py:44
  46.3 7.8 %shard_map.79 = (f32[544,4096]{1,0:T(8,128)S(1)}, f32[8,128]{1,0:T(8,128)S(1)}, bf16[4096,768]{1,0:T(8,128)(2,1)S(1)}, bf16[4096,768]{1,0:T(8,128)(2,1)S(1)}) custom-call(bf16[1,4096,3072]{2,1,0:T(8,128)(2,1)} %weights_hbm.5, bf16[544,768]{1,0:T(8,128)(2,1)S(1)} %shard_map.74.refs_0_, bf16[544,768]{1,0:T(8,128)(2,1)S(1)} %shard_map.76.refs_1_, ...), custom_call_target="tpu_custom_call" | custom-call | flops 1 | bytes 1 | tf_op jit(solution)/shard_map/pallas_call | solution.py:295
  54.4 0.6 copy.24
  55.0 1.6 %collective-permute-done.17.refs_5_ = bf16[512,768]{1,0:T(8,128)(2,1)S(1)} collective-permute-done((bf16[512,768]{1,0:T(8,128)(2,1)S(1)}, bf16[512,768]{1,0:T(8,128)(2,1)S(1)}, u32[]{:S(2)}, u32[]{:S(2)}) %collective-permute-start.17) | collective-permute-done | bytes 786464 | tf_op jit(solution)/shard_map/ppermute | solution.py:44
  56.6 10.1 %shard_map.86 = bf16[1,2,1,68,4,4096]{5,4,3,2,1,0:T(4,128)(2,1)} custom-call(bf16[2,272,512]{2,1,0:T(8,128)(2,1)S(1)} %get-tuple-element.9.places_ref.refs_1_, f32[128,128]{1,0:T(8,128)S(1)} %get-tuple-element.10.weights_ref, f32[544,4096]{1,0:T(8,128)S(1)} %get-tuple-element.11.total_ref, bf16[4096,768]{1,0:T(8,128)(2,1)S(1)} %get-tuple-element.12.refs_0_, ...), custom_call_target="tpu_custom_call" | custom-call | flops 6845104128 | bytes 12582912 | tf_op jit(solution)/shard_map/pallas_call | solution.py:349
  (60 shorter events, 1.1 us)
Async XLA Ops:
  1.5 4.3 %collective-permute-start = (bf16[80,768]{1,0:T(8,128)(2,1)S(1)}, bf16[80,768]{1,0:T(8,128)(2,1)S(1)}, u32[]{:S(2)}, u32[]{:S(2)}) collective-permute-start(bf16[80,768]{1,0:T(8,128)(2,1)S(1)} %slice.146), channel_id=1, source_target_pairs={{0,16},{4,20},{8,24},{12,28},{16,0},{20,4},{24,8},{28,12},{1,17},{... | collective-permute-start | bytes 368648 | tf_op jit(solution)/shard_map/ppermute | solution.py:25
  5.8 16.7 %collective-permute-start.1 = (bf16[192,768]{1,0:T(8,128)(2,1)S(1)}, bf16[192,768]{1,0:T(8,128)(2,1)S(1)}, u32[]{:S(2)}, u32[]{:S(2)}) collective-permute-start(bf16[192,768]{1,0:T(8,128)(2,1)S(1)} %shard_map.69), channel_id=1, source_target_pairs={{0,16},{4,20},{8,24},{12,28},{16,0},{20,4},{24,8},{28,12},{1,17},{... | collective-permute-start | bytes 884744 | tf_op jit(solution)/shard_map/ppermute | solution.py:25
  7.1 10.5 %collective-permute-start.2 = (bf16[176,768]{1,0:T(8,128)(2,1)S(1)}, bf16[176,768]{1,0:T(8,128)(2,1)S(1)}, u32[]{:S(2)}, u32[]{:S(2)}) collective-permute-start(bf16[176,768]{1,0:T(8,128)(2,1)S(1)} %slice.145.refs_0_), channel_id=1, source_target_pairs={{0,16},{4,20},{8,24},{12,28},{16,8},{20,12},{24,0},{28,4},{1,17},{... | collective-permute-start | bytes 811016 | tf_op jit(solution)/shard_map/ppermute | solution.py:25
  7.3 4.0 %collective-permute-start.5 = (bf16[80,768]{1,0:T(8,128)(2,1)S(1)}, bf16[80,768]{1,0:T(8,128)(2,1)S(1)}, u32[]{:S(2)}, u32[]{:S(2)}) collective-permute-start(bf16[80,768]{1,0:T(8,128)(2,1)S(1)} %collective-permute-done.refs_2_.refs_0_), channel_id=1, source_target_pairs={{0,2},{1,3},{2,0},{3,1},{4,6},{5,7},{6,4},{7,5},{8,10},{9,11},{10,... | collective-permute-start | bytes 368648 | tf_op jit(solution)/shard_map/ppermute | solution.py:44
  11.4 13.0 %collective-permute-start.6 = (bf16[160,768]{1,0:T(8,128)(2,1)S(1)}, bf16[160,768]{1,0:T(8,128)(2,1)S(1)}, u32[]{:S(2)}, u32[]{:S(2)}) collective-permute-start(bf16[160,768]{1,0:T(8,128)(2,1)S(1)} %shard_map.72.refs_2_.refs_0_), channel_id=1, source_target_pairs={{0,8},{1,9},{2,10},{3,11},{4,12},{5,13},{6,14},{7,15},{8,0},{9,1},... | collective-permute-start | bytes 737288 | tf_op jit(solution)/shard_map/ppermute | solution.py:39
  13.8 10.3 %collective-permute-start.11 = (bf16[160,768]{1,0:T(8,128)(2,1)S(1)}, bf16[160,768]{1,0:T(8,128)(2,1)S(1)}, u32[]{:S(2)}, u32[]{:S(2)}) collective-permute-start(bf16[160,768]{1,0:T(8,128)(2,1)S(1)} %shard_map.72.refs_2_.refs_0_), channel_id=1, source_target_pairs={{0,4},{1,5},{2,6},{3,7},{4,0},{5,1},{6,2},{7,3},{8,12},{9,13},{10,... | collective-permute-start | bytes 737288 | tf_op jit(solution)/shard_map/ppermute | solution.py:39
  17.7 12.6 %collective-permute-start.12 = (bf16[192,768]{1,0:T(8,128)(2,1)S(1)}, bf16[192,768]{1,0:T(8,128)(2,1)S(1)}, u32[]{:S(2)}, u32[]{:S(2)}) collective-permute-start(bf16[192,768]{1,0:T(8,128)(2,1)S(1)} %shard_map.82), channel_id=1, source_target_pairs={{0,16},{4,20},{8,24},{12,28},{16,12},{20,8},{24,4},{28,0},{1,17},{... | collective-permute-start | bytes 884744 | tf_op jit(solution)/shard_map/ppermute | solution.py:25
  22.6 7.8 %collective-permute-start.3 = (bf16[192,768]{1,0:T(8,128)(2,1)S(1)}, bf16[192,768]{1,0:T(8,128)(2,1)S(1)}, u32[]{:S(2)}, u32[]{:S(2)}) collective-permute-start(bf16[192,768]{1,0:T(8,128)(2,1)S(1)} %shard_map.70), channel_id=1, source_target_pairs={{0,2},{1,3},{2,0},{3,1},{4,6},{5,7},{6,4},{7,5},{8,10},{9,11},{10,... | collective-permute-start | bytes 884744 | tf_op jit(solution)/shard_map/ppermute | solution.py:44
  23.9 16.5 %collective-permute-start.10 = (bf16[192,768]{1,0:T(8,128)(2,1)S(1)}, bf16[192,768]{1,0:T(8,128)(2,1)S(1)}, u32[]{:S(2)}, u32[]{:S(2)}) collective-permute-start(bf16[192,768]{1,0:T(8,128)(2,1)S(1)} %shard_map.80), channel_id=1, source_target_pairs={{0,16},{4,20},{8,24},{12,28},{16,4},{20,0},{24,12},{28,8},{1,17},{... | collective-permute-start | bytes 884744 | tf_op jit(solution)/shard_map/ppermute | solution.py:25
  24.1 12.7 %collective-permute-start.8 = (bf16[192,768]{1,0:T(8,128)(2,1)S(1)}, bf16[192,768]{1,0:T(8,128)(2,1)S(1)}, u32[]{:S(2)}, u32[]{:S(2)}) collective-permute-start(bf16[192,768]{1,0:T(8,128)(2,1)S(1)} %collective-permute-done.1.refs_2_.refs_1_), channel_id=1, source_target_pairs={{0,2},{1,3},{2,0},{3,1},{4,6},{5,7},{6,4},{7,5},{8,10},{9,11},{10,... | collective-permute-start | bytes 884744 | tf_op jit(solution)/shard_map/ppermute | solution.py:44
  24.4 29.7 %collective-permute-start.16 = (bf16[160,768]{1,0:T(8,128)(2,1)S(1)}, bf16[160,768]{1,0:T(8,128)(2,1)S(1)}, u32[]{:S(2)}, u32[]{:S(2)}) collective-permute-start(bf16[160,768]{1,0:T(8,128)(2,1)S(1)} %shard_map.84), channel_id=1, source_target_pairs={{0,12},{1,13},{2,14},{3,15},{4,8},{5,9},{6,10},{7,11},{8,4},{9,5},... | collective-permute-start | bytes 737288 | tf_op jit(solution)/shard_map/ppermute | solution.py:39
  30.4 8.2 %collective-permute-start.4 = (bf16[2,16,128]{2,1,0:T(8,128)(2,1)S(1)}, bf16[2,16,128]{2,1,0:T(8,128)(2,1)S(1)}, u32[]{:S(2)}, u32[]{:S(2)}) collective-permute-start(bf16[2,16,128]{2,1,0:T(8,128)(2,1)S(1)} %pad_maximum_fusion.1), channel_id=1, source_target_pairs={{0,1},{1,0},{2,3},{3,2},{4,5},{5,4},{6,7},{7,6},{8,9},{9,8},{10,11... | collective-permute-start | bytes 24584 | tf_op jit(solution)/shard_map/ppermute | solution.py:44
  35.2 18.9 %collective-permute-start.15 = (bf16[176,768]{1,0:T(8,128)(2,1)S(1)}, bf16[176,768]{1,0:T(8,128)(2,1)S(1)}, u32[]{:S(2)}, u32[]{:S(2)}) collective-permute-start(bf16[176,768]{1,0:T(8,128)(2,1)S(1)} %slice.157.refs_2_), channel_id=1, source_target_pairs={{0,2},{1,3},{2,0},{3,1},{4,6},{5,7},{6,4},{7,5},{8,10},{9,11},{10,... | collective-permute-start | bytes 811016 | tf_op jit(solution)/shard_map/ppermute | solution.py:44
  36.8 5.0 %collective-permute-start.9 = (bf16[512,768]{1,0:T(8,128)(2,1)S(1)}, bf16[512,768]{1,0:T(8,128)(2,1)S(1)}, u32[]{:S(2)}, u32[]{:S(2)}) collective-permute-start(bf16[512,768]{1,0:T(8,128)(2,1)S(1)} %shard_map.75.refs_0_), channel_id=1, source_target_pairs={{0,1},{1,0},{2,3},{3,2},{4,5},{5,4},{6,7},{7,6},{8,9},{9,8},{10,11... | collective-permute-start | bytes 2359304 | tf_op jit(solution)/shard_map/ppermute | solution.py:44
  38.6 5.3 %collective-permute-start.7 = (bf16[512,768]{1,0:T(8,128)(2,1)S(1)}, bf16[512,768]{1,0:T(8,128)(2,1)S(1)}, u32[]{:S(2)}, u32[]{:S(2)}) collective-permute-start(bf16[512,768]{1,0:T(8,128)(2,1)S(1)} %shard_map.73.refs_0_), channel_id=1, source_target_pairs={{0,1},{1,0},{2,3},{3,2},{4,5},{5,4},{6,7},{7,6},{8,9},{9,8},{10,11... | collective-permute-start | bytes 2359304 | tf_op jit(solution)/shard_map/ppermute | solution.py:44
  40.5 13.7 %collective-permute-start.14 = (bf16[176,768]{1,0:T(8,128)(2,1)S(1)}, bf16[176,768]{1,0:T(8,128)(2,1)S(1)}, u32[]{:S(2)}, u32[]{:S(2)}) collective-permute-start(bf16[176,768]{1,0:T(8,128)(2,1)S(1)} %slice.156.refs_0_), channel_id=1, source_target_pairs={{0,2},{1,3},{2,0},{3,1},{4,6},{5,7},{6,4},{7,5},{8,10},{9,11},{10,... | collective-permute-start | bytes 811016 | tf_op jit(solution)/shard_map/ppermute | solution.py:44
  41.8 12.5 %collective-permute-start.18 = (bf16[16,768]{1,0:T(8,128)(2,1)S(1)}, bf16[16,768]{1,0:T(8,128)(2,1)S(1)}, u32[]{:S(2)}, u32[]{:S(2)}) collective-permute-start(bf16[16,768]{1,0:T(8,128)(2,1)S(1)} %shard_map.87), channel_id=1, source_target_pairs={{16,8},{20,12},{24,0},{28,4},{17,9},{21,13},{25,1},{29,5},{18,10},... | collective-permute-start | bytes 73736 | tf_op jit(solution)/shard_map/ppermute | solution.py:405
  44.6 10.3 %collective-permute-start.13 = (bf16[512,768]{1,0:T(8,128)(2,1)S(1)}, bf16[512,768]{1,0:T(8,128)(2,1)S(1)}, u32[]{:S(2)}, u32[]{:S(2)}) collective-permute-start(bf16[512,768]{1,0:T(8,128)(2,1)S(1)} %shard_map.83.refs_2_), channel_id=1, source_target_pairs={{0,1},{1,0},{2,3},{3,2},{4,5},{5,4},{6,7},{7,6},{8,9},{9,8},{10,11... | collective-permute-start | bytes 2359304 | tf_op jit(solution)/shard_map/ppermute | solution.py:44
  54.2 2.4 %collective-permute-start.17 = (bf16[512,768]{1,0:T(8,128)(2,1)S(1)}, bf16[512,768]{1,0:T(8,128)(2,1)S(1)}, u32[]{:S(2)}, u32[]{:S(2)}) collective-permute-start(bf16[512,768]{1,0:T(8,128)(2,1)S(1)} %shard_map.85.refs_4_), channel_id=1, source_target_pairs={{0,1},{1,0},{2,3},{3,2},{4,5},{5,4},{6,7},{7,6},{8,9},{9,8},{10,11... | collective-permute-start | bytes 2359304 | tf_op jit(solution)/shard_map/ppermute | solution.py:44

commit v7 on v6

--- a/solution.py
+++ b/solution.py
@@ -453,7 +453,7 @@
                 tokens.append(stacked.transpose(1, 0, 2).reshape(-1, together * share))
         return tokens
 
-    fetch_gates = [[pairs[2]], [pairs[2]]]
+    fetch_gates = [[], [pairs[2]]]
     held = []
     for i in range(half):
         gates = fetch_gates[i] if i < len(fetch_gates) else []

time: 66.9 us -> 66.9 us (level)
    ppermute x5, waiting for transfers between devices: 5.19 us -> 6.12 us  [from_next(): return lax.ppermute(x, ('pipe', 'dp'), pairs)]
    ppermute x10, waiting for transfers between devices: 4.65 us -> 3.75 us  [swap(): return lax.ppermute(x, 'expert', [(e, e ^ bit) for e in range(experts)])]
where the time goes in v7:
time: 66.9 us; the launch traced here: 66.7 us
  Pallas kernels  27.5 us (41%)
  starting transfers between devices  25.5 us (38%)
  waiting for transfers between devices  9.88 us (15%)
  local copies, waits for them, and re-layouts  2.6 us (4%)
  between operations  0.98 us (1%)
    ppermute x10, starting transfers between devices, swap(): return lax.ppermute(x, 'expert', [(e, e ^ bit) for e in range(experts)])  13.9 us
    pallas_call x1, Pallas kernels, multiply_last(): pl.pallas_call(functools.partial(last_kernel, groups, cut, len(tokens[0])...  10.1 us
    pallas_call x1, Pallas kernels, multiply_first(): pl.pallas_call(functools.partial(first_kernel, min(1024, hidden), len(row...  7.8 us
    ppermute x5, starting transfers between devices, from_next(): return lax.ppermute(x, ('pipe', 'dp'), pairs)  7.77 us
    ppermute x5, waiting for transfers between devices, from_next(): return lax.ppermute(x, ('pipe', 'dp'), pairs)  6.12 us
    pallas_call x2, Pallas kernels, fetch(): pl.pallas_call(functools.partial(fetch_kernel, which), in_specs=[pl.Block...  5.79 us
    ppermute x10, waiting for transfers between devices, swap(): return lax.ppermute(x, 'expert', [(e, e ^ bit) for e in range(experts)])  3.75 us
    ppermute x3, starting transfers between devices, from_share(): return lax.ppermute(x, ('pipe', 'dp', 'expert'), pairs)  2.61 us
  transfers between devices with their start and end apart: 19, of which 7 were waited for; matrix products, arithmetic and copies ran while one was open for 3% of the time, Pallas kernels for 26%

profile of v7, /device:TPU:9, one launch (start us, length us, event | category | flops | bytes accessed | tf_op | source)
XLA Modules:
  0.0 66.7 jit_solution(4146133138810935949)
XLA Ops:
  0.6 0.9 %slice.146 = bf16[80,768]{1,0:T(8,128)(2,1)S(1)} slice(bf16[256,768]{1,0:T(8,128)(2,1)} %bitcast.69), slice={[176:256], [0:768]} | slice | bytes 245760 | tf_op jit(solution)/shard_map/slice | solution.py:381
  1.5 1.3 %collective-permute-start = (bf16[80,768]{1,0:T(8,128)(2,1)S(1)}, bf16[80,768]{1,0:T(8,128)(2,1)S(1)}, u32[]{:S(2)}, u32[]{:S(2)}) collective-permute-start(bf16[80,768]{1,0:T(8,128)(2,1)S(1)} %slice.146), channel_id=1, source_target_pairs={{0,16},{4,20},{8,24},{12,28},{16,0},{20,4},{24,8},{28,12},{1,17},{... | collective-permute-start | bytes 368648 | tf_op jit(solution)/shard_map/ppermute | solution.py:25
  2.8 1.0 %slice.145.refs_0_ = bf16[176,768]{1,0:T(8,128)(2,1)S(1)} slice(bf16[256,768]{1,0:T(8,128)(2,1)} %bitcast.70), slice={[0:176], [0:768]} | slice | bytes 540672 | tf_op jit(solution)/shard_map/slice | solution.py:381
  3.8 1.7 %shard_map.68.refs_1_.refs_0_ = bf16[16,768]{1,0:T(8,128)(2,1)S(1)} custom-call(f32[2,2,128]{2,1,0:T(2,128)} %bitcast.85, s32[2,2,128]{2,1,0:T(2,128)} %bitcast.86, bf16[2,128,768]{2,1,0:T(8,128)(2,1)} %bitcast.71, bf16[2,128,2,768]{3,2,1,0:T(2,128)(2,1)} %bitcast.72), custom_call_target="tpu_custom_call" | custom-call | tf_op jit(solution)/shard_map/pallas_call | solution.py:105
  5.5 0.3 collective-permute-done.refs_2_.refs_0_
  5.8 1.3 %collective-permute-start.1 = (bf16[192,768]{1,0:T(8,128)(2,1)S(1)}, bf16[192,768]{1,0:T(8,128)(2,1)S(1)}, u32[]{:S(2)}, u32[]{:S(2)}) collective-permute-start(bf16[192,768]{1,0:T(8,128)(2,1)S(1)} %shard_map.69), channel_id=1, source_target_pairs={{0,16},{4,20},{8,24},{12,28},{16,0},{20,4},{24,8},{28,12},{1,17},{... | collective-permute-start | bytes 884744 | tf_op jit(solution)/shard_map/ppermute | solution.py:25
  7.1 0.3 collective-permute-start.2
  7.3 1.2 %collective-permute-start.5 = (bf16[80,768]{1,0:T(8,128)(2,1)S(1)}, bf16[80,768]{1,0:T(8,128)(2,1)S(1)}, u32[]{:S(2)}, u32[]{:S(2)}) collective-permute-start(bf16[80,768]{1,0:T(8,128)(2,1)S(1)} %collective-permute-done.refs_2_.refs_0_), channel_id=1, source_target_pairs={{0,2},{1,3},{2,0},{3,1},{4,6},{5,7},{6,4},{7,5},{8,10},{9,11},{10,... | collective-permute-start | bytes 368648 | tf_op jit(solution)/shard_map/ppermute | solution.py:44
  8.6 2.9 %shard_map.77.refs_2_ = bf16[4096,768]{1,0:T(8,128)(2,1)S(1)} custom-call(bf16[1,4096,3072]{2,1,0:T(8,128)(2,1)} %weights_hbm.5), custom_call_target="tpu_custom_call" | custom-call | tf_op jit(solution)/shard_map/pallas_call | solution.py:248
  11.5 2.4 %collective-permute-start.6 = (bf16[160,768]{1,0:T(8,128)(2,1)S(1)}, bf16[160,768]{1,0:T(8,128)(2,1)S(1)}, u32[]{:S(2)}, u32[]{:S(2)}) collective-permute-start(bf16[160,768]{1,0:T(8,128)(2,1)S(1)} %shard_map.72.refs_2_.refs_0_), channel_id=1, source_target_pairs={{0,8},{1,9},{2,10},{3,11},{4,12},{5,13},{6,14},{7,15},{8,0},{9,1},... | collective-permute-start | bytes 737288 | tf_op jit(solution)/shard_map/ppermute | solution.py:39
  13.9 0.2 collective-permute-start.11
  14.1 3.6 %collective-permute-done.2.refs_0_.refs_2_ = bf16[176,768]{1,0:T(8,128)(2,1)S(1)} collective-permute-done((bf16[176,768]{1,0:T(8,128)(2,1)S(1)}, bf16[176,768]{1,0:T(8,128)(2,1)S(1)}, u32[]{:S(2)}, u32[]{:S(2)}) %collective-permute-start.2) | collective-permute-done | bytes 270368 | tf_op jit(solution)/shard_map/ppermute | solution.py:25
  17.7 4.9 %collective-permute-start.12 = (bf16[192,768]{1,0:T(8,128)(2,1)S(1)}, bf16[192,768]{1,0:T(8,128)(2,1)S(1)}, u32[]{:S(2)}, u32[]{:S(2)}) collective-permute-start(bf16[192,768]{1,0:T(8,128)(2,1)S(1)} %shard_map.82), channel_id=1, source_target_pairs={{0,16},{4,20},{8,24},{12,28},{16,12},{20,8},{24,4},{28,0},{1,17},{... | collective-permute-start | bytes 884744 | tf_op jit(solution)/shard_map/ppermute | solution.py:25
  22.6 1.3 %collective-permute-start.3 = (bf16[192,768]{1,0:T(8,128)(2,1)S(1)}, bf16[192,768]{1,0:T(8,128)(2,1)S(1)}, u32[]{:S(2)}, u32[]{:S(2)}) collective-permute-start(bf16[192,768]{1,0:T(8,128)(2,1)S(1)} %shard_map.70), channel_id=1, source_target_pairs={{0,2},{1,3},{2,0},{3,1},{4,6},{5,7},{6,4},{7,5},{8,10},{9,11},{10,... | collective-permute-start | bytes 884744 | tf_op jit(solution)/shard_map/ppermute | solution.py:44
  24.1 0.3 collective-permute-start.8
  24.5 2.9 %shard_map.78.refs_3_ = bf16[4096,768]{1,0:T(8,128)(2,1)S(1)} custom-call(bf16[1,4096,3072]{2,1,0:T(8,128)(2,1)} %weights_hbm.5, bf16[160,768]{1,0:T(8,128)(2,1)S(1)} %collective-permute-done.6.refs_2_.refs_0_), custom_call_target="tpu_custom_call" | custom-call | tf_op jit(solution)/shard_map/pallas_call | solution.py:248
  27.4 1.1 %collective-permute-done.12 = bf16[192,768]{1,0:T(8,128)(2,1)S(1)} collective-permute-done((bf16[192,768]{1,0:T(8,128)(2,1)S(1)}, bf16[192,768]{1,0:T(8,128)(2,1)S(1)}, u32[]{:S(2)}, u32[]{:S(2)}) %collective-permute-start.12) | collective-permute-done | bytes 294944 | tf_op jit(solution)/shard_map/ppermute | solution.py:25
  28.4 2.0 %collective-permute-done.3 = bf16[192,768]{1,0:T(8,128)(2,1)S(1)} collective-permute-done((bf16[192,768]{1,0:T(8,128)(2,1)S(1)}, bf16[192,768]{1,0:T(8,128)(2,1)S(1)}, u32[]{:S(2)}, u32[]{:S(2)}) %collective-permute-start.3) | collective-permute-done | bytes 294944 | tf_op jit(solution)/shard_map/ppermute | solution.py:44
  30.4 4.8 %collective-permute-start.4 = (bf16[2,16,128]{2,1,0:T(8,128)(2,1)S(1)}, bf16[2,16,128]{2,1,0:T(8,128)(2,1)S(1)}, u32[]{:S(2)}, u32[]{:S(2)}) collective-permute-start(bf16[2,16,128]{2,1,0:T(8,128)(2,1)S(1)} %pad_maximum_fusion.1), channel_id=1, source_target_pairs={{0,1},{1,0},{2,3},{3,2},{4,5},{5,4},{6,7},{7,6},{8,9},{9,8},{10,11... | collective-permute-start | bytes 24584 | tf_op jit(solution)/shard_map/ppermute | solution.py:44
  35.2 1.3 %collective-permute-start.15 = (bf16[176,768]{1,0:T(8,128)(2,1)S(1)}, bf16[176,768]{1,0:T(8,128)(2,1)S(1)}, u32[]{:S(2)}, u32[]{:S(2)}) collective-permute-start(bf16[176,768]{1,0:T(8,128)(2,1)S(1)} %slice.157.refs_2_), channel_id=1, source_target_pairs={{0,2},{1,3},{2,0},{3,1},{4,6},{5,7},{6,4},{7,5},{8,10},{9,11},{10,... | collective-permute-start | bytes 811016 | tf_op jit(solution)/shard_map/ppermute | solution.py:44
  36.8 1.7 %collective-permute-start.9 = (bf16[512,768]{1,0:T(8,128)(2,1)S(1)}, bf16[512,768]{1,0:T(8,128)(2,1)S(1)}, u32[]{:S(2)}, u32[]{:S(2)}) collective-permute-start(bf16[512,768]{1,0:T(8,128)(2,1)S(1)} %shard_map.75.refs_0_), channel_id=1, source_target_pairs={{0,1},{1,0},{2,3},{3,2},{4,5},{5,4},{6,7},{7,6},{8,9},{9,8},{10,11... | collective-permute-start | bytes 2359304 | tf_op jit(solution)/shard_map/ppermute | solution.py:44
  38.9 0.3 shard_map.71
  39.2 1.2 %collective-permute-done.10.refs_0_ = bf16[192,768]{1,0:T(8,128)(2,1)S(1)} collective-permute-done((bf16[192,768]{1,0:T(8,128)(2,1)S(1)}, bf16[192,768]{1,0:T(8,128)(2,1)S(1)}, u32[]{:S(2)}, u32[]{:S(2)}) %collective-permute-start.10) | collective-permute-done | bytes 294944 | tf_op jit(solution)/shard_map/ppermute | solution.py:25
  40.5 1.3 %collective-permute-start.14 = (bf16[176,768]{1,0:T(8,128)(2,1)S(1)}, bf16[176,768]{1,0:T(8,128)(2,1)S(1)}, u32[]{:S(2)}, u32[]{:S(2)}) collective-permute-start(bf16[176,768]{1,0:T(8,128)(2,1)S(1)} %slice.156.refs_0_), channel_id=1, source_target_pairs={{0,2},{1,3},{2,0},{3,1},{4,6},{5,7},{6,4},{7,5},{8,10},{9,11},{10,... | collective-permute-start | bytes 811016 | tf_op jit(solution)/shard_map/ppermute | solution.py:44
  41.8 1.3 %collective-permute-start.18 = (bf16[16,768]{1,0:T(8,128)(2,1)S(1)}, bf16[16,768]{1,0:T(8,128)(2,1)S(1)}, u32[]{:S(2)}, u32[]{:S(2)}) collective-permute-start(bf16[16,768]{1,0:T(8,128)(2,1)S(1)} %shard_map.87), channel_id=1, source_target_pairs={{16,8},{20,12},{24,0},{28,4},{17,9},{21,13},{25,1},{29,5},{18,10},... | collective-permute-start | bytes 73736 | tf_op jit(solution)/shard_map/ppermute | solution.py:405
  43.2 0.7 %shard_map.76.refs_1_ = bf16[544,768]{1,0:T(8,128)(2,1)S(1)} custom-call(bf16[2,272,512]{2,1,0:T(8,128)(2,1)S(1)} %get-tuple-element.9.places_ref.refs_1_, f32[128,128]{1,0:T(8,128)S(1)} %get-tuple-element.10.weights_ref, bf16[512,768]{1,0:T(8,128)(2,1)S(1)} %shard_map.75.refs_0_, bf16[512,768]{1,0:T(8,128)(2,1)S(1)} %collective-permute-done.9.refs_1_), custom_call_target="tpu_custom_call" | custom-call | tf_op jit(solution)/shard_map/pallas_call | solution.py:205
  43.9 0.7 %shard_map.74.refs_0_ = bf16[544,768]{1,0:T(8,128)(2,1)S(1)} custom-call(bf16[2,272,512]{2,1,0:T(8,128)(2,1)S(1)} %get-tuple-element.9.places_ref.refs_1_, f32[128,128]{1,0:T(8,128)S(1)} %get-tuple-element.10.weights_ref, bf16[512,768]{1,0:T(8,128)(2,1)S(1)} %shard_map.73.refs_0_, bf16[512,768]{1,0:T(8,128)(2,1)S(1)} %collective-permute-done.7.refs_1_), custom_call_target="tpu_custom_call" | custom-call | tf_op jit(solution)/shard_map/pallas_call | solution.py:205
  44.6 1.7 %collective-permute-start.13 = (bf16[512,768]{1,0:T(8,128)(2,1)S(1)}, bf16[512,768]{1,0:T(8,128)(2,1)S(1)}, u32[]{:S(2)}, u32[]{:S(2)}) collective-permute-start(bf16[512,768]{1,0:T(8,128)(2,1)S(1)} %shard_map.83.refs_2_), channel_id=1, source_target_pairs={{0,1},{1,0},{2,3},{3,2},{4,5},{5,4},{6,7},{7,6},{8,9},{9,8},{10,11... | collective-permute-start | bytes 2359304 | tf_op jit(solution)/shard_map/ppermute | solution.py:44
  46.3 7.8 %shard_map.79 = (f32[544,4096]{1,0:T(8,128)S(1)}, f32[8,128]{1,0:T(8,128)S(1)}, bf16[4096,768]{1,0:T(8,128)(2,1)S(1)}, bf16[4096,768]{1,0:T(8,128)(2,1)S(1)}) custom-call(bf16[1,4096,3072]{2,1,0:T(8,128)(2,1)} %weights_hbm.5, bf16[544,768]{1,0:T(8,128)(2,1)S(1)} %shard_map.74.refs_0_, bf16[544,768]{1,0:T(8,128)(2,1)S(1)} %shard_map.76.refs_1_, ...), custom_call_target="tpu_custom_call" | custom-call | flops 1 | bytes 1 | tf_op jit(solution)/shard_map/pallas_call | solution.py:295
  54.4 0.6 copy.24
  55.0 1.6 %collective-permute-done.17.refs_5_ = bf16[512,768]{1,0:T(8,128)(2,1)S(1)} collective-permute-done((bf16[512,768]{1,0:T(8,128)(2,1)S(1)}, bf16[512,768]{1,0:T(8,128)(2,1)S(1)}, u32[]{:S(2)}, u32[]{:S(2)}) %collective-permute-start.17) | collective-permute-done | bytes 786464 | tf_op jit(solution)/shard_map/ppermute | solution.py:44
  56.5 10.1 %shard_map.86 = bf16[1,2,1,68,4,4096]{5,4,3,2,1,0:T(4,128)(2,1)} custom-call(bf16[2,272,512]{2,1,0:T(8,128)(2,1)S(1)} %get-tuple-element.9.places_ref.refs_1_, f32[128,128]{1,0:T(8,128)S(1)} %get-tuple-element.10.weights_ref, f32[544,4096]{1,0:T(8,128)S(1)} %get-tuple-element.11.total_ref, bf16[4096,768]{1,0:T(8,128)(2,1)S(1)} %get-tuple-element.12.refs_0_, ...), custom_call_target="tpu_custom_call" | custom-call | flops 6845104128 | bytes 12582912 | tf_op jit(solution)/shard_map/pallas_call | solution.py:349
  (60 shorter events, 1.2 us)
Async XLA Ops:
  1.5 4.3 %collective-permute-start = (bf16[80,768]{1,0:T(8,128)(2,1)S(1)}, bf16[80,768]{1,0:T(8,128)(2,1)S(1)}, u32[]{:S(2)}, u32[]{:S(2)}) collective-permute-start(bf16[80,768]{1,0:T(8,128)(2,1)S(1)} %slice.146), channel_id=1, source_target_pairs={{0,16},{4,20},{8,24},{12,28},{16,0},{20,4},{24,8},{28,12},{1,17},{... | collective-permute-start | bytes 368648 | tf_op jit(solution)/shard_map/ppermute | solution.py:25
  5.8 16.7 %collective-permute-start.1 = (bf16[192,768]{1,0:T(8,128)(2,1)S(1)}, bf16[192,768]{1,0:T(8,128)(2,1)S(1)}, u32[]{:S(2)}, u32[]{:S(2)}) collective-permute-start(bf16[192,768]{1,0:T(8,128)(2,1)S(1)} %shard_map.69), channel_id=1, source_target_pairs={{0,16},{4,20},{8,24},{12,28},{16,0},{20,4},{24,8},{28,12},{1,17},{... | collective-permute-start | bytes 884744 | tf_op jit(solution)/shard_map/ppermute | solution.py:25
  7.1 10.5 %collective-permute-start.2 = (bf16[176,768]{1,0:T(8,128)(2,1)S(1)}, bf16[176,768]{1,0:T(8,128)(2,1)S(1)}, u32[]{:S(2)}, u32[]{:S(2)}) collective-permute-start(bf16[176,768]{1,0:T(8,128)(2,1)S(1)} %slice.145.refs_0_), channel_id=1, source_target_pairs={{0,16},{4,20},{8,24},{12,28},{16,8},{20,12},{24,0},{28,4},{1,17},{... | collective-permute-start | bytes 811016 | tf_op jit(solution)/shard_map/ppermute | solution.py:25
  7.3 4.1 %collective-permute-start.5 = (bf16[80,768]{1,0:T(8,128)(2,1)S(1)}, bf16[80,768]{1,0:T(8,128)(2,1)S(1)}, u32[]{:S(2)}, u32[]{:S(2)}) collective-permute-start(bf16[80,768]{1,0:T(8,128)(2,1)S(1)} %collective-permute-done.refs_2_.refs_0_), channel_id=1, source_target_pairs={{0,2},{1,3},{2,0},{3,1},{4,6},{5,7},{6,4},{7,5},{8,10},{9,11},{10,... | collective-permute-start | bytes 368648 | tf_op jit(solution)/shard_map/ppermute | solution.py:44
  11.5 12.8 %collective-permute-start.6 = (bf16[160,768]{1,0:T(8,128)(2,1)S(1)}, bf16[160,768]{1,0:T(8,128)(2,1)S(1)}, u32[]{:S(2)}, u32[]{:S(2)}) collective-permute-start(bf16[160,768]{1,0:T(8,128)(2,1)S(1)} %shard_map.72.refs_2_.refs_0_), channel_id=1, source_target_pairs={{0,8},{1,9},{2,10},{3,11},{4,12},{5,13},{6,14},{7,15},{8,0},{9,1},... | collective-permute-start | bytes 737288 | tf_op jit(solution)/shard_map/ppermute | solution.py:39
  13.9 10.2 %collective-permute-start.11 = (bf16[160,768]{1,0:T(8,128)(2,1)S(1)}, bf16[160,768]{1,0:T(8,128)(2,1)S(1)}, u32[]{:S(2)}, u32[]{:S(2)}) collective-permute-start(bf16[160,768]{1,0:T(8,128)(2,1)S(1)} %shard_map.72.refs_2_.refs_0_), channel_id=1, source_target_pairs={{0,4},{1,5},{2,6},{3,7},{4,0},{5,1},{6,2},{7,3},{8,12},{9,13},{10,... | collective-permute-start | bytes 737288 | tf_op jit(solution)/shard_map/ppermute | solution.py:39
  17.7 10.8 %collective-permute-start.12 = (bf16[192,768]{1,0:T(8,128)(2,1)S(1)}, bf16[192,768]{1,0:T(8,128)(2,1)S(1)}, u32[]{:S(2)}, u32[]{:S(2)}) collective-permute-start(bf16[192,768]{1,0:T(8,128)(2,1)S(1)} %shard_map.82), channel_id=1, source_target_pairs={{0,16},{4,20},{8,24},{12,28},{16,12},{20,8},{24,4},{28,0},{1,17},{... | collective-permute-start | bytes 884744 | tf_op jit(solution)/shard_map/ppermute | solution.py:25
  22.6 7.8 %collective-permute-start.3 = (bf16[192,768]{1,0:T(8,128)(2,1)S(1)}, bf16[192,768]{1,0:T(8,128)(2,1)S(1)}, u32[]{:S(2)}, u32[]{:S(2)}) collective-permute-start(bf16[192,768]{1,0:T(8,128)(2,1)S(1)} %shard_map.70), channel_id=1, source_target_pairs={{0,2},{1,3},{2,0},{3,1},{4,6},{5,7},{6,4},{7,5},{8,10},{9,11},{10,... | collective-permute-start | bytes 884744 | tf_op jit(solution)/shard_map/ppermute | solution.py:44
  23.9 16.5 %collective-permute-start.10 = (bf16[192,768]{1,0:T(8,128)(2,1)S(1)}, bf16[192,768]{1,0:T(8,128)(2,1)S(1)}, u32[]{:S(2)}, u32[]{:S(2)}) collective-permute-start(bf16[192,768]{1,0:T(8,128)(2,1)S(1)} %shard_map.80), channel_id=1, source_target_pairs={{0,16},{4,20},{8,24},{12,28},{16,4},{20,0},{24,12},{28,8},{1,17},{... | collective-permute-start | bytes 884744 | tf_op jit(solution)/shard_map/ppermute | solution.py:25
  24.1 12.7 %collective-permute-start.8 = (bf16[192,768]{1,0:T(8,128)(2,1)S(1)}, bf16[192,768]{1,0:T(8,128)(2,1)S(1)}, u32[]{:S(2)}, u32[]{:S(2)}) collective-permute-start(bf16[192,768]{1,0:T(8,128)(2,1)S(1)} %collective-permute-done.1.refs_2_.refs_1_), channel_id=1, source_target_pairs={{0,2},{1,3},{2,0},{3,1},{4,6},{5,7},{6,4},{7,5},{8,10},{9,11},{10,... | collective-permute-start | bytes 884744 | tf_op jit(solution)/shard_map/ppermute | solution.py:44
  24.4 29.7 %collective-permute-start.16 = (bf16[160,768]{1,0:T(8,128)(2,1)S(1)}, bf16[160,768]{1,0:T(8,128)(2,1)S(1)}, u32[]{:S(2)}, u32[]{:S(2)}) collective-permute-start(bf16[160,768]{1,0:T(8,128)(2,1)S(1)} %shard_map.84), channel_id=1, source_target_pairs={{0,12},{1,13},{2,14},{3,15},{4,8},{5,9},{6,10},{7,11},{8,4},{9,5},... | collective-permute-start | bytes 737288 | tf_op jit(solution)/shard_map/ppermute | solution.py:39
  30.4 8.2 %collective-permute-start.4 = (bf16[2,16,128]{2,1,0:T(8,128)(2,1)S(1)}, bf16[2,16,128]{2,1,0:T(8,128)(2,1)S(1)}, u32[]{:S(2)}, u32[]{:S(2)}) collective-permute-start(bf16[2,16,128]{2,1,0:T(8,128)(2,1)S(1)} %pad_maximum_fusion.1), channel_id=1, source_target_pairs={{0,1},{1,0},{2,3},{3,2},{4,5},{5,4},{6,7},{7,6},{8,9},{9,8},{10,11... | collective-permute-start | bytes 24584 | tf_op jit(solution)/shard_map/ppermute | solution.py:44
  35.2 18.9 %collective-permute-start.15 = (bf16[176,768]{1,0:T(8,128)(2,1)S(1)}, bf16[176,768]{1,0:T(8,128)(2,1)S(1)}, u32[]{:S(2)}, u32[]{:S(2)}) collective-permute-start(bf16[176,768]{1,0:T(8,128)(2,1)S(1)} %slice.157.refs_2_), channel_id=1, source_target_pairs={{0,2},{1,3},{2,0},{3,1},{4,6},{5,7},{6,4},{7,5},{8,10},{9,11},{10,... | collective-permute-start | bytes 811016 | tf_op jit(solution)/shard_map/ppermute | solution.py:44
  36.8 5.0 %collective-permute-start.9 = (bf16[512,768]{1,0:T(8,128)(2,1)S(1)}, bf16[512,768]{1,0:T(8,128)(2,1)S(1)}, u32[]{:S(2)}, u32[]{:S(2)}) collective-permute-start(bf16[512,768]{1,0:T(8,128)(2,1)S(1)} %shard_map.75.refs_0_), channel_id=1, source_target_pairs={{0,1},{1,0},{2,3},{3,2},{4,5},{5,4},{6,7},{7,6},{8,9},{9,8},{10,11... | collective-permute-start | bytes 2359304 | tf_op jit(solution)/shard_map/ppermute | solution.py:44
  38.6 5.3 %collective-permute-start.7 = (bf16[512,768]{1,0:T(8,128)(2,1)S(1)}, bf16[512,768]{1,0:T(8,128)(2,1)S(1)}, u32[]{:S(2)}, u32[]{:S(2)}) collective-permute-start(bf16[512,768]{1,0:T(8,128)(2,1)S(1)} %shard_map.73.refs_0_), channel_id=1, source_target_pairs={{0,1},{1,0},{2,3},{3,2},{4,5},{5,4},{6,7},{7,6},{8,9},{9,8},{10,11... | collective-permute-start | bytes 2359304 | tf_op jit(solution)/shard_map/ppermute | solution.py:44
  40.5 13.6 %collective-permute-start.14 = (bf16[176,768]{1,0:T(8,128)(2,1)S(1)}, bf16[176,768]{1,0:T(8,128)(2,1)S(1)}, u32[]{:S(2)}, u32[]{:S(2)}) collective-permute-start(bf16[176,768]{1,0:T(8,128)(2,1)S(1)} %slice.156.refs_0_), channel_id=1, source_target_pairs={{0,2},{1,3},{2,0},{3,1},{4,6},{5,7},{6,4},{7,5},{8,10},{9,11},{10,... | collective-permute-start | bytes 811016 | tf_op jit(solution)/shard_map/ppermute | solution.py:44
  41.8 12.5 %collective-permute-start.18 = (bf16[16,768]{1,0:T(8,128)(2,1)S(1)}, bf16[16,768]{1,0:T(8,128)(2,1)S(1)}, u32[]{:S(2)}, u32[]{:S(2)}) collective-permute-start(bf16[16,768]{1,0:T(8,128)(2,1)S(1)} %shard_map.87), channel_id=1, source_target_pairs={{16,8},{20,12},{24,0},{28,4},{17,9},{21,13},{25,1},{29,5},{18,10},... | collective-permute-start | bytes 73736 | tf_op jit(solution)/shard_map/ppermute | solution.py:405
  44.6 10.3 %collective-permute-start.13 = (bf16[512,768]{1,0:T(8,128)(2,1)S(1)}, bf16[512,768]{1,0:T(8,128)(2,1)S(1)}, u32[]{:S(2)}, u32[]{:S(2)}) collective-permute-start(bf16[512,768]{1,0:T(8,128)(2,1)S(1)} %shard_map.83.refs_2_), channel_id=1, source_target_pairs={{0,1},{1,0},{2,3},{3,2},{4,5},{5,4},{6,7},{7,6},{8,9},{9,8},{10,11... | collective-permute-start | bytes 2359304 | tf_op jit(solution)/shard_map/ppermute | solution.py:44
  54.2 2.4 %collective-permute-start.17 = (bf16[512,768]{1,0:T(8,128)(2,1)S(1)}, bf16[512,768]{1,0:T(8,128)(2,1)S(1)}, u32[]{:S(2)}, u32[]{:S(2)}) collective-permute-start(bf16[512,768]{1,0:T(8,128)(2,1)S(1)} %shard_map.85.refs_4_), channel_id=1, source_target_pairs={{0,1},{1,0},{2,3},{3,2},{4,5},{5,4},{6,7},{7,6},{8,9},{9,8},{10,11... | collective-permute-start | bytes 2359304 | tf_op jit(solution)/shard_map/ppermute | solution.py:44
